TPU v7x, 512 devices: a whole 4x4x16 slice. The times are simulated.
512 devices in a mesh: stream: 32 (over y_hi, z), azim: 16 (over x, y_lo, core).
Axes of the slice: x: 4, y: 4 (y_hi: 2, y_lo: 2; y = y_hi * 2 + y_lo), z: 16, core: 2. Of those that a mesh axis runs over, the one named last changes fastest.
Arguments:
- element_load: float32 [512, 32, 2048], P(None, 'stream', 'azim'), may hold values from -180 to 180
- metric: float32 [3, 512, 32, 2048], P(None, None, 'stream', 'azim'), may hold values from 0.4 to 2.5
- element_order: int32 [32, 2048], P('stream', 'azim'), may hold values from 0 to 127, as said below
Outputs:
- correction: float32 [512, 32, 2048], P(None, 'stream', 'azim')
Inputs may be any that keep to these rules, and one draw needn't show every extreme that they name: `element_order`: within each device's block of 128 columns, each row lists every index 0 to 127 once.
All inputs are finite; a program needn't handle non-finite values.
Results may differ from a plain program's by a relative error of at most 0.0003.
Values sent between devices are 32-bit elements; how exact they have to be, the bound alone decides.
No kernel may reach another device: no remote copies, remote signals or barrier semaphores. Data moves between devices by JAX's collectives and lax.ppermute only.
A program may use at most 128 MiB of HBM per device.

v0:
```python
import jax
import jax.numpy as jnp
import numpy as np
from jax import lax
from jax.experimental import pallas as pl
from jax.experimental.pallas import tpu as pltpu
from jax.sharding import PartitionSpec as P

ITERS = 6
LOW_EIG = 0.3
HIGH_EIG = 3.0
CENTER = 0.5 * (HIGH_EIG + LOW_EIG)
HALF_WIDTH = 0.5 * (HIGH_EIG - LOW_EIG)
FIRST_RHO = HALF_WIDTH / CENTER
SECOND_RHO = 1.0 / (2.0 * CENTER / HALF_WIDTH - FIRST_RHO)
KEEP = SECOND_RHO * FIRST_RHO
GAIN = 2.0 * SECOND_RHO / HALF_WIDTH
LANES = 128
HALF = 64
F32 = jnp.float32


def legendre_pair(degree, places):
    previous = places * 0.0 + 1.0
    current = places.copy()
    for k in range(2, degree + 1):
        following = ((2 * k - 1) * places * current - (k - 1) * previous) / k
        previous = current
        current = following
    return (current, previous)


def gll_table(points):
    degree = points - 1
    places = np.cos(np.pi * np.arange(points) / degree)
    for _ in range(60):
        top, below = legendre_pair(degree, places)
        places = places - (places * top - below) / (points * top)
    nodes = np.sort(places)
    nodes[0] = -1.0
    nodes[-1] = 1.0
    at_nodes = legendre_pair(degree, nodes)[0]
    weights = 2.0 / (degree * (degree + 1) * at_nodes**2)
    deriv = np.zeros((points, points))
    for i in range(points):
        for j in range(points):
            if i != j:
                deriv[i, j] = at_nodes[i] / (at_nodes[j] * (nodes[i] - nodes[j]))
    deriv[0, 0] = -degree * (degree + 1) / 4.0
    deriv[-1, -1] = degree * (degree + 1) / 4.0
    return (nodes, weights, deriv)


def lagrange_table(source, target):
    out = np.ones((len(target), len(source)))
    for j in range(len(source)):
        for k in range(len(source)):
            if k != j:
                out[:, j] *= (target - source[k]) / (source[j] - source[k])
    return out


N8, W8, D8 = gll_table(8)
N4, W4, D4 = gll_table(4)
N2, W2, D2 = gll_table(2)


def kron3(a, b, c):
    return np.kron(np.kron(a, b), c)


def cube(w):
    return (w[:, None, None] * w[None, :, None] * w[None, None, :]).reshape(-1)


def share(n):
    edge = np.ones(n)
    edge[0] = edge[-1] = 0.5
    return cube(edge)


def grads(d):
    i = np.eye(d.shape[0])
    return [kron3(d, i, i), kron3(i, d, i), kron3(i, i, d)]


def f32(x):
    return np.asarray(x, np.float32)


def lanes_of(column):
    return np.repeat(f32(column)[:, None], LANES, axis=1)


UP8 = lagrange_table(N4, N8)
UP4 = lagrange_table(N2, N4)
TO4 = lagrange_table(N8, N4)
TO2 = lagrange_table(N8, N2)

C_BD = f32(np.kron(np.eye(16), D8))
C_BDT = f32(np.kron(np.eye(16), D8.T))
C_BSQ = f32(np.kron(np.eye(16), (D8 * D8).T))
C_SAMPLE = f32(np.concatenate([kron3(TO4, TO4, TO4), kron3(TO2, TO2, TO2)]))
C_UP8 = f32(kron3(UP8, UP8, UP8))
C_DOWN8 = f32(kron3(UP8, UP8, UP8).T)
C_UP4 = f32(kron3(UP4, UP4, UP4))
C_DOWN4 = f32(kron3(UP4, UP4, UP4).T)
C_UP4X3 = np.zeros((192, 16), np.float32)
for layer in range(3):
    C_UP4X3[64 * layer : 64 * layer + 64, 4 * layer : 4 * layer + 8] = C_UP4
C_G4 = f32(np.concatenate(grads(D4)))
C_G4T = f32(np.concatenate(grads(D4)).T)
C_SQ4 = f32((np.concatenate(grads(D4)) ** 2).T)
C_W4 = lanes_of(cube(W4) / np.exp(kron3(TO4, TO4, TO4) @ np.log(cube(W8))))
C_W2 = lanes_of(cube(W2) / np.exp(kron3(TO2, TO2, TO2) @ np.log(cube(W8))))
C_M4 = lanes_of(share(4))
FIRST = np.r_[0:64, 64:80, 128:144]
LAST = np.r_[0:64, 112:128, 176:192]
CONSTANTS = {
    "bd": C_BD, "bdt": C_BDT, "bsq": C_BSQ, "sample": C_SAMPLE, "w4": C_W4, "w2": C_W2,
    "sq4": C_SQ4, "gm": C_G4, "gmt": C_G4T, "m4": C_M4, "down8": C_DOWN8, "down4": C_DOWN4,
    "up4": C_UP4X3, "up8": C_UP8, "gm_first": C_G4[FIRST], "gmt_first": C_G4T[:16, FIRST],
    "gm_last": C_G4[LAST], "gmt_last": C_G4T[48:, LAST],
}


def pack_constants():
    rows, places, start = [], {}, 0
    for name, value in CONSTANTS.items():
        blocks = -(-value.shape[1] // LANES)
        padded = np.zeros((value.shape[0], blocks * LANES), np.float32)
        padded[:, : value.shape[1]] = value
        rows += [padded[:, k * LANES : (k + 1) * LANES] for k in range(blocks)]
        places[name] = (start, value.shape, blocks)
        start += value.shape[0] * blocks
    return np.concatenate(rows), places


PACK, PLACES = pack_constants()


class Constant:
    def __init__(self, ref, name):
        self.ref, self.name = ref, name

    def __getitem__(self, index):
        start, (rows, columns), blocks = PLACES[self.name]
        parts = []
        for k in range(blocks):
            width = min(LANES, columns - k * LANES)
            parts.append(self.ref[start + k * rows : start + (k + 1) * rows, :width])
        value = parts[0] if blocks == 1 else jnp.concatenate(parts, axis=1)
        return value if index is Ellipsis else value[index]


def dot(a, b):
    return jnp.dot(a, b, preferred_element_type=F32, precision=lax.Precision.HIGHEST)


def iota(rows, axis):
    return lax.broadcasted_iota(jnp.int32, (rows, LANES), axis)


def wide(ref, start, size):
    return jnp.concatenate([ref[0, start : start + size], ref[1, start : start + size]], axis=1)


def put(ref, start, size, value):
    ref[0, start : start + size] = value[:, :LANES]
    ref[1, start : start + size] = value[:, LANES:]


def total(terms):
    out = terms[0]
    for t in terms[1:]:
        out = out + t
    return out


def contract(v, matrix, sign):
    n = len(v)
    h = n // 2
    even = [v[k] + v[n - 1 - k] for k in range(h)]
    odd = [v[k] - v[n - 1 - k] for k in range(h)]
    out = [None] * n
    for i in range(h):
        p = total([even[k] * float(0.5 * (matrix[i, k] + matrix[i, n - 1 - k])) for k in range(h)])
        q = total([odd[k] * float(0.5 * (matrix[i, k] - matrix[i, n - 1 - k])) for k in range(h)])
        out[i] = p + q
        out[n - 1 - i] = q - p if sign < 0 else p - q
    return out


def fine_rows(s, a):
    return s * 64 + a * 8


PLANES = [(0, 7), (1, 2), (3, 4), (5, 6)]


def pair(ref, p, base=0):
    return jnp.concatenate([wide(ref, base + 64 * s, 64) for s in p], axis=0)


def put_pair(ref, p, value):
    for k, s in enumerate(p):
        put(ref, 64 * s, 64, value[64 * k : 64 * k + 64])


def fine_stream(u, g, acc):
    for h in range(2):
        for a in range(8):
            at = [fine_rows(s, a) for s in range(8)]
            grad = contract([u[h, r : r + 8] for r in at], D8, -1)
            back = contract([grad[s] * g[h, r : r + 8] for s, r in enumerate(at)], D8.T, -1)
            for s, r in enumerate(at):
                acc[h, r : r + 8] = back[s]


def fine_cross(u, g, acc, bd, bdt, pairs):
    for p in pairs:
        flux = dot(bd[...], pair(u, p)) * pair(g, p, 1024)
        put_pair(acc, p, pair(acc, p) + dot(bdt[...], flux))
        for s in p:
            for h in range(2):
                at = [fine_rows(s, a) for a in range(8)]
                grad = contract([u[h, r : r + 8] for r in at], D8, -1)
                flux = [grad[a] * g[h, 512 + r : 520 + r] for a, r in enumerate(at)]
                back = contract(flux, D8.T, -1)
                for a, r in enumerate(at):
                    acc[h, r : r + 8] += back[a]


def fine_apply(u, g, acc, bd, bdt):
    fine_stream(u, g, acc)
    fine_cross(u, g, acc, bd, bdt, PLANES)


def fine_front(u, g, acc, bd, bdt):
    fine_stream(u, g, acc)
    fine_cross(u, g, acc, bd, bdt, PLANES[:1])
    join_fine(acc, (0, 7))


def left(x0, x1):
    near = iota(x0.shape[0], 1) < LANES - 16
    y0, y1 = pltpu.roll(x0, LANES - 16, 1), pltpu.roll(x1, LANES - 16, 1)
    return jnp.where(near, y0, y1), jnp.where(near, y1, y0)


def right(x0, x1):
    near = iota(x0.shape[0], 1) >= 16
    y0, y1 = pltpu.roll(x0, 16, 1), pltpu.roll(x1, 16, 1)
    return jnp.where(near, y0, y1), jnp.where(near, y1, y0)


def join_radial(x, points, start, rows):
    place = iota(rows, 1) % 16
    first = pl.ds(start, rows, stride=points)
    last = pl.ds(start + points - 1, rows, stride=points)
    for h in range(2):
        view = x.at[h]
        low, high = view[first, :], view[last, :]
        view[first, :] = jnp.where(place == 0, 0.0, low + pltpu.roll(high, 1, 1))
        view[last, :] = jnp.where(place == 15, 0.0, high + pltpu.roll(low, LANES - 1, 1))


def join_fine(x, planes=range(8)):
    for s in planes:
        join_radial(x, 8, 64 * s, 8)
        lo, hi = fine_rows(s, 0), fine_rows(s, 7)
        low = [x[h, lo : lo + 8] for h in range(2)]
        high = [x[h, hi : hi + 8] for h in range(2)]
        to_low, to_high = right(*high), left(*low)
        for h in range(2):
            x[h, lo : lo + 8] = low[h] + to_low[h]
            x[h, hi : hi + 8] = high[h] + to_high[h]


def join_mid(x):
    join_radial(x, 4, 0, 16)
    first = iota(8, 0) < 4
    for s in range(4):
        lo, hi = s * 16, s * 16 + 8
        low = [x[h, lo : lo + 8] for h in range(2)]
        high = [x[h, hi : hi + 8] for h in range(2)]
        to_low = right(*[pltpu.roll(t, 4, 0) for t in high])
        to_high = left(*[pltpu.roll(t, 4, 0) for t in low])
        for h in range(2):
            x[h, lo : lo + 8] = low[h] + jnp.where(first, to_low[h], 0.0)
            x[h, hi : hi + 8] = high[h] + jnp.where(first, 0.0, to_high[h])


def is_even(place, k):
    return lax.rem(place[k], 2) == 0


def full_of(x, faces, h, r, offset=0):
    even, far, near = faces
    rows = x.shape[1]
    plane = {512: 64, 64: 16}[rows]
    value = x[h, r : r + 8]
    if r < plane:
        at = offset + r
        return value + jnp.where(even, far[h, at : at + 8], near[h, at : at + 8])
    if r >= rows - plane:
        at = offset + r - (rows - plane)
        return value + jnp.where(even, near[h, at : at + 8], far[h, at : at + 8])
    return value


def send_faces(x, even, far, near, plane, offset=0):
    rows = x.shape[1]
    last = rows - plane
    one = pl.multiple_of(jnp.where(even, last, 0), 8)
    two = pl.multiple_of(jnp.where(even, 0, last), 8)
    for h in range(2):
        near[h, offset : offset + plane] = x[h, pl.ds(one, plane), :]
        far[h, offset : offset + plane] = x[h, pl.ds(two, plane), :]


def wall_mask(points):
    place, node = iota(8, 1) % 16, iota(8, 0) % points
    return ((node == 0) & (place == 0)) | ((node == points - 1) & (place == 15))


def own_part(half0, half1):
    near = iota(half0.shape[0], 1) < HALF
    return pltpu.roll(jnp.where(near, half1, half0), HALF, 1)


def tiles(rows):
    return [(h, r) for h in range(2) for r in range(0, rows, 8)]


def mid_apply(u, g4, acc, gm, gmt):
    flux = dot(gm[...], wide(u, 0, 64)) * wide(g4, 0, 192)
    put(acc, 0, 64, dot(gmt[...], flux))


def fine_diagonal(g, diag, bsq):
    square = (D8 * D8).T
    for c in range(4):
        rows = slice(128 * c, 128 * c + 128)
        diag[rows] = dot(bsq[...], g[1024 + 128 * c : 1152 + 128 * c])
    for axis in range(2):
        for fixed in range(8):
            at = [fine_rows(k, fixed) if axis == 0 else fine_rows(fixed, k) for k in range(8)]
            back = contract([g[512 * axis + r : 512 * axis + r + 8] for r in at], square, 1)
            for k, r in enumerate(at):
                diag[r : r + 8] += back[k]


def halves_up_down(a, b):
    near = iota(8, 1) < HALF
    up = jnp.where(near, a, pltpu.roll(b, HALF, 1))
    return up, jnp.where(near, pltpu.roll(a, HALF, 1), b)


def before_after(even, x, y):
    p, n = jnp.where(even, x, y), jnp.where(even, y, x)
    near = iota(8, 1) < HALF
    first = (jnp.where(near, p, 0.0), jnp.where(near, 0.0, pltpu.roll(n, HALF, 1)))
    second = (jnp.where(near, pltpu.roll(p, HALF, 1), 0.0), jnp.where(near, 0.0, n))
    return first, second


def order_kernel(pos, metric, load, order, g, rolled, far, near):
    even = is_even(pos, 1)
    slots = jnp.broadcast_to(pltpu.roll(order[...], HALF, 1), (8, LANES))
    wr = total([jnp.where(iota(8, 0) == k, float(W8[k]), 0.0) for k in range(8)])
    for r in range(0, 1536, 8):
        scale = wr * float(W8[(r % 512) // 64] * W8[(r // 8) % 8])
        g[r : r + 8] = jnp.take_along_axis(metric[r : r + 8], slots, axis=1) * scale
    for r in range(0, 512, 8):
        rolled[r : r + 8] = pltpu.roll(load[r : r + 8], HALF, 1)
    for r in range(0, 1024, 8):
        other = g[1024 + r : 1032 + r] if r < 512 else rolled[r - 512 : r - 504]
        up, down = halves_up_down(g[r : r + 8], other)
        far[r : r + 8] = jnp.where(even, down, up)
        near[r : r + 8] = jnp.where(even, up, down)


def own_kernel(g, bsq, diag):
    fine_diagonal(g, diag, bsq)


def setup_kernel(
    pos, g, rolled, diag, x, y, bsq, g8, load, diag8, face_a, face_b, ghost, ghost_diag
):
    near = iota(8, 1) < HALF
    even_a = is_even(pos, 1)

    def place(out, row, own, sides):
        out[0, row : row + 8] = jnp.where(near, sides[0], own)
        out[1, row : row + 8] = jnp.where(near, own, sides[1])

    for r in range(0, 1024, 8):
        first, second = before_after(even_a, x[r : r + 8], y[r : r + 8])
        place(g8, r, g[r : r + 8], first)
        ghost[r : r + 8] = first[0] + first[1]
        if r < 512:
            place(g8, 1024 + r, g[1024 + r : 1032 + r], second)
            ghost[1024 + r : 1032 + r] = second[0] + second[1]
        else:
            place(load, r - 512, rolled[r - 512 : r - 504], second)
    fine_diagonal(ghost, ghost_diag, bsq)
    for r in range(0, 512, 8):
        side = ghost_diag[r : r + 8]
        place(diag8, r, diag[r : r + 8], (side, side))
    for x in (load, diag8):
        join_fine(x)
    even = is_even(pos, 0)
    send_faces(load, even, face_a, face_b, 64)
    send_faces(diag8, even, face_a, face_b, 64, 64)


def coarsen_kernel(g8, w4, w2, sample, sq4, g4, diag4, edges, upper):
    low = []
    for d in range(3):
        coarse = jnp.exp(dot(sample[...], jnp.log(wide(g8, 512 * d, 512))))
        put(g4, 64 * d, 64, coarse[:64] * jnp.concatenate([w4[...], w4[...]], axis=1))
        low.append([coarse[64:72, :LANES] * w2[...], coarse[64:72, LANES:] * w2[...]])
    put(diag4, 0, 64, dot(sq4[...], wide(g4, 0, 192)))
    join_mid(diag4)

    def corner(d, i, j, k):
        row = 4 * i + 2 * j + k
        return [t[row : row + 1] for t in low[d]]

    def add(x, y):
        return [x[0] + y[0], x[1] + y[1]]

    def quarter(x):
        return [0.25 * x[0], 0.25 * x[1]]

    def outward(x):
        return [pltpu.roll(x[0], 1, 1), pltpu.roll(x[1], 1, 1)]

    es = [[quarter(add(corner(0, 0, j, k), corner(0, 1, j, k))) for k in range(2)] for j in range(2)]
    ea = [[quarter(add(corner(1, i, 0, k), corner(1, i, 1, k))) for k in range(2)] for i in range(2)]
    er = [[quarter(add(corner(2, i, j, 0), corner(2, i, j, 1))) for j in range(2)] for i in range(2)]
    col = [add(es[0][k], list(right(*es[1][k]))) for k in range(2)]
    edge_s = add(col[0], outward(col[1]))
    edge_a = [add(ea[i][0], outward(ea[i][1])) for i in range(2)]
    edge_r = [add(er[i][0], list(right(*er[i][1]))) for i in range(2)]
    off_wall = iota(1, 1) % 16 != 0
    rows = [jnp.where(off_wall, own_part(*x), 0.0) for x in (edge_s, edge_a[0], edge_a[1])]
    rows += [own_part(*x) for x in edge_r]
    none = jnp.zeros((5, LANES), F32)
    edges[...] = jnp.concatenate([rows[0], rows[1], rows[3], none], axis=0)
    upper[...] = jnp.concatenate([rows[0], rows[2], rows[4], none], axis=0)


def first_kernel(
    pos, load, diag8, a, b, g8, bd, bdt, res, inv8, u, acc, face_a, face_b
):
    even = is_even(pos, 0)
    got = (even, a, b)
    wall8 = wall_mask(8)
    for h, r in tiles(512):
        diag = full_of(diag8, got, h, r, 64)
        inv = jnp.where(wall8, 0.0, 1.0 / jnp.where(wall8, 1.0, diag))
        full = full_of(load, got, h, r)
        res[h, r : r + 8] = full
        inv8[h, r : r + 8] = inv
        u[h, r : r + 8] = inv * full * (1.0 / CENTER)
    fine_front(u, g8, acc, bd, bdt)
    send_faces(acc, even, face_a, face_b, 64)


def inner_kernel(u, g8, start, bd, bdt, acc):
    for h, r in tiles(512):
        acc[h, r : r + 8] = start[h, r : r + 8]
    fine_cross(u, g8, acc, bd, bdt, PLANES[1:])
    join_fine(acc, range(1, 7))


def second_kernel(
    pos, res, inv8, acc, a, b, diag4, upper, g8, bd, bdt, down8,
    kept, t4, face_a, face_b, u, back, part,
):
    even = is_even(pos, 0)
    got = (even, a, b)
    edge = jnp.where((iota(8, 0) == 0) | (iota(8, 0) == 7), 0.5, 1.0)
    for h, r in tiles(512):
        inv, before = inv8[h, r : r + 8], res[h, r : r + 8]
        now = before - full_of(acc, got, h, r)
        old = inv * before * (1.0 / CENTER)
        new = KEEP * old + GAIN * inv * now
        kept[h, r : r + 8] = old + new
        kept[h, 512 + r : 520 + r] = now
        kept[h, 1024 + r : 1032 + r] = new
        u[h, r : r + 8] = new
    fine_apply(u, g8, back, bd, bdt)
    for h, r in tiles(512):
        s, c = r // 64, (r // 8) % 8
        scale = (0.5 if s in (0, 7) else 1.0) * (0.5 if c in (0, 7) else 1.0)
        part[r : r + 8, h * LANES : h * LANES + LANES] = (
            kept[h, 512 + r : 520 + r] * (edge * scale) - back[h, r : r + 8]
        )
    put(t4, 0, 64, dot(down8[...], part[...]))
    join_mid(t4)
    send_faces(t4, even, face_a, face_b, 16)
    send_faces(diag4, even, face_a, face_b, 16, 16)
    for face in (face_a, face_b):
        for h in range(2):
            face[h, 32:40] = upper[...]


def third_kernel(
    pos, t4, diag4, edges, a, b, g4, gm, gmt, res, inv4, edge, acc, face_a, face_b, u
):
    even = is_even(pos, 0)
    got = (even, a, b)
    wall = wall_mask(4)
    for h, r in tiles(64):
        full = full_of(t4, got, h, r)
        diag = full_of(diag4, got, h, r, 16)
        inv = jnp.where(wall, 0.0, 1.0 / jnp.where(wall, 1.0, diag))
        res[h, r : r + 8] = full
        inv4[h, r : r + 8] = inv
        u[h, r : r + 8] = inv * full * (1.0 / CENTER)
    lower = jnp.where(even, a[0, 32:40], b[0, 32:40])
    edge[...] = edges[...] + jnp.where(iota(8, 0) == 0, 0.0, lower)
    mid_apply(u, g4, acc, gm, gmt)
    join_mid(acc)
    send_faces(acc, even, face_a, face_b, 16)


def fourth_kernel(
    pos, res, acc, inv4, edge, a, b, g4, gm, gmt, m4, down4, corners, one, two, keep, part
):
    got = (is_even(pos, 0), a, b)
    for h, r in tiles(64):
        inv, before = inv4[h, r : r + 8], res[h, r : r + 8]
        now = before - full_of(acc, got, h, r)
        old = inv * before * (1.0 / CENTER)
        new = KEEP * old + GAIN * inv * now
        keep[h, r : r + 8] = now
        keep[h, 64 + r : 72 + r] = new
        keep[h, 128 + r : 136 + r] = old + new
    even_a = is_even(pos, 1)
    one[...] = jnp.where(even_a, keep[0], keep[1])
    two[...] = jnp.where(even_a, keep[1], keep[0])
    flux = dot(gm[...], wide(keep, 64, 64)) * wide(g4, 0, 192)
    put(part, 0, 64, dot(gmt[...], flux))
    for h, r in tiles(64):
        part[h, r : r + 8] = m4[r : r + 8] * keep[h, r : r + 8] - part[h, r : r + 8]
    low = dot(down4[...], wide(part, 0, 64))
    near = iota(8, 1) < HALF
    half0 = jnp.where(near, 0.0, low[:, :LANES])
    half1 = jnp.where(near, low[:, LANES:], 0.0)

    def corner(i, j, k):
        row = 4 * i + 2 * j + k
        return [half0[row : row + 1], half1[row : row + 1]]

    lane = iota(1, 1)
    mine, extra = [], []
    for i in range(2):
        columns = []
        for k in range(2):
            shifted = right(*corner(i, 1, k))
            straight = corner(i, 0, k)
            columns.append([straight[0] + shifted[0], straight[1] + shifted[1]])
        both = [columns[0][h] + pltpu.roll(columns[1][h], 1, 1) for h in range(2)]
        both = [jnp.where(lane % 16 == 0, 0.0, t) for t in both]
        mine.append(own_part(*both))
        extra.append(both[1])
    sides = jnp.where(lane < 16, pltpu.roll(extra[0], HALF, 1), 0.0) + jnp.where(
        (lane >= 16) & (lane < 32), pltpu.roll(extra[1], HALF + 16, 1), 0.0
    )
    none = jnp.zeros((2, LANES), F32)
    corners[...] = jnp.concatenate(mine + [sides, edge[0:3], none], axis=0)


def groups(ns):
    return max(1, ns // 8)


def side_kernel(pos, to_far, to_near, one, two, g4, gm, gmt, wider, far, near_side, back):
    near = iota(8, 1) < HALF
    even, even_a = is_even(pos, 0), is_even(pos, 1)
    for r in range(0, 192, 8):
        x, y = one[r : r + 8], two[r : r + 8]
        before, after = jnp.where(even_a, x, y), jnp.where(even_a, y, x)
        x, y = to_far[r : r + 8], to_near[r : r + 8]
        lower, upper = jnp.where(even_a, x, y), jnp.where(even_a, y, x)
        halves = (jnp.where(near, before, lower), jnp.where(near, upper, after))
        for h in range(2):
            wider[h, r : r + 8] = halves[h]
    flux = dot(gm[...], wide(wider, 64, 64)) * wide(g4, 0, 192)
    put(back, 0, 64, dot(gmt[...], flux))
    one = pl.multiple_of(jnp.where(even, 48, 0), 8)
    two = pl.multiple_of(jnp.where(even, 0, 48), 8)
    for out, plane in ((near_side, one), (far, two)):
        for h in range(2):
            out[h, 0:64] = g4[h, 0:64]
            out[h, 64:80] = g4[h, pl.ds(64 + plane, 16), :]
            out[h, 80:96] = g4[h, pl.ds(128 + plane, 16), :]
            out[h, 96:112] = back[h, pl.ds(plane, 16), :]


def column_kernel(rows, first, out):
    ns = rows.shape[0] // 8
    n = ns // groups(ns)

    def field(k):
        return rows[pl.ds(k, ns, stride=8), :]

    def later(x):
        return pltpu.roll(x, 1, 0)

    sides = field(2)
    over = jnp.where(iota(ns, 1) < 16, sides + later(pltpu.roll(sides, LANES - 16, 1)), 0.0)
    out[0:ns] = field(0) + later(field(1))
    for k in range(3):
        out[(1 + k) * ns : (2 + k) * ns] = field(3 + k)
    parts = [over[k * n : k * n + n] for k in range(groups(ns))]
    out[4 * ns : 4 * ns + n] = total(
        [pltpu.roll(p, 16 * k, 1) if k else p for k, p in enumerate(parts)]
    )


def pass_kernel(rows, first, second, out):
    out[...] = rows[...]


def coarse_kernel(
    pos, columns, others, wider, far, near_side, g4, inv4, gm, gmt, up4, gm_first, gmt_first,
    gm_last, gmt_last,
    res, u, sol, acc, face_a, face_b, vals, x2, es, ea, er, es0, ea0, er0, dg, ri,
):
    ns = x2.shape[0]
    na = x2.shape[1] // LANES
    width = na * LANES

    n = ns // groups(ns)
    size = 4 * ns + n
    even_a = is_even(pos, 1)

    def rows_of(d, start, count):
        at = d // 2 * size + start
        x, y = columns[at : at + count], others[at : at + count]
        return jnp.where(even_a, x, y) if d % 2 == 0 else jnp.where(even_a, y, x)

    def field(k):
        return [rows_of(d, k * ns, ns) for d in range(na)]

    def side(d):
        packed = rows_of(d, 4 * ns, n)
        parts = [pltpu.roll(packed, LANES - 16 * k, 1) if k else packed for k in range(groups(ns))]
        return jnp.where(iota(ns, 1) < 16, jnp.concatenate(parts, axis=0), 0.0)

    def roll_l(x, k):
        return pltpu.roll(x, k % width, 1)

    lane = iota(ns, 1)
    wall, top = lane % 16 == 0, lane % 16 == 15
    at = [slice(d * LANES, d * LANES + LANES) for d in range(na)]

    def towards_next(y, d):
        return jnp.where(lane < LANES - 16, y[d], y[(d + 1) % na])

    def towards_last(y, d):
        return jnp.where(lane < 16, y[d - 1], y[d])

    ea_all, er_all = field(2), field(3)
    ea_roll = [pltpu.roll(t, 16, 1) for t in ea_all]
    for d, es_d in enumerate(field(1)):
        es0_d, ea0_d = pltpu.roll(es_d, 1, 0), towards_last(ea_roll, d)
        er0_d = pltpu.roll(er_all[d], 1, 1)
        both = es_d + es0_d + ea_all[d] + ea0_d + er_all[d] + er0_d
        es[:, at[d]], ea[:, at[d]] = es_d, ea_all[d]
        es0[:, at[d]], ea0[:, at[d]] = es0_d, ea0_d
        er[:, at[d]] = jnp.where(wall | top, 0.0, er_all[d])
        er0[:, at[d]] = jnp.where(wall | (lane % 16 == 1), 0.0, er0_d)
        dg[:, at[d]] = jnp.where(wall, 0.0, both)
        ri[:, at[d]] = jnp.where(wall, 0.0, 1.0 / jnp.where(wall, 1.0, both))

    def inner(terms):
        return jnp.sum(jnp.sum(total(terms), axis=0, keepdims=True), axis=1, keepdims=True)

    first = field(0)
    r = [first[d] + side((d - 1) % na) for d in range(na)]
    p = [ri[:, at[d]] * r[d] for d in range(na)]
    gz = inner([r[d] * p[d] for d in range(na)])
    x = [jnp.zeros_like(t) for t in r]
    for it in range(ITERS):
        ahead = [pltpu.roll(t, LANES - 16, 1) for t in p]
        behind = [pltpu.roll(t, 16, 1) for t in p]
        q, terms = [], []
        for d in range(na):
            t, k = p[d], at[d]
            out = dg[:, k] * t
            out = out - es[:, k] * pltpu.roll(t, ns - 1, 0) - es0[:, k] * pltpu.roll(t, 1, 0)
            out = out - ea[:, k] * towards_next(ahead, d) - ea0[:, k] * towards_last(behind, d)
            out = out - er[:, k] * pltpu.roll(t, LANES - 1, 1) - er0[:, k] * pltpu.roll(t, 1, 1)
            q.append(out)
            terms.append(t * out)
        alpha = gz / inner(terms)
        x = [x[d] + alpha * p[d] for d in range(na)]
        if it + 1 < ITERS:
            r = [r[d] - alpha * q[d] for d in range(na)]
            z = [ri[:, at[d]] * r[d] for d in range(na)]
            new = inner([r[d] * z[d] for d in range(na)])
            beta = new / gz
            p = [z[d] + beta * p[d] for d in range(na)]
            gz = new
    for d in range(na):
        x2[:, at[d]] = x[d]

    s, a = pos[0], pos[1]
    blocks = [lax.rem(a + na - 1, na), a, lax.rem(a + 1, na)]
    for t in range(4):
        line = x2[pl.ds(lax.rem(s + ns - 1 + t, ns), 1), :]
        for j in range(2):
            for k in range(2):
                n = 4 * t + 2 * j + k
                vals[n : n + 1, :] = roll_l(line, -(16 * j + k)) if j + k else line
    near = iota(16, 1) < HALF
    b = [
        pltpu.roll(vals[:, pl.ds(pl.multiple_of(t * LANES, LANES), LANES)], HALF, 1) for t in blocks
    ]
    ext = jnp.concatenate([jnp.where(near, b[0], b[1]), jnp.where(near, b[1], b[2])], axis=1)
    rise = dot(up4[...], ext)
    even = is_even(pos, 0)
    x, y = wide(far, 0, 112), wide(near_side, 0, 112)
    below, above = jnp.where(even, x, y), jnp.where(even, y, x)
    low = dot(gmt_last[...], dot(gm_last[...], rise[:64]) * below[:96]) + below[96:]
    high = dot(gmt_first[...], dot(gm_first[...], rise[128:]) * above[:96]) + above[96:]
    flux = dot(gm[...], rise[64:128] + wide(wider, 64, 64)) * wide(g4, 0, 192)
    back = dot(gmt[...], flux)
    put(acc, 0, 16, back[:16] + low)
    put(acc, 16, 32, back[16:48])
    put(acc, 48, 16, back[48:] + high)
    join_mid(acc)
    put(sol, 0, 64, wide(wider, 128, 64) + rise[64:128])
    for h, r in tiles(64):
        now = wider[h, r : r + 8] - acc[h, r : r + 8]
        new = inv4[h, r : r + 8] * now * (1.0 / CENTER)
        res[h, r : r + 8] = now
        u[h, r : r + 8] = new
        sol[h, r : r + 8] += new
    mid_apply(u, g4, acc, gm, gmt)
    join_mid(acc)
    send_faces(acc, even, face_a, face_b, 16)


def sixth_kernel(
    pos, res, u, sol, acc, a, b, inv4, up8, kept, g8, bd, bdt,
    out, v8, acc2, face_a, face_b, y4,
):
    even = is_even(pos, 0)
    for h, r in tiles(64):
        now = res[h, r : r + 8] - full_of(acc, (even, a, b), h, r)
        new = KEEP * u[h, r : r + 8] + GAIN * inv4[h, r : r + 8] * now
        y4[h, r : r + 8] = sol[h, r : r + 8] + new
    put(v8, 0, 512, dot(up8[...], wide(y4, 0, 64)))
    for h, r in tiles(512):
        e8 = v8[h, r : r + 8]
        out[h, r : r + 8] = kept[h, r : r + 8] + e8
        v8[h, r : r + 8] = kept[h, 1024 + r : 1032 + r] + e8
    fine_front(v8, g8, acc2, bd, bdt)
    send_faces(acc2, even, face_a, face_b, 64)


def seventh_kernel(
    pos, kept, sol, acc, a, b, inv8, g8, bd, bdt, res, out, u, acc2, face_a, face_b
):
    even = is_even(pos, 0)
    for h, r in tiles(512):
        now = kept[h, 512 + r : 520 + r] - full_of(acc, (even, a, b), h, r)
        new = inv8[h, r : r + 8] * now * (1.0 / CENTER)
        res[h, r : r + 8] = now
        u[h, r : r + 8] = new
        out[h, r : r + 8] = sol[h, r : r + 8] + new
    fine_front(u, g8, acc2, bd, bdt)
    send_faces(acc2, even, face_a, face_b, 64)


def inner_last_kernel(u, g8, acc, res, sol, inv8, bd, bdt, out, full):
    for h, r in tiles(384):
        full[h, 64 + r : 72 + r] = acc[h, 64 + r : 72 + r]
    fine_cross(u, g8, full, bd, bdt, PLANES[1:])
    join_fine(full, range(1, 7))
    for r in range(64, 448, 8):
        halves = []
        for h in range(2):
            now = res[h, r : r + 8] - full[h, r : r + 8]
            new = KEEP * u[h, r : r + 8] + GAIN * inv8[h, r : r + 8] * now
            halves.append(sol[h, r : r + 8] + new)
        out[r - 64 : r - 56] = own_part(*halves)


def last_kernel(pos, res, sol, u, acc, a, b, inv8, inner, out):
    got = (is_even(pos, 0), a, b)
    out[64:448] = inner[...]
    for r in [*range(0, 64, 8), *range(448, 512, 8)]:
        halves = []
        for h in range(2):
            now = res[h, r : r + 8] - full_of(acc, got, h, r)
            new = KEEP * u[h, r : r + 8] + GAIN * inv8[h, r : r + 8] * now
            halves.append(sol[h, r : r + 8] + new)
        out[r : r + 8] = own_part(*halves)


def call(kernel, args, outs, scratch=(), scalars=1):
    vmem = pl.BlockSpec(memory_space=pltpu.VMEM)
    smem = pl.BlockSpec(memory_space=pltpu.SMEM)
    arrays = [x for x in args if not isinstance(x, str)]
    named = len(arrays) < len(args)

    def body(*refs):
        rest = iter(refs)
        given = [next(rest) for _ in arrays[: len(arrays) - named]]
        held = next(rest) if named else None
        given = iter(given)
        full = [Constant(held, x) if isinstance(x, str) else next(given) for x in args]
        kernel(*full, *rest)

    if named:
        arrays.append(PACK)
    return pl.pallas_call(
        body,
        out_shape=[jax.ShapeDtypeStruct(s, F32) for s in outs],
        in_specs=[smem] * scalars + [vmem] * (len(arrays) - scalars),
        out_specs=[vmem] * len(outs),
        scratch_shapes=[pltpu.VMEM(s, F32) for s in scratch],
        compiler_params=pltpu.CompilerParams(vmem_limit_bytes=32 * 1024 * 1024),
        name=kernel.__name__,
    )(*arrays)


def exchange(far, near, axis):
    size = lax.axis_size(axis)
    pairs_far = [(i, (i + 1 if i % 2 else i - 1) % size) for i in range(size)]
    pairs_near = [(i, i ^ 1) for i in range(size)]
    return lax.ppermute(far, axis, pairs_far), lax.ppermute(near, axis, pairs_near)


def spread(x, axis, groups=None):
    size = len(groups[0]) if groups else lax.axis_size(axis)
    copies = jnp.broadcast_to(x[None], (size,) + x.shape)
    return lax.all_to_all(copies, axis, 0, 0, axis_index_groups=groups).reshape(-1, LANES)


def on_device(element_load, metric, element_order):
    ns, na = lax.axis_size("stream"), lax.axis_size("azim")
    fine, mid = (2, 512, LANES), (2, 64, LANES)
    face8, face4 = [(2, 64, LANES)] * 2, [(2, 16, LANES)] * 2
    pos = jnp.stack([lax.axis_index("stream"), lax.axis_index("azim")]).astype(jnp.int32)
    g, rolled, a, b = call(
        order_kernel,
        (pos, metric.reshape(1536, LANES), element_load.reshape(512, LANES), element_order),
        [(1536, LANES), (512, LANES), (1024, LANES), (1024, LANES)],
    )
    a, b = exchange(a, b, "azim")
    (diag,) = call(own_kernel, (g, "bsq"), [(512, LANES)], scalars=0)

    def inner(u, acc):
        (acc,) = call(inner_kernel, (u, g8, acc, "bd", "bdt"), [fine], (), 0)
        return acc

    g8, load, diag8, a, b = call(
        setup_kernel,
        (pos, g, rolled, diag, a, b, "bsq"),
        [(2, 1536, LANES), fine, fine] + [(2, 128, LANES)] * 2,
        [(1536, LANES), (512, LANES)],
    )
    a, b = exchange(a, b, "stream")
    res8, inv8, u8, acc, a, b = call(
        first_kernel,
        (pos, load, diag8, a, b, g8, "bd", "bdt"),
        [fine, fine, fine, fine] + face8,
    )
    a, b = exchange(a, b, "stream")
    acc = inner(u8, acc)
    g4, diag4, edges, upper = call(
        coarsen_kernel,
        (g8, "w4", "w2", "sample", "sq4"),
        [(2, 192, LANES), mid, (8, LANES), (8, LANES)],
        scalars=0,
    )
    kept, t4, a, b = call(
        second_kernel,
        (pos, res8, inv8, acc, a, b, diag4, upper, g8, "bd", "bdt", "down8"),
        [(2, 1536, LANES), mid] + [(2, 40, LANES)] * 2,
        [fine, fine, (512, 2 * LANES)],
    )
    a, b = exchange(a, b, "stream")
    res4, inv4, edges, acc, a, b = call(
        third_kernel,
        (pos, t4, diag4, edges, a, b, g4, "gm", "gmt"),
        [mid, mid, (8, LANES), mid] + face4,
        [mid],
    )
    a, b = exchange(a, b, "stream")
    corners, *kept4 = call(
        fourth_kernel,
        (pos, res4, acc, inv4, edges, a, b, g4, "gm", "gmt", "m4", "down4"),
        [(8, LANES), (192, LANES), (192, LANES)],
        [(2, 192, LANES), mid],
    )
    columns = spread(corners, "stream")
    a, b = exchange(*kept4, "azim")
    wider, a, b = call(
        side_kernel,
        (pos, *kept4, a, b, g4, "gm", "gmt"),
        [(2, 192, LANES)] + [(2, 112, LANES)] * 2,
        [mid],
    )
    sides = exchange(a, b, "stream")
    size = 4 * ns + ns // groups(ns)
    (columns,) = call(
        column_kernel, (columns, wider), [(size, LANES)], (), 0
    )
    cores = [list(range(core, na, 2)) for core in range(2)]
    columns = spread(columns, "azim", cores)
    (columns,) = call(pass_kernel, (columns, *sides), [columns.shape], (), 0)
    others = lax.ppermute(columns, "azim", [(i, i ^ 1) for i in range(na)])
    whole = (ns, na * LANES)
    res4, u4, sol4, acc, a, b = call(
        coarse_kernel,
        (
            pos,
            columns,
            others,
            wider,
            *sides,
            g4,
            inv4,
            "gm",
            "gmt",
            "up4",
            "gm_first",
            "gmt_first",
            "gm_last",
            "gmt_last",
        ),
        [mid, mid, mid, mid] + face4,
        [(16, na * LANES)] + [whole] * 9,
    )
    a, b = exchange(a, b, "stream")
    sol8, v8, acc, a, b = call(
        sixth_kernel,
        (pos, res4, u4, sol4, acc, a, b, inv4, "up8", kept, g8, "bd", "bdt"),
        [fine, fine, fine] + face8,
        [mid],
    )
    a, b = exchange(a, b, "stream")
    acc = inner(v8, acc)
    res8, sol8, u8, acc, a, b = call(
        seventh_kernel,
        (pos, kept, sol8, acc, a, b, inv8, g8, "bd", "bdt"),
        [fine, fine, fine, fine] + face8,
    )
    a, b = exchange(a, b, "stream")
    (inside,) = call(
        inner_last_kernel,
        (u8, g8, acc, res8, sol8, inv8, "bd", "bdt"),
        [(384, LANES)],
        [fine],
        scalars=0,
    )
    (out,) = call(last_kernel, (pos, res8, sol8, u8, acc, a, b, inv8, inside), [(512, LANES)])
    return out.reshape(element_load.shape)


def solution(mesh):
    placed = (P(None, "stream", "azim"), P(None, None, "stream", "azim"), P("stream", "azim"))
    return jax.shard_map(
        on_device, mesh=mesh, in_specs=placed, out_specs=P(None, "stream", "azim"), check_vma=False
    )
```

profile of v0, /device:TPU:2, one launch (start us, length us, event | category | flops | bytes accessed | tf_op | source)
XLA Modules:
  0.0 179.8 jit_solution(10341445142723075661)
XLA Ops:
  0.1 1.1 copy-done.7
  1.2 0.9 copy-done.14
  2.8 1.2 order_kernel.1
  4.0 2.9 %collective-permute-start = (f32[1024,128]{1,0:T(8,128)S(1)}, f32[1024,128]{1,0:T(8,128)S(1)}, u32[]{:S(2)}, u32[]{:S(2)}) collective-permute-start(f32[1024,128]{1,0:T(8,128)S(1)} %get-tuple-element.59), channel_id=1, source_target_pairs={{0,15},{1,2},{2,1},{3,4},{4,3},{5,6},{6,5},{7,8},{8,7},{9,10},{10,... | collective-permute-start | bytes 1572872 | tf_op jit(solution)/shard_map/ppermute | solution.py:840
  6.9 2.6 %collective-permute-start.1 = (f32[1024,128]{1,0:T(8,128)S(1)}, f32[1024,128]{1,0:T(8,128)S(1)}, u32[]{:S(2)}, u32[]{:S(2)}) collective-permute-start(f32[1024,128]{1,0:T(8,128)S(1)} %get-tuple-element.60), channel_id=1, source_target_pairs={{0,1},{1,0},{2,3},{3,2},{4,5},{5,4},{6,7},{7,6},{8,9},{9,8},{10,11... | collective-permute-start | bytes 1572872 | tf_op jit(solution)/shard_map/ppermute | solution.py:840
  9.6 1.3 copy-done
  11.3 4.3 %collective-permute-done.refs_4_ = f32[1024,128]{1,0:T(8,128)S(1)} collective-permute-done((f32[1024,128]{1,0:T(8,128)S(1)}, f32[1024,128]{1,0:T(8,128)S(1)}, u32[]{:S(2)}, u32[]{:S(2)}) %collective-permute-start) | collective-permute-done | bytes 524320 | tf_op jit(solution)/shard_map/ppermute | solution.py:840
  15.6 1.9 %setup_kernel.1 = (f32[2,1536,128]{2,1,0:T(8,128)S(1)}, f32[2,512,128]{2,1,0:T(8,128)S(1)}, f32[2,512,128]{2,1,0:T(8,128)S(1)}, f32[2,128,128]{2,1,0:T(8,128)S(1)}, f32[2,128,128]{2,1,0:T(8,128)S(1)}) custom-call(s32[2]{0:T(128)S(1)} %pad_add_fusion.refs_0_, f32[1536,128]{1,0:T(8,128)S(1)} %get-tuple-element.57.refs_0_.refs_1_, ...), custom_call_target="tpu_custom_call" | custom-call | tf_op jit(solution)/shard_map/setup_kernel/pallas_call | solution.py:825
  17.4 14.0 %collective-permute-start.2 = (f32[2,128,128]{2,1,0:T(8,128)S(1)}, f32[2,128,128]{2,1,0:T(8,128)S(1)}, u32[]{:S(2)}, u32[]{:S(2)}) collective-permute-start(f32[2,128,128]{2,1,0:T(8,128)S(1)} %get-tuple-element.63), channel_id=1, source_target_pairs={{0,496},{16,32},{32,16},{48,64},{64,48},{80,96},{96,80},{112,128},... | collective-permute-start | bytes 393224 | tf_op jit(solution)/shard_map/ppermute | solution.py:840
  31.5 1.9 %collective-permute-start.3 = (f32[2,128,128]{2,1,0:T(8,128)S(1)}, f32[2,128,128]{2,1,0:T(8,128)S(1)}, u32[]{:S(2)}, u32[]{:S(2)}) collective-permute-start(f32[2,128,128]{2,1,0:T(8,128)S(1)} %get-tuple-element.64), channel_id=1, source_target_pairs={{0,16},{16,0},{32,48},{48,32},{64,80},{80,64},{96,112},{112,96},{1... | collective-permute-start | bytes 393224 | tf_op jit(solution)/shard_map/ppermute | solution.py:840
  33.4 1.0 collective-permute-done.2.refs_3_
  34.4 3.9 %collective-permute-done.3.refs_4_ = f32[2,128,128]{2,1,0:T(8,128)S(1)} collective-permute-done((f32[2,128,128]{2,1,0:T(8,128)S(1)}, f32[2,128,128]{2,1,0:T(8,128)S(1)}, u32[]{:S(2)}, u32[]{:S(2)}) %collective-permute-start.3) | collective-permute-done | bytes 131104 | tf_op jit(solution)/shard_map/ppermute | solution.py:840
  38.4 1.8 first_kernel.1
  40.1 3.6 %collective-permute-start.4 = (f32[2,64,128]{2,1,0:T(8,128)S(1)}, f32[2,64,128]{2,1,0:T(8,128)S(1)}, u32[]{:S(2)}, u32[]{:S(2)}) collective-permute-start(f32[2,64,128]{2,1,0:T(8,128)S(1)} %get-tuple-element.70), channel_id=1, source_target_pairs={{0,496},{16,32},{32,16},{48,64},{64,48},{80,96},{96,80},{112,128},... | collective-permute-start | bytes 196616 | tf_op jit(solution)/shard_map/ppermute | solution.py:840
  43.8 1.9 %collective-permute-start.5 = (f32[2,64,128]{2,1,0:T(8,128)S(1)}, f32[2,64,128]{2,1,0:T(8,128)S(1)}, u32[]{:S(2)}, u32[]{:S(2)}) collective-permute-start(f32[2,64,128]{2,1,0:T(8,128)S(1)} %get-tuple-element.71), channel_id=1, source_target_pairs={{0,16},{16,0},{32,48},{48,32},{64,80},{80,64},{96,112},{112,96},{1... | collective-permute-start | bytes 196616 | tf_op jit(solution)/shard_map/ppermute | solution.py:840
  45.7 1.5 coarsen_kernel.1
  47.2 1.3 inner_kernel.2.refs_3_
  48.5 1.4 collective-permute-done.4.refs_4_
  49.9 2.9 %second_kernel.1 = (f32[2,1536,128]{2,1,0:T(8,128)S(1)}, f32[2,64,128]{2,1,0:T(8,128)S(1)}, f32[2,40,128]{2,1,0:T(8,128)S(1)}, f32[2,40,128]{2,1,0:T(8,128)S(1)}) custom-call(s32[2]{0:T(128)S(1)} %pad_add_fusion.refs_0_, f32[2,512,128]{2,1,0:T(8,128)S(1)} %get-tuple-element.66.refs_1_, f32[2,512,128]{2,1,0:T(8,128)S(1)} %get-tuple-element.67.refs_2_.refs_6_.refs_5_.refs_7_, ...), custom_call_target="tpu_custom_call" | custom-call | tf_op jit(solution)/shard_map/second_kernel/pallas_call | solution.py:825
  52.8 5.8 %collective-permute-start.6 = (f32[2,40,128]{2,1,0:T(8,128)S(1)}, f32[2,40,128]{2,1,0:T(8,128)S(1)}, u32[]{:S(2)}, u32[]{:S(2)}) collective-permute-start(f32[2,40,128]{2,1,0:T(8,128)S(1)} %get-tuple-element.77), channel_id=1, source_target_pairs={{0,496},{16,32},{32,16},{48,64},{64,48},{80,96},{96,80},{112,128},... | collective-permute-start | bytes 122888 | tf_op jit(solution)/shard_map/ppermute | solution.py:840
  58.7 1.9 %collective-permute-start.7 = (f32[2,40,128]{2,1,0:T(8,128)S(1)}, f32[2,40,128]{2,1,0:T(8,128)S(1)}, u32[]{:S(2)}, u32[]{:S(2)}) collective-permute-start(f32[2,40,128]{2,1,0:T(8,128)S(1)} %get-tuple-element.78), channel_id=1, source_target_pairs={{0,16},{16,0},{32,48},{48,32},{64,80},{80,64},{96,112},{112,96},{1... | collective-permute-start | bytes 122888 | tf_op jit(solution)/shard_map/ppermute | solution.py:840
  60.6 1.7 collective-permute-done.6.refs_4_
  62.3 2.3 %collective-permute-done.7.refs_5_ = f32[2,40,128]{2,1,0:T(8,128)S(1)} collective-permute-done((f32[2,40,128]{2,1,0:T(8,128)S(1)}, f32[2,40,128]{2,1,0:T(8,128)S(1)}, u32[]{:S(2)}, u32[]{:S(2)}) %collective-permute-start.7) | collective-permute-done | bytes 40992 | tf_op jit(solution)/shard_map/ppermute | solution.py:840
  64.7 1.4 third_kernel.1
  66.0 3.5 %collective-permute-start.8 = (f32[2,16,128]{2,1,0:T(8,128)S(1)}, f32[2,16,128]{2,1,0:T(8,128)S(1)}, u32[]{:S(2)}, u32[]{:S(2)}) collective-permute-start(f32[2,16,128]{2,1,0:T(8,128)S(1)} %get-tuple-element.84), channel_id=1, source_target_pairs={{0,496},{16,32},{32,16},{48,64},{64,48},{80,96},{96,80},{112,128},... | collective-permute-start | bytes 49160 | tf_op jit(solution)/shard_map/ppermute | solution.py:840
  69.6 1.9 %collective-permute-start.9 = (f32[2,16,128]{2,1,0:T(8,128)S(1)}, f32[2,16,128]{2,1,0:T(8,128)S(1)}, u32[]{:S(2)}, u32[]{:S(2)}) collective-permute-start(f32[2,16,128]{2,1,0:T(8,128)S(1)} %get-tuple-element.85), channel_id=1, source_target_pairs={{0,16},{16,0},{32,48},{48,32},{64,80},{80,64},{96,112},{112,96},{1... | collective-permute-start | bytes 49160 | tf_op jit(solution)/shard_map/ppermute | solution.py:840
  71.5 3.8 %collective-permute-done.8.refs_5_ = f32[2,16,128]{2,1,0:T(8,128)S(1)} collective-permute-done((f32[2,16,128]{2,1,0:T(8,128)S(1)}, f32[2,16,128]{2,1,0:T(8,128)S(1)}, u32[]{:S(2)}, u32[]{:S(2)}) %collective-permute-start.8) | collective-permute-done | bytes 16416 | tf_op jit(solution)/shard_map/ppermute | solution.py:840
  75.3 1.6 fourth_kernel.1
  78.8 5.7 %all-to-all-start = ((f32[32,8,128]{2,1,0:T(8,128)}), f32[32,8,128]{2,1,0:T(8,128)}, u32[]{:S(2)}, u32[]{:S(2)}) async-start(f32[32,8,128]{2,1,0:T(8,128)} %broadcast_in_dim.4), calls=%async_computation | async-start | bytes 262144 | tf_op jit(solution)/shard_map/all_to_all | solution.py:846
  84.6 1.9 %collective-permute-start.10 = (f32[192,128]{1,0:T(8,128)}, f32[192,128]{1,0:T(8,128)S(1)}, u32[]{:S(2)}, u32[]{:S(2)}) collective-permute-start(f32[192,128]{1,0:T(8,128)} %copy-done.15), channel_id=1, source_target_pairs={{0,15},{1,2},{2,1},{3,4},{4,3},{5,6},{6,5},{7,8},{8,7},{9,10},{10,... | collective-permute-start | bytes 294920 | tf_op jit(solution)/shard_map/ppermute | solution.py:840
  86.5 7.2 %collective-permute-start.11 = (f32[192,128]{1,0:T(8,128)}, f32[192,128]{1,0:T(8,128)S(1)}, u32[]{:S(2)}, u32[]{:S(2)}) collective-permute-start(f32[192,128]{1,0:T(8,128)} %copy-done.17), channel_id=1, source_target_pairs={{0,1},{1,0},{2,3},{3,2},{4,5},{5,4},{6,7},{7,6},{8,9},{9,8},{10,11... | collective-permute-start | bytes 294920 | tf_op jit(solution)/shard_map/ppermute | solution.py:840
  93.7 1.1 collective-permute-done.11.refs_4_
  94.8 0.9 copy-done.16
  96.6 1.2 side_kernel.1
  99.8 2.1 %all-to-all-done = f32[32,8,128]{2,1,0:T(8,128)} async-done(((f32[32,8,128]{2,1,0:T(8,128)}), f32[32,8,128]{2,1,0:T(8,128)}, u32[]{:S(2)}, u32[]{:S(2)}) %all-to-all-start) | async-done | bytes 131104 | tf_op jit(solution)/shard_map/all_to_all | solution.py:846
  101.9 0.9 copy-done.5
  102.8 1.1 column_kernel.1
  104.7 9.2 %all-to-all-start.1 = ((f32[8,136,128]{2,1,0:T(8,128)}), f32[8,136,128]{2,1,0:T(8,128)}, u32[]{:S(2)}, u32[]{:S(2)}) async-start(f32[8,136,128]{2,1,0:T(8,128)} %broadcast_in_dim.5), calls=%async_computation.1 | async-start | bytes 1114112 | tf_op jit(solution)/shard_map/all_to_all | solution.py:846
  113.9 2.4 %collective-permute-start.12 = (f32[2,112,128]{2,1,0:T(8,128)}, f32[2,112,128]{2,1,0:T(8,128)S(1)}, u32[]{:S(2)}, u32[]{:S(2)}) collective-permute-start(f32[2,112,128]{2,1,0:T(8,128)} %copy-done.21), channel_id=1, source_target_pairs={{0,496},{16,32},{32,16},{48,64},{64,48},{80,96},{96,80},{112,128},... | collective-permute-start | bytes 344072 | tf_op jit(solution)/shard_map/ppermute | solution.py:840
  116.3 2.2 %collective-permute-start.13 = (f32[2,112,128]{2,1,0:T(8,128)}, f32[2,112,128]{2,1,0:T(8,128)S(1)}, u32[]{:S(2)}, u32[]{:S(2)}) collective-permute-start(f32[2,112,128]{2,1,0:T(8,128)} %copy-done.20), channel_id=1, source_target_pairs={{0,16},{16,0},{32,48},{48,32},{64,80},{80,64},{96,112},{112,96},{1... | collective-permute-start | bytes 344072 | tf_op jit(solution)/shard_map/ppermute | solution.py:840
  118.5 5.9 %collective-permute-done.12.refs_1_.refs_4_ = f32[2,112,128]{2,1,0:T(8,128)S(1)} collective-permute-done((f32[2,112,128]{2,1,0:T(8,128)}, f32[2,112,128]{2,1,0:T(8,128)S(1)}, u32[]{:S(2)}, u32[]{:S(2)}) %collective-permute-start.12) | collective-permute-done | bytes 114720 | tf_op jit(solution)/shard_map/ppermute | solution.py:840
  125.7 0.9 copy-done.11
  126.6 0.9 copy-done.13
  127.5 1.1 pass_kernel.1.refs_1_
  128.6 2.2 %collective-permute-start.14 = (f32[1088,128]{1,0:T(8,128)S(1)}, f32[1088,128]{1,0:T(8,128)S(1)}, u32[]{:S(2)}, u32[]{:S(2)}) collective-permute-start(f32[1088,128]{1,0:T(8,128)S(1)} %pass_kernel.1.refs_1_), channel_id=1, source_target_pairs={{0,1},{1,0},{2,3},{3,2},{4,5},{5,4},{6,7},{7,6},{8,9},{9,8},{10,11... | collective-permute-start | bytes 1671176 | tf_op jit(solution)/shard_map/ppermute | solution.py:922
  130.8 1.7 collective-permute-done.14.refs_2_
  132.6 0.9 copy-done.6
  134.4 7.4 %coarse_kernel.1 = (f32[2,64,128]{2,1,0:T(8,128)S(1)}, f32[2,64,128]{2,1,0:T(8,128)S(1)}, f32[2,64,128]{2,1,0:T(8,128)S(1)}, f32[2,64,128]{2,1,0:T(8,128)S(1)}, ...) custom-call(s32[2]{0:T(128)S(1)} %pad_add_fusion.refs_0_, f32[1088,128]{1,0:T(8,128)S(1)} %pass_kernel.1.refs_1_, ...), custom_call_target="tpu_custom_call" | custom-call | tf_op jit(solution)/shard_map/coarse_kernel/pallas_call | solution.py:825
  141.8 5.2 %collective-permute-start.15 = (f32[2,16,128]{2,1,0:T(8,128)S(1)}, f32[2,16,128]{2,1,0:T(8,128)S(1)}, u32[]{:S(2)}, u32[]{:S(2)}) collective-permute-start(f32[2,16,128]{2,1,0:T(8,128)S(1)} %get-tuple-element.96), channel_id=1, source_target_pairs={{0,496},{16,32},{32,16},{48,64},{64,48},{80,96},{96,80},{112,128},... | collective-permute-start | bytes 49160 | tf_op jit(solution)/shard_map/ppermute | solution.py:840
  147.0 1.9 %collective-permute-start.16 = (f32[2,16,128]{2,1,0:T(8,128)S(1)}, f32[2,16,128]{2,1,0:T(8,128)S(1)}, u32[]{:S(2)}, u32[]{:S(2)}) collective-permute-start(f32[2,16,128]{2,1,0:T(8,128)S(1)} %get-tuple-element.97), channel_id=1, source_target_pairs={{0,16},{16,0},{32,48},{48,32},{64,80},{80,64},{96,112},{112,96},{1... | collective-permute-start | bytes 49160 | tf_op jit(solution)/shard_map/ppermute | solution.py:840
  148.9 2.1 %collective-permute-done.15.refs_5_ = f32[2,16,128]{2,1,0:T(8,128)S(1)} collective-permute-done((f32[2,16,128]{2,1,0:T(8,128)S(1)}, f32[2,16,128]{2,1,0:T(8,128)S(1)}, u32[]{:S(2)}, u32[]{:S(2)}) %collective-permute-start.15) | collective-permute-done | bytes 16416 | tf_op jit(solution)/shard_map/ppermute | solution.py:840
  151.1 1.6 collective-permute-done.16.refs_6_
  152.6 2.2 %sixth_kernel.1 = (f32[2,512,128]{2,1,0:T(8,128)S(1)}, f32[2,512,128]{2,1,0:T(8,128)S(1)}, f32[2,512,128]{2,1,0:T(8,128)S(1)}, f32[2,64,128]{2,1,0:T(8,128)S(1)}, f32[2,64,128]{2,1,0:T(8,128)S(1)}) custom-call(s32[2]{0:T(128)S(1)} %pad_add_fusion.refs_0_, f32[2,64,128]{2,1,0:T(8,128)S(1)} %get-tuple-element.92.refs_1_, ...), custom_call_target="tpu_custom_call" | custom-call | tf_op jit(solution)/shard_map/sixth_kernel/pallas_call | solution.py:825
  154.8 4.3 %collective-permute-start.17 = (f32[2,64,128]{2,1,0:T(8,128)S(1)}, f32[2,64,128]{2,1,0:T(8,128)S(1)}, u32[]{:S(2)}, u32[]{:S(2)}) collective-permute-start(f32[2,64,128]{2,1,0:T(8,128)S(1)} %get-tuple-element.101), channel_id=1, source_target_pairs={{0,496},{16,32},{32,16},{48,64},{64,48},{80,96},{96,80},{112,128},... | collective-permute-start | bytes 196616 | tf_op jit(solution)/shard_map/ppermute | solution.py:840
  159.1 1.9 %collective-permute-start.18 = (f32[2,64,128]{2,1,0:T(8,128)S(1)}, f32[2,64,128]{2,1,0:T(8,128)S(1)}, u32[]{:S(2)}, u32[]{:S(2)}) collective-permute-start(f32[2,64,128]{2,1,0:T(8,128)S(1)} %get-tuple-element.102), channel_id=1, source_target_pairs={{0,16},{16,0},{32,48},{48,32},{64,80},{80,64},{96,112},{112,96},{1... | collective-permute-start | bytes 196616 | tf_op jit(solution)/shard_map/ppermute | solution.py:840
  161.0 1.3 inner_kernel.3.refs_3_
  162.3 2.3 %collective-permute-done.17.refs_4_ = f32[2,64,128]{2,1,0:T(8,128)S(1)} collective-permute-done((f32[2,64,128]{2,1,0:T(8,128)S(1)}, f32[2,64,128]{2,1,0:T(8,128)S(1)}, u32[]{:S(2)}, u32[]{:S(2)}) %collective-permute-start.17) | collective-permute-done | bytes 65568 | tf_op jit(solution)/shard_map/ppermute | solution.py:840
  165.3 1.8 %seventh_kernel.1 = (f32[2,512,128]{2,1,0:T(8,128)S(1)}, f32[2,512,128]{2,1,0:T(8,128)S(1)}, f32[2,512,128]{2,1,0:T(8,128)S(1)}, f32[2,512,128]{2,1,0:T(8,128)S(...) custom-call(s32[2]{0:T(128)S(1)} %pad_add_fusion.refs_0_, f32[2,1536,128]{2,1,0:T(8,128)S(1)} %copy-done.3, ...), custom_call_target="tpu_custom_call" | custom-call | tf_op jit(solution)/shard_map/seventh_kernel/pallas_call | solution.py:825
  167.1 5.2 %collective-permute-start.19 = (f32[2,64,128]{2,1,0:T(8,128)S(1)}, f32[2,64,128]{2,1,0:T(8,128)S(1)}, u32[]{:S(2)}, u32[]{:S(2)}) collective-permute-start(f32[2,64,128]{2,1,0:T(8,128)S(1)} %get-tuple-element.107), channel_id=1, source_target_pairs={{0,496},{16,32},{32,16},{48,64},{64,48},{80,96},{96,80},{112,128},... | collective-permute-start | bytes 196616 | tf_op jit(solution)/shard_map/ppermute | solution.py:840
  172.3 1.9 %collective-permute-start.20 = (f32[2,64,128]{2,1,0:T(8,128)S(1)}, f32[2,64,128]{2,1,0:T(8,128)S(1)}, u32[]{:S(2)}, u32[]{:S(2)}) collective-permute-start(f32[2,64,128]{2,1,0:T(8,128)S(1)} %get-tuple-element.108), channel_id=1, source_target_pairs={{0,16},{16,0},{32,48},{48,32},{64,80},{80,64},{96,112},{112,96},{1... | collective-permute-start | bytes 196616 | tf_op jit(solution)/shard_map/ppermute | solution.py:840
  174.2 1.4 inner_last_kernel.1.refs_8_
  175.6 1.3 collective-permute-done.19.refs_5_
  176.8 1.6 collective-permute-done.20.refs_6_
  178.4 1.4 last_kernel.1
  (47 shorter events, 9.6 us)
Async XLA Ops:
  0.1 1.1 copy-start.7
  1.2 0.9 copy-start.14
  2.2 0.7 copy-start.19
  4.0 11.5 %collective-permute-start = (f32[1024,128]{1,0:T(8,128)S(1)}, f32[1024,128]{1,0:T(8,128)S(1)}, u32[]{:S(2)}, u32[]{:S(2)}) collective-permute-start(f32[1024,128]{1,0:T(8,128)S(1)} %get-tuple-element.59), channel_id=1, source_target_pairs={{0,15},{1,2},{2,1},{3,4},{4,3},{5,6},{6,5},{7,8},{8,7},{9,10},{10,... | collective-permute-start | bytes 1572872 | tf_op jit(solution)/shard_map/ppermute | solution.py:840
  6.9 8.6 %collective-permute-start.1 = (f32[1024,128]{1,0:T(8,128)S(1)}, f32[1024,128]{1,0:T(8,128)S(1)}, u32[]{:S(2)}, u32[]{:S(2)}) collective-permute-start(f32[1024,128]{1,0:T(8,128)S(1)} %get-tuple-element.60), channel_id=1, source_target_pairs={{0,1},{1,0},{2,3},{3,2},{4,5},{5,4},{6,7},{7,6},{8,9},{9,8},{10,11... | collective-permute-start | bytes 1572872 | tf_op jit(solution)/shard_map/ppermute | solution.py:840
  9.6 1.3 copy-start
  10.9 4.7 %copy-start.1 = (f32[2448,128]{1,0:T(8,128)S(1)}, f32[2448,128]{1,0:T(8,128)}, u32[]{:S(2)}) copy-start(f32[2448,128]{1,0:T(8,128)} %constant.11.clone.refs_1_.refs_6_.refs_3_.refs_9_.refs_7_.refs_8_.refs_10_) | copy-start | bytes 3760132
  17.4 17.0 %collective-permute-start.2 = (f32[2,128,128]{2,1,0:T(8,128)S(1)}, f32[2,128,128]{2,1,0:T(8,128)S(1)}, u32[]{:S(2)}, u32[]{:S(2)}) collective-permute-start(f32[2,128,128]{2,1,0:T(8,128)S(1)} %get-tuple-element.63), channel_id=1, source_target_pairs={{0,496},{16,32},{32,16},{48,64},{64,48},{80,96},{96,80},{112,128},... | collective-permute-start | bytes 393224 | tf_op jit(solution)/shard_map/ppermute | solution.py:840
  31.5 6.9 %collective-permute-start.3 = (f32[2,128,128]{2,1,0:T(8,128)S(1)}, f32[2,128,128]{2,1,0:T(8,128)S(1)}, u32[]{:S(2)}, u32[]{:S(2)}) collective-permute-start(f32[2,128,128]{2,1,0:T(8,128)S(1)} %get-tuple-element.64), channel_id=1, source_target_pairs={{0,16},{16,0},{32,48},{48,32},{64,80},{80,64},{96,112},{112,96},{1... | collective-permute-start | bytes 393224 | tf_op jit(solution)/shard_map/ppermute | solution.py:840
  40.1 9.8 %collective-permute-start.4 = (f32[2,64,128]{2,1,0:T(8,128)S(1)}, f32[2,64,128]{2,1,0:T(8,128)S(1)}, u32[]{:S(2)}, u32[]{:S(2)}) collective-permute-start(f32[2,64,128]{2,1,0:T(8,128)S(1)} %get-tuple-element.70), channel_id=1, source_target_pairs={{0,496},{16,32},{32,16},{48,64},{64,48},{80,96},{96,80},{112,128},... | collective-permute-start | bytes 196616 | tf_op jit(solution)/shard_map/ppermute | solution.py:840
  43.8 6.2 %collective-permute-start.5 = (f32[2,64,128]{2,1,0:T(8,128)S(1)}, f32[2,64,128]{2,1,0:T(8,128)S(1)}, u32[]{:S(2)}, u32[]{:S(2)}) collective-permute-start(f32[2,64,128]{2,1,0:T(8,128)S(1)} %get-tuple-element.71), channel_id=1, source_target_pairs={{0,16},{16,0},{32,48},{48,32},{64,80},{80,64},{96,112},{112,96},{1... | collective-permute-start | bytes 196616 | tf_op jit(solution)/shard_map/ppermute | solution.py:840
  52.8 24.1 %copy-start.2 = (f32[2,1536,128]{2,1,0:T(8,128)}, f32[2,1536,128]{2,1,0:T(8,128)S(1)}, u32[]{:S(2)}) copy-start(f32[2,1536,128]{2,1,0:T(8,128)S(1)} %get-tuple-element.74.refs_8_.refs_1_) | copy-start | bytes 4718596
  52.8 9.5 %collective-permute-start.6 = (f32[2,40,128]{2,1,0:T(8,128)S(1)}, f32[2,40,128]{2,1,0:T(8,128)S(1)}, u32[]{:S(2)}, u32[]{:S(2)}) collective-permute-start(f32[2,40,128]{2,1,0:T(8,128)S(1)} %get-tuple-element.77), channel_id=1, source_target_pairs={{0,496},{16,32},{32,16},{48,64},{64,48},{80,96},{96,80},{112,128},... | collective-permute-start | bytes 122888 | tf_op jit(solution)/shard_map/ppermute | solution.py:840
  58.7 6.0 %collective-permute-start.7 = (f32[2,40,128]{2,1,0:T(8,128)S(1)}, f32[2,40,128]{2,1,0:T(8,128)S(1)}, u32[]{:S(2)}, u32[]{:S(2)}) collective-permute-start(f32[2,40,128]{2,1,0:T(8,128)S(1)} %get-tuple-element.78), channel_id=1, source_target_pairs={{0,16},{16,0},{32,48},{48,32},{64,80},{80,64},{96,112},{112,96},{1... | collective-permute-start | bytes 122888 | tf_op jit(solution)/shard_map/ppermute | solution.py:840
  66.0 12.1 %copy-start.8 = (f32[2,64,128]{2,1,0:T(8,128)}, f32[2,64,128]{2,1,0:T(8,128)S(1)}, u32[]{:S(2)}) copy-start(f32[2,64,128]{2,1,0:T(8,128)S(1)} %get-tuple-element.82.refs_3_.refs_7_) | copy-start | bytes 196612
  66.0 9.2 %collective-permute-start.8 = (f32[2,16,128]{2,1,0:T(8,128)S(1)}, f32[2,16,128]{2,1,0:T(8,128)S(1)}, u32[]{:S(2)}, u32[]{:S(2)}) collective-permute-start(f32[2,16,128]{2,1,0:T(8,128)S(1)} %get-tuple-element.84), channel_id=1, source_target_pairs={{0,496},{16,32},{32,16},{48,64},{64,48},{80,96},{96,80},{112,128},... | collective-permute-start | bytes 49160 | tf_op jit(solution)/shard_map/ppermute | solution.py:840
  69.6 5.7 %collective-permute-start.9 = (f32[2,16,128]{2,1,0:T(8,128)S(1)}, f32[2,16,128]{2,1,0:T(8,128)S(1)}, u32[]{:S(2)}, u32[]{:S(2)}) collective-permute-start(f32[2,16,128]{2,1,0:T(8,128)S(1)} %get-tuple-element.85), channel_id=1, source_target_pairs={{0,16},{16,0},{32,48},{48,32},{64,80},{80,64},{96,112},{112,96},{1... | collective-permute-start | bytes 49160 | tf_op jit(solution)/shard_map/ppermute | solution.py:840
  76.9 0.6 copy-start.15
  77.5 0.6 copy-start.17
  78.8 23.0 %all-to-all-start = ((f32[32,8,128]{2,1,0:T(8,128)}), f32[32,8,128]{2,1,0:T(8,128)}, u32[]{:S(2)}, u32[]{:S(2)}) async-start(f32[32,8,128]{2,1,0:T(8,128)} %broadcast_in_dim.4), calls=%async_computation | async-start | bytes 262144 | tf_op jit(solution)/shard_map/all_to_all | solution.py:846
  84.6 9.1 %collective-permute-start.10 = (f32[192,128]{1,0:T(8,128)}, f32[192,128]{1,0:T(8,128)S(1)}, u32[]{:S(2)}, u32[]{:S(2)}) collective-permute-start(f32[192,128]{1,0:T(8,128)} %copy-done.15), channel_id=1, source_target_pairs={{0,15},{1,2},{2,1},{3,4},{4,3},{5,6},{6,5},{7,8},{8,7},{9,10},{10,... | collective-permute-start | bytes 294920 | tf_op jit(solution)/shard_map/ppermute | solution.py:840
  86.5 8.3 %collective-permute-start.11 = (f32[192,128]{1,0:T(8,128)}, f32[192,128]{1,0:T(8,128)S(1)}, u32[]{:S(2)}, u32[]{:S(2)}) collective-permute-start(f32[192,128]{1,0:T(8,128)} %copy-done.17), channel_id=1, source_target_pairs={{0,1},{1,0},{2,3},{3,2},{4,5},{5,4},{6,7},{7,6},{8,9},{9,8},{10,11... | collective-permute-start | bytes 294920 | tf_op jit(solution)/shard_map/ppermute | solution.py:840
  94.8 0.9 copy-start.16
  95.7 0.9 copy-start.18
  97.8 0.7 copy-start.4
  98.5 0.6 copy-start.20
  99.2 0.7 copy-start.21
  101.9 0.9 copy-start.5
  104.7 21.0 %all-to-all-start.1 = ((f32[8,136,128]{2,1,0:T(8,128)}), f32[8,136,128]{2,1,0:T(8,128)}, u32[]{:S(2)}, u32[]{:S(2)}) async-start(f32[8,136,128]{2,1,0:T(8,128)} %broadcast_in_dim.5), calls=%async_computation.1 | async-start | bytes 1114112 | tf_op jit(solution)/shard_map/all_to_all | solution.py:846
  113.9 10.5 %collective-permute-start.12 = (f32[2,112,128]{2,1,0:T(8,128)}, f32[2,112,128]{2,1,0:T(8,128)S(1)}, u32[]{:S(2)}, u32[]{:S(2)}) collective-permute-start(f32[2,112,128]{2,1,0:T(8,128)} %copy-done.21), channel_id=1, source_target_pairs={{0,496},{16,32},{32,16},{48,64},{64,48},{80,96},{96,80},{112,128},... | collective-permute-start | bytes 344072 | tf_op jit(solution)/shard_map/ppermute | solution.py:840
  116.3 8.8 %collective-permute-start.13 = (f32[2,112,128]{2,1,0:T(8,128)}, f32[2,112,128]{2,1,0:T(8,128)S(1)}, u32[]{:S(2)}, u32[]{:S(2)}) collective-permute-start(f32[2,112,128]{2,1,0:T(8,128)} %copy-done.20), channel_id=1, source_target_pairs={{0,16},{16,0},{32,48},{48,32},{64,80},{80,64},{96,112},{112,96},{1... | collective-permute-start | bytes 344072 | tf_op jit(solution)/shard_map/ppermute | solution.py:840
  124.4 0.7 copy-start.10
  125.1 0.6 copy-start.12
  125.7 0.9 copy-start.11
  126.6 0.9 copy-start.13
  128.6 24.0 %copy-start.3 = (f32[2,1536,128]{2,1,0:T(8,128)S(1)}, f32[2,1536,128]{2,1,0:T(8,128)}, u32[]{:S(2)}) copy-start(f32[2,1536,128]{2,1,0:T(8,128)} %copy-done.2) | copy-start | bytes 4718596
  128.6 4.0 %collective-permute-start.14 = (f32[1088,128]{1,0:T(8,128)S(1)}, f32[1088,128]{1,0:T(8,128)S(1)}, u32[]{:S(2)}, u32[]{:S(2)}) collective-permute-start(f32[1088,128]{1,0:T(8,128)S(1)} %pass_kernel.1.refs_1_), channel_id=1, source_target_pairs={{0,1},{1,0},{2,3},{3,2},{4,5},{5,4},{6,7},{7,6},{8,9},{9,8},{10,11... | collective-permute-start | bytes 1671176 | tf_op jit(solution)/shard_map/ppermute | solution.py:922
  132.6 0.9 copy-start.6
  133.5 0.8 copy-start.9
  141.8 9.2 %collective-permute-start.15 = (f32[2,16,128]{2,1,0:T(8,128)S(1)}, f32[2,16,128]{2,1,0:T(8,128)S(1)}, u32[]{:S(2)}, u32[]{:S(2)}) collective-permute-start(f32[2,16,128]{2,1,0:T(8,128)S(1)} %get-tuple-element.96), channel_id=1, source_target_pairs={{0,496},{16,32},{32,16},{48,64},{64,48},{80,96},{96,80},{112,128},... | collective-permute-start | bytes 49160 | tf_op jit(solution)/shard_map/ppermute | solution.py:840
  147.0 5.6 %collective-permute-start.16 = (f32[2,16,128]{2,1,0:T(8,128)S(1)}, f32[2,16,128]{2,1,0:T(8,128)S(1)}, u32[]{:S(2)}, u32[]{:S(2)}) collective-permute-start(f32[2,16,128]{2,1,0:T(8,128)S(1)} %get-tuple-element.97), channel_id=1, source_target_pairs={{0,16},{16,0},{32,48},{48,32},{64,80},{80,64},{96,112},{112,96},{1... | collective-permute-start | bytes 49160 | tf_op jit(solution)/shard_map/ppermute | solution.py:840
  154.8 9.8 %collective-permute-start.17 = (f32[2,64,128]{2,1,0:T(8,128)S(1)}, f32[2,64,128]{2,1,0:T(8,128)S(1)}, u32[]{:S(2)}, u32[]{:S(2)}) collective-permute-start(f32[2,64,128]{2,1,0:T(8,128)S(1)} %get-tuple-element.101), channel_id=1, source_target_pairs={{0,496},{16,32},{32,16},{48,64},{64,48},{80,96},{96,80},{112,128},... | collective-permute-start | bytes 196616 | tf_op jit(solution)/shard_map/ppermute | solution.py:840
  159.1 6.2 %collective-permute-start.18 = (f32[2,64,128]{2,1,0:T(8,128)S(1)}, f32[2,64,128]{2,1,0:T(8,128)S(1)}, u32[]{:S(2)}, u32[]{:S(2)}) collective-permute-start(f32[2,64,128]{2,1,0:T(8,128)S(1)} %get-tuple-element.102), channel_id=1, source_target_pairs={{0,16},{16,0},{32,48},{48,32},{64,80},{80,64},{96,112},{112,96},{1... | collective-permute-start | bytes 196616 | tf_op jit(solution)/shard_map/ppermute | solution.py:840
  167.1 9.8 %collective-permute-start.19 = (f32[2,64,128]{2,1,0:T(8,128)S(1)}, f32[2,64,128]{2,1,0:T(8,128)S(1)}, u32[]{:S(2)}, u32[]{:S(2)}) collective-permute-start(f32[2,64,128]{2,1,0:T(8,128)S(1)} %get-tuple-element.107), channel_id=1, source_target_pairs={{0,496},{16,32},{32,16},{48,64},{64,48},{80,96},{96,80},{112,128},... | collective-permute-start | bytes 196616 | tf_op jit(solution)/shard_map/ppermute | solution.py:840
  172.3 6.2 %collective-permute-start.20 = (f32[2,64,128]{2,1,0:T(8,128)S(1)}, f32[2,64,128]{2,1,0:T(8,128)S(1)}, u32[]{:S(2)}, u32[]{:S(2)}) collective-permute-start(f32[2,64,128]{2,1,0:T(8,128)S(1)} %get-tuple-element.108), channel_id=1, source_target_pairs={{0,16},{16,0},{32,48},{48,32},{64,80},{80,64},{96,112},{112,96},{1... | collective-permute-start | bytes 196616 | tf_op jit(solution)/shard_map/ppermute | solution.py:840
where the time goes:
time: 181 us; the launch traced here: 180 us
  starting transfers between devices  91.5 us (51%)
  waiting for transfers between devices  38.9 us (21%)
  Pallas kernels  32.6 us (18%)
  local copies, waits for them, and re-layouts  16.4 us (9%)
    ppermute x10, starting transfers between devices, exchange(): lax.ppermute(far, axis, pairs_far)  48.8 us
    pallas_call x18, Pallas kernels, call(): pl.pallas_call(body, out_shape=[jax.ShapeDtypeStruct(s, F32) for s in out...  32.6 us
    ppermute x10, starting transfers between devices, exchange(): lax.ppermute(near, axis, pairs_near)  25.5 us
    ppermute x10, waiting for transfers between devices, exchange(): lax.ppermute(far, axis, pairs_far)  23.8 us
    all_to_all x2, starting transfers between devices, spread(): lax.all_to_all(copies, axis, 0, 0, axis_index_groups=groups)  14.9 us
    unnamed x44, local copies, waits for them, and re-layouts  14.9 us
    ppermute x10, waiting for transfers between devices, exchange(): lax.ppermute(near, axis, pairs_near)  11.2 us
  transfers between devices with their start and end apart: 23, of which 17 were waited for; matrix products, arithmetic and copies ran while one was open for 0% of the time, Pallas kernels for 4%

commit v1 on v0

--- a/solution.py
+++ b/solution.py
@@ -153,8 +153,8 @@
         return value if index is Ellipsis else value[index]
 
 
-def dot(a, b):
-    return jnp.dot(a, b, preferred_element_type=F32, precision=lax.Precision.HIGHEST)
+def dot(a, b, precision=lax.Precision.HIGH):
+    return jnp.dot(a, b, preferred_element_type=F32, precision=precision)
 
 
 def iota(rows, axis):
@@ -418,7 +418,8 @@
 def coarsen_kernel(g8, w4, w2, sample, sq4, g4, diag4, edges, upper):
     low = []
     for d in range(3):
-        coarse = jnp.exp(dot(sample[...], jnp.log(wide(g8, 512 * d, 512))))
+        logs = jnp.log(wide(g8, 512 * d, 512))
+        coarse = jnp.exp(dot(sample[...], logs, lax.Precision.HIGHEST))
         put(g4, 64 * d, 64, coarse[:64] * jnp.concatenate([w4[...], w4[...]], axis=1))
         low.append([coarse[64:72, :LANES] * w2[...], coarse[64:72, LANES:] * w2[...]])
     put(diag4, 0, 64, dot(sq4[...], wide(g4, 0, 192)))
@@ -621,10 +622,6 @@
     out[4 * ns : 4 * ns + n] = total(
         [pltpu.roll(p, 16 * k, 1) if k else p for k, p in enumerate(parts)]
     )
-
-
-def pass_kernel(rows, first, second, out):
-    out[...] = rows[...]
 
 
 def coarse_kernel(
@@ -777,7 +774,9 @@
         u[h, r : r + 8] = new
         out[h, r : r + 8] = sol[h, r : r + 8] + new
     fine_front(u, g8, acc2, bd, bdt)
-    send_faces(acc2, even, face_a, face_b, 64)
+    for out, plane in ((face_b, jnp.where(even, 448, 0)), (face_a, jnp.where(even, 0, 448))):
+        rows = pl.ds(pl.multiple_of(plane, 8), 64)
+        out[...] = own_part(acc2[0, rows, :], acc2[1, rows, :])
 
 
 def inner_last_kernel(u, g8, acc, res, sol, inv8, bd, bdt, out, full):
@@ -795,15 +794,19 @@
 
 
 def last_kernel(pos, res, sol, u, acc, a, b, inv8, inner, out):
-    got = (is_even(pos, 0), a, b)
+    even = is_even(pos, 0)
     out[64:448] = inner[...]
     for r in [*range(0, 64, 8), *range(448, 512, 8)]:
         halves = []
         for h in range(2):
-            now = res[h, r : r + 8] - full_of(acc, got, h, r)
-            new = KEEP * u[h, r : r + 8] + GAIN * inv8[h, r : r + 8] * now
-            halves.append(sol[h, r : r + 8] + new)
-        out[r : r + 8] = own_part(*halves)
+            inv = inv8[h, r : r + 8]
+            now = res[h, r : r + 8] - acc[h, r : r + 8]
+            halves.append(sol[h, r : r + 8] + KEEP * u[h, r : r + 8] + GAIN * inv * now)
+        at = r % 64
+        x, y = a[at : at + 8], b[at : at + 8]
+        face = jnp.where(even, x, y) if r < 64 else jnp.where(even, y, x)
+        inv = own_part(inv8[0, r : r + 8], inv8[1, r : r + 8])
+        out[r : r + 8] = own_part(*halves) - GAIN * inv * face
 
 
 def call(kernel, args, outs, scratch=(), scalars=1):
@@ -918,7 +921,6 @@
     )
     cores = [list(range(core, na, 2)) for core in range(2)]
     columns = spread(columns, "azim", cores)
-    (columns,) = call(pass_kernel, (columns, *sides), [columns.shape], (), 0)
     others = lax.ppermute(columns, "azim", [(i, i ^ 1) for i in range(na)])
     whole = (ns, na * LANES)
     res4, u4, sol4, acc, a, b = call(
@@ -954,7 +956,7 @@
     res8, sol8, u8, acc, a, b = call(
         seventh_kernel,
         (pos, kept, sol8, acc, a, b, inv8, g8, "bd", "bdt"),
-        [fine, fine, fine, fine] + face8,
+        [fine, fine, fine, fine] + [(64, LANES)] * 2,
     )
     a, b = exchange(a, b, "stream")
     (inside,) = call(

time: 181 us -> 177 us (0.978)
  the two profiles are of different devices: /device:TPU:2 before, /device:TPU:8 now
where the time goes in v1:
time: 177 us; the launch traced here: 176 us
  starting transfers between devices  76.5 us (43%)
  waiting for transfers between devices  48.3 us (27%)
  Pallas kernels  27 us (15%)
  blocking collectives  13.2 us (7%)
  local copies, waits for them, and re-layouts  10.7 us (6%)
    ppermute x10, starting transfers between devices, exchange(): lax.ppermute(far, axis, pairs_far)  47.9 us
    ppermute x10, waiting for transfers between devices, exchange(): lax.ppermute(far, axis, pairs_far)  32 us
    pallas_call x17, Pallas kernels, call(): pl.pallas_call(body, out_shape=[jax.ShapeDtypeStruct(s, F32) for s in out...  27 us
    ppermute x10, starting transfers between devices, exchange(): lax.ppermute(near, axis, pairs_near)  20.9 us
    all_to_all x1, blocking collectives, spread(): lax.all_to_all(copies, axis, 0, 0, axis_index_groups=groups)  13.2 us
    ppermute x10, waiting for transfers between devices, exchange(): lax.ppermute(near, axis, pairs_near)  10.4 us
    unnamed x40, local copies, waits for them, and re-layouts  10 us
    all_to_all x1, waiting for transfers between devices, spread(): lax.all_to_all(copies, axis, 0, 0, axis_index_groups=groups)  5.94 us
  transfers between devices with their start and end apart: 22, of which 16 were waited for; matrix products, arithmetic and copies ran while one was open for 0% of the time, Pallas kernels for 3%

profile of v1, /device:TPU:8, one launch (start us, length us, event | category | flops | bytes accessed | tf_op | source)
XLA Modules:
  0.0 176.2 jit_solution(16438443663231524178)
XLA Ops:
  0.1 1.1 copy-done.7
  1.2 0.9 copy-done.10
  2.2 0.7 copy-done.15
  2.8 1.2 order_kernel.1
  4.0 1.9 %collective-permute-start = (f32[1024,128]{1,0:T(8,128)S(1)}, f32[1024,128]{1,0:T(8,128)S(1)}, u32[]{:S(2)}, u32[]{:S(2)}) collective-permute-start(f32[1024,128]{1,0:T(8,128)S(1)} %get-tuple-element.59), channel_id=1, source_target_pairs={{0,15},{1,2},{2,1},{3,4},{4,3},{5,6},{6,5},{7,8},{8,7},{9,10},{10,... | collective-permute-start | bytes 1572872 | tf_op jit(solution)/shard_map/ppermute | solution.py:843
  6.0 3.4 %collective-permute-start.1 = (f32[1024,128]{1,0:T(8,128)S(1)}, f32[1024,128]{1,0:T(8,128)S(1)}, u32[]{:S(2)}, u32[]{:S(2)}) collective-permute-start(f32[1024,128]{1,0:T(8,128)S(1)} %get-tuple-element.60), channel_id=1, source_target_pairs={{0,1},{1,0},{2,3},{3,2},{4,5},{5,4},{6,7},{7,6},{8,9},{9,8},{10,11... | collective-permute-start | bytes 1572872 | tf_op jit(solution)/shard_map/ppermute | solution.py:843
  9.4 1.3 copy-done
  11.0 9.2 %collective-permute-done.refs_4_ = f32[1024,128]{1,0:T(8,128)S(1)} collective-permute-done((f32[1024,128]{1,0:T(8,128)S(1)}, f32[1024,128]{1,0:T(8,128)S(1)}, u32[]{:S(2)}, u32[]{:S(2)}) %collective-permute-start) | collective-permute-done | bytes 524320 | tf_op jit(solution)/shard_map/ppermute | solution.py:843
  20.2 1.8 %setup_kernel.1 = (f32[2,1536,128]{2,1,0:T(8,128)S(1)}, f32[2,512,128]{2,1,0:T(8,128)S(1)}, f32[2,512,128]{2,1,0:T(8,128)S(1)}, f32[2,128,128]{2,1,0:T(8,128)S(1)}, f32[2,128,128]{2,1,0:T(8,128)S(1)}) custom-call(s32[2]{0:T(128)S(1)} %pad_add_fusion.refs_0_, f32[1536,128]{1,0:T(8,128)S(1)} %get-tuple-element.57.refs_0_.refs_1_, ...), custom_call_target="tpu_custom_call" | custom-call | tf_op jit(solution)/shard_map/setup_kernel/pallas_call | solution.py:828
  21.9 13.1 %collective-permute-start.2 = (f32[2,128,128]{2,1,0:T(8,128)S(1)}, f32[2,128,128]{2,1,0:T(8,128)S(1)}, u32[]{:S(2)}, u32[]{:S(2)}) collective-permute-start(f32[2,128,128]{2,1,0:T(8,128)S(1)} %get-tuple-element.63), channel_id=1, source_target_pairs={{0,496},{16,32},{32,16},{48,64},{64,48},{80,96},{96,80},{112,128},... | collective-permute-start | bytes 393224 | tf_op jit(solution)/shard_map/ppermute | solution.py:843
  35.1 1.9 %collective-permute-start.3 = (f32[2,128,128]{2,1,0:T(8,128)S(1)}, f32[2,128,128]{2,1,0:T(8,128)S(1)}, u32[]{:S(2)}, u32[]{:S(2)}) collective-permute-start(f32[2,128,128]{2,1,0:T(8,128)S(1)} %get-tuple-element.64), channel_id=1, source_target_pairs={{0,16},{16,0},{32,48},{48,32},{64,80},{80,64},{96,112},{112,96},{1... | collective-permute-start | bytes 393224 | tf_op jit(solution)/shard_map/ppermute | solution.py:843
  37.0 1.0 collective-permute-done.2.refs_3_
  38.0 3.9 %collective-permute-done.3.refs_4_ = f32[2,128,128]{2,1,0:T(8,128)S(1)} collective-permute-done((f32[2,128,128]{2,1,0:T(8,128)S(1)}, f32[2,128,128]{2,1,0:T(8,128)S(1)}, u32[]{:S(2)}, u32[]{:S(2)}) %collective-permute-start.3) | collective-permute-done | bytes 131104 | tf_op jit(solution)/shard_map/ppermute | solution.py:843
  41.9 1.6 first_kernel.1
  43.5 3.6 %collective-permute-start.4 = (f32[2,64,128]{2,1,0:T(8,128)S(1)}, f32[2,64,128]{2,1,0:T(8,128)S(1)}, u32[]{:S(2)}, u32[]{:S(2)}) collective-permute-start(f32[2,64,128]{2,1,0:T(8,128)S(1)} %get-tuple-element.70), channel_id=1, source_target_pairs={{0,496},{16,32},{32,16},{48,64},{64,48},{80,96},{96,80},{112,128},... | collective-permute-start | bytes 196616 | tf_op jit(solution)/shard_map/ppermute | solution.py:843
  47.1 1.9 %collective-permute-start.5 = (f32[2,64,128]{2,1,0:T(8,128)S(1)}, f32[2,64,128]{2,1,0:T(8,128)S(1)}, u32[]{:S(2)}, u32[]{:S(2)}) collective-permute-start(f32[2,64,128]{2,1,0:T(8,128)S(1)} %get-tuple-element.71), channel_id=1, source_target_pairs={{0,16},{16,0},{32,48},{48,32},{64,80},{80,64},{96,112},{112,96},{1... | collective-permute-start | bytes 196616 | tf_op jit(solution)/shard_map/ppermute | solution.py:843
  49.1 1.4 coarsen_kernel.1
  50.5 0.8 inner_kernel.2.refs_3_
  51.3 2.0 %collective-permute-done.4.refs_4_ = f32[2,64,128]{2,1,0:T(8,128)S(1)} collective-permute-done((f32[2,64,128]{2,1,0:T(8,128)S(1)}, f32[2,64,128]{2,1,0:T(8,128)S(1)}, u32[]{:S(2)}, u32[]{:S(2)}) %collective-permute-start.4) | collective-permute-done | bytes 65568 | tf_op jit(solution)/shard_map/ppermute | solution.py:843
  53.3 2.2 %second_kernel.1 = (f32[2,1536,128]{2,1,0:T(8,128)S(1)}, f32[2,64,128]{2,1,0:T(8,128)S(1)}, f32[2,40,128]{2,1,0:T(8,128)S(1)}, f32[2,40,128]{2,1,0:T(8,128)S(1)}) custom-call(s32[2]{0:T(128)S(1)} %pad_add_fusion.refs_0_, f32[2,512,128]{2,1,0:T(8,128)S(1)} %get-tuple-element.66.refs_1_, f32[2,512,128]{2,1,0:T(8,128)S(1)} %get-tuple-element.67.refs_2_.refs_6_.refs_5_.refs_7_, ...), custom_call_target="tpu_custom_call" | custom-call | tf_op jit(solution)/shard_map/second_kernel/pallas_call | solution.py:828
  55.6 5.8 %collective-permute-start.6 = (f32[2,40,128]{2,1,0:T(8,128)S(1)}, f32[2,40,128]{2,1,0:T(8,128)S(1)}, u32[]{:S(2)}, u32[]{:S(2)}) collective-permute-start(f32[2,40,128]{2,1,0:T(8,128)S(1)} %get-tuple-element.77), channel_id=1, source_target_pairs={{0,496},{16,32},{32,16},{48,64},{64,48},{80,96},{96,80},{112,128},... | collective-permute-start | bytes 122888 | tf_op jit(solution)/shard_map/ppermute | solution.py:843
  61.4 1.9 %collective-permute-start.7 = (f32[2,40,128]{2,1,0:T(8,128)S(1)}, f32[2,40,128]{2,1,0:T(8,128)S(1)}, u32[]{:S(2)}, u32[]{:S(2)}) collective-permute-start(f32[2,40,128]{2,1,0:T(8,128)S(1)} %get-tuple-element.78), channel_id=1, source_target_pairs={{0,16},{16,0},{32,48},{48,32},{64,80},{80,64},{96,112},{112,96},{1... | collective-permute-start | bytes 122888 | tf_op jit(solution)/shard_map/ppermute | solution.py:843
  63.4 1.7 collective-permute-done.6.refs_4_
  65.1 2.2 %collective-permute-done.7.refs_5_ = f32[2,40,128]{2,1,0:T(8,128)S(1)} collective-permute-done((f32[2,40,128]{2,1,0:T(8,128)S(1)}, f32[2,40,128]{2,1,0:T(8,128)S(1)}, u32[]{:S(2)}, u32[]{:S(2)}) %collective-permute-start.7) | collective-permute-done | bytes 40992 | tf_op jit(solution)/shard_map/ppermute | solution.py:843
  67.3 1.2 third_kernel.1
  68.5 3.6 %collective-permute-start.8 = (f32[2,16,128]{2,1,0:T(8,128)S(1)}, f32[2,16,128]{2,1,0:T(8,128)S(1)}, u32[]{:S(2)}, u32[]{:S(2)}) collective-permute-start(f32[2,16,128]{2,1,0:T(8,128)S(1)} %get-tuple-element.84), channel_id=1, source_target_pairs={{0,496},{16,32},{32,16},{48,64},{64,48},{80,96},{96,80},{112,128},... | collective-permute-start | bytes 49160 | tf_op jit(solution)/shard_map/ppermute | solution.py:843
  72.1 1.9 %collective-permute-start.9 = (f32[2,16,128]{2,1,0:T(8,128)S(1)}, f32[2,16,128]{2,1,0:T(8,128)S(1)}, u32[]{:S(2)}, u32[]{:S(2)}) collective-permute-start(f32[2,16,128]{2,1,0:T(8,128)S(1)} %get-tuple-element.85), channel_id=1, source_target_pairs={{0,16},{16,0},{32,48},{48,32},{64,80},{80,64},{96,112},{112,96},{1... | collective-permute-start | bytes 49160 | tf_op jit(solution)/shard_map/ppermute | solution.py:843
  74.1 3.7 %collective-permute-done.8.refs_5_ = f32[2,16,128]{2,1,0:T(8,128)S(1)} collective-permute-done((f32[2,16,128]{2,1,0:T(8,128)S(1)}, f32[2,16,128]{2,1,0:T(8,128)S(1)}, u32[]{:S(2)}, u32[]{:S(2)}) %collective-permute-start.8) | collective-permute-done | bytes 16416 | tf_op jit(solution)/shard_map/ppermute | solution.py:843
  77.8 1.3 fourth_kernel.1
  80.4 0.7 broadcast_in_dim.4
  81.1 5.7 %all-to-all-start = ((f32[32,8,128]{2,1,0:T(8,128)}), f32[32,8,128]{2,1,0:T(8,128)}, u32[]{:S(2)}, u32[]{:S(2)}) async-start(f32[32,8,128]{2,1,0:T(8,128)} %broadcast_in_dim.4), calls=%async_computation | async-start | bytes 262144 | tf_op jit(solution)/shard_map/all_to_all | solution.py:849
  86.8 1.9 %collective-permute-start.10 = (f32[192,128]{1,0:T(8,128)}, f32[192,128]{1,0:T(8,128)S(1)}, u32[]{:S(2)}, u32[]{:S(2)}) collective-permute-start(f32[192,128]{1,0:T(8,128)} %copy-done.11), channel_id=1, source_target_pairs={{0,15},{1,2},{2,1},{3,4},{4,3},{5,6},{6,5},{7,8},{8,7},{9,10},{10,... | collective-permute-start | bytes 294920 | tf_op jit(solution)/shard_map/ppermute | solution.py:843
  88.7 1.9 %collective-permute-start.11 = (f32[192,128]{1,0:T(8,128)}, f32[192,128]{1,0:T(8,128)S(1)}, u32[]{:S(2)}, u32[]{:S(2)}) collective-permute-start(f32[192,128]{1,0:T(8,128)} %copy-done.13), channel_id=1, source_target_pairs={{0,1},{1,0},{2,3},{3,2},{4,5},{5,4},{6,7},{7,6},{8,9},{9,8},{10,11... | collective-permute-start | bytes 294920 | tf_op jit(solution)/shard_map/ppermute | solution.py:843
  90.7 2.5 %collective-permute-done.10.refs_3_ = f32[192,128]{1,0:T(8,128)S(1)} collective-permute-done((f32[192,128]{1,0:T(8,128)}, f32[192,128]{1,0:T(8,128)S(1)}, u32[]{:S(2)}, u32[]{:S(2)}) %collective-permute-start.10) | collective-permute-done | bytes 98336 | tf_op jit(solution)/shard_map/ppermute | solution.py:843
  93.1 0.9 copy-done.12
  94.0 0.9 copy-done.14
  94.9 1.0 side_kernel.1
  95.9 0.7 copy-done.4
  96.6 0.6 copy-done.16
  97.9 5.9 %all-to-all-done = f32[32,8,128]{2,1,0:T(8,128)} async-done(((f32[32,8,128]{2,1,0:T(8,128)}), f32[32,8,128]{2,1,0:T(8,128)}, u32[]{:S(2)}, u32[]{:S(2)}) %all-to-all-start) | async-done | bytes 131104 | tf_op jit(solution)/shard_map/all_to_all | solution.py:849
  103.8 0.9 copy-done.5
  104.8 1.1 column_kernel.1
  105.9 13.2 %all_to_all.10 = f32[8,136,128]{2,1,0:T(8,128)S(1)} all-to-all(f32[8,136,128]{2,1,0:T(8,128)S(1)} %broadcast_in_dim.5), channel_id=1, replica_groups={{0,2,4,6,8,10,12,14},{1,3,5,7,9,11,13,15},{16,18,20,22,24,26,28,30},{17..., dimensions={0} | all-to-all | bytes 1114112 | tf_op jit(solution)/shard_map/all_to_all | solution.py:849
  119.2 2.0 %collective-permute-start.12 = (f32[1088,128]{1,0:T(8,128)S(1)}, f32[1088,128]{1,0:T(8,128)S(1)}, u32[]{:S(2)}, u32[]{:S(2)}) collective-permute-start(f32[1088,128]{1,0:T(8,128)S(1)} %bitcast.9), channel_id=1, source_target_pairs={{0,1},{1,0},{2,3},{3,2},{4,5},{5,4},{6,7},{7,6},{8,9},{9,8},{10,11... | collective-permute-start | bytes 1671176 | tf_op jit(solution)/shard_map/ppermute | solution.py:924
  121.2 2.8 %collective-permute-start.13 = (f32[2,112,128]{2,1,0:T(8,128)S(1)}, f32[2,112,128]{2,1,0:T(8,128)S(1)}, u32[]{:S(2)}, u32[]{:S(2)}) collective-permute-start(f32[2,112,128]{2,1,0:T(8,128)S(1)} %copy-done.19), channel_id=1, source_target_pairs={{0,496},{16,32},{32,16},{48,64},{64,48},{80,96},{96,80},{112,128},... | collective-permute-start | bytes 344072 | tf_op jit(solution)/shard_map/ppermute | solution.py:843
  124.1 2.1 %collective-permute-start.14 = (f32[2,112,128]{2,1,0:T(8,128)S(1)}, f32[2,112,128]{2,1,0:T(8,128)S(1)}, u32[]{:S(2)}, u32[]{:S(2)}) collective-permute-start(f32[2,112,128]{2,1,0:T(8,128)S(1)} %copy-done.17), channel_id=1, source_target_pairs={{0,16},{16,0},{32,48},{48,32},{64,80},{80,64},{96,112},{112,96},{1... | collective-permute-start | bytes 344072 | tf_op jit(solution)/shard_map/ppermute | solution.py:843
  126.2 6.1 %collective-permute-done.13.refs_4_ = f32[2,112,128]{2,1,0:T(8,128)S(1)} collective-permute-done((f32[2,112,128]{2,1,0:T(8,128)S(1)}, f32[2,112,128]{2,1,0:T(8,128)S(1)}, u32[]{:S(2)}, u32[]{:S(2)}) %collective-permute-start.13) | collective-permute-done | bytes 114720 | tf_op jit(solution)/shard_map/ppermute | solution.py:843
  132.3 6.6 %coarse_kernel.1 = (f32[2,64,128]{2,1,0:T(8,128)S(1)}, f32[2,64,128]{2,1,0:T(8,128)S(1)}, f32[2,64,128]{2,1,0:T(8,128)S(1)}, f32[2,64,128]{2,1,0:T(8,128)S(1)}, ...) custom-call(s32[2]{0:T(128)S(1)} %pad_add_fusion.refs_0_, f32[1088,128]{1,0:T(8,128)S(1)} %bitcast.10, ...), custom_call_target="tpu_custom_call" | custom-call | tf_op jit(solution)/shard_map/coarse_kernel/pallas_call | solution.py:828
  138.9 5.6 %collective-permute-start.15 = (f32[2,16,128]{2,1,0:T(8,128)S(1)}, f32[2,16,128]{2,1,0:T(8,128)S(1)}, u32[]{:S(2)}, u32[]{:S(2)}) collective-permute-start(f32[2,16,128]{2,1,0:T(8,128)S(1)} %get-tuple-element.96), channel_id=1, source_target_pairs={{0,496},{16,32},{32,16},{48,64},{64,48},{80,96},{96,80},{112,128},... | collective-permute-start | bytes 49160 | tf_op jit(solution)/shard_map/ppermute | solution.py:843
  144.5 1.9 %collective-permute-start.16 = (f32[2,16,128]{2,1,0:T(8,128)S(1)}, f32[2,16,128]{2,1,0:T(8,128)S(1)}, u32[]{:S(2)}, u32[]{:S(2)}) collective-permute-start(f32[2,16,128]{2,1,0:T(8,128)S(1)} %get-tuple-element.97), channel_id=1, source_target_pairs={{0,16},{16,0},{32,48},{48,32},{64,80},{80,64},{96,112},{112,96},{1... | collective-permute-start | bytes 49160 | tf_op jit(solution)/shard_map/ppermute | solution.py:843
  146.4 1.7 collective-permute-done.15.refs_5_
  148.2 2.0 %collective-permute-done.16.refs_6_ = f32[2,16,128]{2,1,0:T(8,128)S(1)} collective-permute-done((f32[2,16,128]{2,1,0:T(8,128)S(1)}, f32[2,16,128]{2,1,0:T(8,128)S(1)}, u32[]{:S(2)}, u32[]{:S(2)}) %collective-permute-start.16) | collective-permute-done | bytes 16416 | tf_op jit(solution)/shard_map/ppermute | solution.py:843
  150.1 1.6 sixth_kernel.1
  151.8 3.9 %collective-permute-start.17 = (f32[2,64,128]{2,1,0:T(8,128)S(1)}, f32[2,64,128]{2,1,0:T(8,128)S(1)}, u32[]{:S(2)}, u32[]{:S(2)}) collective-permute-start(f32[2,64,128]{2,1,0:T(8,128)S(1)} %get-tuple-element.101), channel_id=1, source_target_pairs={{0,496},{16,32},{32,16},{48,64},{64,48},{80,96},{96,80},{112,128},... | collective-permute-start | bytes 196616 | tf_op jit(solution)/shard_map/ppermute | solution.py:843
  155.7 1.9 %collective-permute-start.18 = (f32[2,64,128]{2,1,0:T(8,128)S(1)}, f32[2,64,128]{2,1,0:T(8,128)S(1)}, u32[]{:S(2)}, u32[]{:S(2)}) collective-permute-start(f32[2,64,128]{2,1,0:T(8,128)S(1)} %get-tuple-element.102), channel_id=1, source_target_pairs={{0,16},{16,0},{32,48},{48,32},{64,80},{80,64},{96,112},{112,96},{1... | collective-permute-start | bytes 196616 | tf_op jit(solution)/shard_map/ppermute | solution.py:843
  157.6 0.8 inner_kernel.3.refs_3_
  158.4 3.1 %collective-permute-done.17.refs_4_ = f32[2,64,128]{2,1,0:T(8,128)S(1)} collective-permute-done((f32[2,64,128]{2,1,0:T(8,128)S(1)}, f32[2,64,128]{2,1,0:T(8,128)S(1)}, u32[]{:S(2)}, u32[]{:S(2)}) %collective-permute-start.17) | collective-permute-done | bytes 65568 | tf_op jit(solution)/shard_map/ppermute | solution.py:843
  161.8 1.7 seventh_kernel.1
  163.5 5.6 %collective-permute-start.19 = (f32[64,128]{1,0:T(8,128)S(1)}, f32[64,128]{1,0:T(8,128)S(1)}, u32[]{:S(2)}, u32[]{:S(2)}) collective-permute-start(f32[64,128]{1,0:T(8,128)S(1)} %get-tuple-element.107), channel_id=1, source_target_pairs={{0,496},{16,32},{32,16},{48,64},{64,48},{80,96},{96,80},{112,128},... | collective-permute-start | bytes 98312 | tf_op jit(solution)/shard_map/ppermute | solution.py:843
  169.1 1.9 %collective-permute-start.20 = (f32[64,128]{1,0:T(8,128)S(1)}, f32[64,128]{1,0:T(8,128)S(1)}, u32[]{:S(2)}, u32[]{:S(2)}) collective-permute-start(f32[64,128]{1,0:T(8,128)S(1)} %get-tuple-element.108), channel_id=1, source_target_pairs={{0,16},{16,0},{32,48},{48,32},{64,80},{80,64},{96,112},{112,96},{1... | collective-permute-start | bytes 98312 | tf_op jit(solution)/shard_map/ppermute | solution.py:843
  171.0 0.9 inner_last_kernel.1.refs_8_
  171.9 1.0 collective-permute-done.19.refs_5_
  172.9 2.0 %collective-permute-done.20.refs_6_ = f32[64,128]{1,0:T(8,128)S(1)} collective-permute-done((f32[64,128]{1,0:T(8,128)S(1)}, f32[64,128]{1,0:T(8,128)S(1)}, u32[]{:S(2)}, u32[]{:S(2)}) %collective-permute-start.20) | collective-permute-done | bytes 32800 | tf_op jit(solution)/shard_map/ppermute | solution.py:843
  174.9 1.4 last_kernel.1
  (41 shorter events, 2.7 us)
Async XLA Ops:
  0.1 1.1 copy-start.7
  1.2 0.9 copy-start.10
  2.2 0.7 copy-start.15
  4.0 16.1 %collective-permute-start = (f32[1024,128]{1,0:T(8,128)S(1)}, f32[1024,128]{1,0:T(8,128)S(1)}, u32[]{:S(2)}, u32[]{:S(2)}) collective-permute-start(f32[1024,128]{1,0:T(8,128)S(1)} %get-tuple-element.59), channel_id=1, source_target_pairs={{0,15},{1,2},{2,1},{3,4},{4,3},{5,6},{6,5},{7,8},{8,7},{9,10},{10,... | collective-permute-start | bytes 1572872 | tf_op jit(solution)/shard_map/ppermute | solution.py:843
  6.0 14.2 %collective-permute-start.1 = (f32[1024,128]{1,0:T(8,128)S(1)}, f32[1024,128]{1,0:T(8,128)S(1)}, u32[]{:S(2)}, u32[]{:S(2)}) collective-permute-start(f32[1024,128]{1,0:T(8,128)S(1)} %get-tuple-element.60), channel_id=1, source_target_pairs={{0,1},{1,0},{2,3},{3,2},{4,5},{5,4},{6,7},{7,6},{8,9},{9,8},{10,11... | collective-permute-start | bytes 1572872 | tf_op jit(solution)/shard_map/ppermute | solution.py:843
  9.4 1.3 copy-start
  10.7 9.5 %copy-start.1 = (f32[2448,128]{1,0:T(8,128)S(1)}, f32[2448,128]{1,0:T(8,128)}, u32[]{:S(2)}) copy-start(f32[2448,128]{1,0:T(8,128)} %constant.11.clone.refs_1_.refs_6_.refs_3_.refs_9_.refs_7_.refs_8_.refs_10_) | copy-start | bytes 3760132
  21.9 16.1 %collective-permute-start.2 = (f32[2,128,128]{2,1,0:T(8,128)S(1)}, f32[2,128,128]{2,1,0:T(8,128)S(1)}, u32[]{:S(2)}, u32[]{:S(2)}) collective-permute-start(f32[2,128,128]{2,1,0:T(8,128)S(1)} %get-tuple-element.63), channel_id=1, source_target_pairs={{0,496},{16,32},{32,16},{48,64},{64,48},{80,96},{96,80},{112,128},... | collective-permute-start | bytes 393224 | tf_op jit(solution)/shard_map/ppermute | solution.py:843
  35.1 6.9 %collective-permute-start.3 = (f32[2,128,128]{2,1,0:T(8,128)S(1)}, f32[2,128,128]{2,1,0:T(8,128)S(1)}, u32[]{:S(2)}, u32[]{:S(2)}) collective-permute-start(f32[2,128,128]{2,1,0:T(8,128)S(1)} %get-tuple-element.64), channel_id=1, source_target_pairs={{0,16},{16,0},{32,48},{48,32},{64,80},{80,64},{96,112},{112,96},{1... | collective-permute-start | bytes 393224 | tf_op jit(solution)/shard_map/ppermute | solution.py:843
  43.5 9.8 %collective-permute-start.4 = (f32[2,64,128]{2,1,0:T(8,128)S(1)}, f32[2,64,128]{2,1,0:T(8,128)S(1)}, u32[]{:S(2)}, u32[]{:S(2)}) collective-permute-start(f32[2,64,128]{2,1,0:T(8,128)S(1)} %get-tuple-element.70), channel_id=1, source_target_pairs={{0,496},{16,32},{32,16},{48,64},{64,48},{80,96},{96,80},{112,128},... | collective-permute-start | bytes 196616 | tf_op jit(solution)/shard_map/ppermute | solution.py:843
  47.1 6.2 %collective-permute-start.5 = (f32[2,64,128]{2,1,0:T(8,128)S(1)}, f32[2,64,128]{2,1,0:T(8,128)S(1)}, u32[]{:S(2)}, u32[]{:S(2)}) collective-permute-start(f32[2,64,128]{2,1,0:T(8,128)S(1)} %get-tuple-element.71), channel_id=1, source_target_pairs={{0,16},{16,0},{32,48},{48,32},{64,80},{80,64},{96,112},{112,96},{1... | collective-permute-start | bytes 196616 | tf_op jit(solution)/shard_map/ppermute | solution.py:843
  55.6 23.6 %copy-start.2 = (f32[2,1536,128]{2,1,0:T(8,128)}, f32[2,1536,128]{2,1,0:T(8,128)S(1)}, u32[]{:S(2)}) copy-start(f32[2,1536,128]{2,1,0:T(8,128)S(1)} %get-tuple-element.74.refs_8_.refs_1_) | copy-start | bytes 4718596
  55.6 9.5 %collective-permute-start.6 = (f32[2,40,128]{2,1,0:T(8,128)S(1)}, f32[2,40,128]{2,1,0:T(8,128)S(1)}, u32[]{:S(2)}, u32[]{:S(2)}) collective-permute-start(f32[2,40,128]{2,1,0:T(8,128)S(1)} %get-tuple-element.77), channel_id=1, source_target_pairs={{0,496},{16,32},{32,16},{48,64},{64,48},{80,96},{96,80},{112,128},... | collective-permute-start | bytes 122888 | tf_op jit(solution)/shard_map/ppermute | solution.py:843
  61.4 5.9 %collective-permute-start.7 = (f32[2,40,128]{2,1,0:T(8,128)S(1)}, f32[2,40,128]{2,1,0:T(8,128)S(1)}, u32[]{:S(2)}, u32[]{:S(2)}) collective-permute-start(f32[2,40,128]{2,1,0:T(8,128)S(1)} %get-tuple-element.78), channel_id=1, source_target_pairs={{0,16},{16,0},{32,48},{48,32},{64,80},{80,64},{96,112},{112,96},{1... | collective-permute-start | bytes 122888 | tf_op jit(solution)/shard_map/ppermute | solution.py:843
  68.5 11.9 %copy-start.8 = (f32[2,64,128]{2,1,0:T(8,128)}, f32[2,64,128]{2,1,0:T(8,128)S(1)}, u32[]{:S(2)}) copy-start(f32[2,64,128]{2,1,0:T(8,128)S(1)} %get-tuple-element.82.refs_3_.refs_7_) | copy-start | bytes 196612
  68.5 9.2 %collective-permute-start.8 = (f32[2,16,128]{2,1,0:T(8,128)S(1)}, f32[2,16,128]{2,1,0:T(8,128)S(1)}, u32[]{:S(2)}, u32[]{:S(2)}) collective-permute-start(f32[2,16,128]{2,1,0:T(8,128)S(1)} %get-tuple-element.84), channel_id=1, source_target_pairs={{0,496},{16,32},{32,16},{48,64},{64,48},{80,96},{96,80},{112,128},... | collective-permute-start | bytes 49160 | tf_op jit(solution)/shard_map/ppermute | solution.py:843
  72.1 5.6 %collective-permute-start.9 = (f32[2,16,128]{2,1,0:T(8,128)S(1)}, f32[2,16,128]{2,1,0:T(8,128)S(1)}, u32[]{:S(2)}, u32[]{:S(2)}) collective-permute-start(f32[2,16,128]{2,1,0:T(8,128)S(1)} %get-tuple-element.85), channel_id=1, source_target_pairs={{0,16},{16,0},{32,48},{48,32},{64,80},{80,64},{96,112},{112,96},{1... | collective-permute-start | bytes 49160 | tf_op jit(solution)/shard_map/ppermute | solution.py:843
  79.1 0.6 copy-start.11
  79.8 0.6 copy-start.13
  81.1 22.8 %all-to-all-start = ((f32[32,8,128]{2,1,0:T(8,128)}), f32[32,8,128]{2,1,0:T(8,128)}, u32[]{:S(2)}, u32[]{:S(2)}) async-start(f32[32,8,128]{2,1,0:T(8,128)} %broadcast_in_dim.4), calls=%async_computation | async-start | bytes 262144 | tf_op jit(solution)/shard_map/all_to_all | solution.py:849
  86.8 6.3 %collective-permute-start.10 = (f32[192,128]{1,0:T(8,128)}, f32[192,128]{1,0:T(8,128)S(1)}, u32[]{:S(2)}, u32[]{:S(2)}) collective-permute-start(f32[192,128]{1,0:T(8,128)} %copy-done.11), channel_id=1, source_target_pairs={{0,15},{1,2},{2,1},{3,4},{4,3},{5,6},{6,5},{7,8},{8,7},{9,10},{10,... | collective-permute-start | bytes 294920 | tf_op jit(solution)/shard_map/ppermute | solution.py:843
  88.7 4.4 %collective-permute-start.11 = (f32[192,128]{1,0:T(8,128)}, f32[192,128]{1,0:T(8,128)S(1)}, u32[]{:S(2)}, u32[]{:S(2)}) collective-permute-start(f32[192,128]{1,0:T(8,128)} %copy-done.13), channel_id=1, source_target_pairs={{0,1},{1,0},{2,3},{3,2},{4,5},{5,4},{6,7},{7,6},{8,9},{9,8},{10,11... | collective-permute-start | bytes 294920 | tf_op jit(solution)/shard_map/ppermute | solution.py:843
  93.1 0.9 copy-start.12
  94.0 0.9 copy-start.14
  95.9 0.7 copy-start.4
  96.6 0.6 copy-start.16
  97.3 0.6 copy-start.18
  103.8 0.9 copy-start.5
  104.8 16.5 %copy-start.19 = (f32[2,112,128]{2,1,0:T(8,128)S(1)}, f32[2,112,128]{2,1,0:T(8,128)}, u32[]{:S(2)}) copy-start(f32[2,112,128]{2,1,0:T(8,128)} %copy-done.18) | copy-start | bytes 344068
  104.8 19.3 %copy-start.17 = (f32[2,112,128]{2,1,0:T(8,128)S(1)}, f32[2,112,128]{2,1,0:T(8,128)}, u32[]{:S(2)}) copy-start(f32[2,112,128]{2,1,0:T(8,128)} %copy-done.16) | copy-start | bytes 344068
  104.8 27.5 %copy-start.6 = (f32[2,192,128]{2,1,0:T(8,128)S(1)}, f32[2,192,128]{2,1,0:T(8,128)}, u32[]{:S(2)}) copy-start(f32[2,192,128]{2,1,0:T(8,128)} %copy-done.4) | copy-start | bytes 589828
  104.8 27.5 %copy-start.9 = (f32[2,64,128]{2,1,0:T(8,128)S(1)}, f32[2,64,128]{2,1,0:T(8,128)}, u32[]{:S(2)}) copy-start(f32[2,64,128]{2,1,0:T(8,128)} %copy-done.8) | copy-start | bytes 196612
  119.2 31.0 %copy-start.3 = (f32[2,1536,128]{2,1,0:T(8,128)S(1)}, f32[2,1536,128]{2,1,0:T(8,128)}, u32[]{:S(2)}) copy-start(f32[2,1536,128]{2,1,0:T(8,128)} %copy-done.2) | copy-start | bytes 4718596
  119.2 13.1 %collective-permute-start.12 = (f32[1088,128]{1,0:T(8,128)S(1)}, f32[1088,128]{1,0:T(8,128)S(1)}, u32[]{:S(2)}, u32[]{:S(2)}) collective-permute-start(f32[1088,128]{1,0:T(8,128)S(1)} %bitcast.9), channel_id=1, source_target_pairs={{0,1},{1,0},{2,3},{3,2},{4,5},{5,4},{6,7},{7,6},{8,9},{9,8},{10,11... | collective-permute-start | bytes 1671176 | tf_op jit(solution)/shard_map/ppermute | solution.py:924
  121.2 11.1 %collective-permute-start.13 = (f32[2,112,128]{2,1,0:T(8,128)S(1)}, f32[2,112,128]{2,1,0:T(8,128)S(1)}, u32[]{:S(2)}, u32[]{:S(2)}) collective-permute-start(f32[2,112,128]{2,1,0:T(8,128)S(1)} %copy-done.19), channel_id=1, source_target_pairs={{0,496},{16,32},{32,16},{48,64},{64,48},{80,96},{96,80},{112,128},... | collective-permute-start | bytes 344072 | tf_op jit(solution)/shard_map/ppermute | solution.py:843
  124.1 8.2 %collective-permute-start.14 = (f32[2,112,128]{2,1,0:T(8,128)S(1)}, f32[2,112,128]{2,1,0:T(8,128)S(1)}, u32[]{:S(2)}, u32[]{:S(2)}) collective-permute-start(f32[2,112,128]{2,1,0:T(8,128)S(1)} %copy-done.17), channel_id=1, source_target_pairs={{0,16},{16,0},{32,48},{48,32},{64,80},{80,64},{96,112},{112,96},{1... | collective-permute-start | bytes 344072 | tf_op jit(solution)/shard_map/ppermute | solution.py:843
  138.9 9.2 %collective-permute-start.15 = (f32[2,16,128]{2,1,0:T(8,128)S(1)}, f32[2,16,128]{2,1,0:T(8,128)S(1)}, u32[]{:S(2)}, u32[]{:S(2)}) collective-permute-start(f32[2,16,128]{2,1,0:T(8,128)S(1)} %get-tuple-element.96), channel_id=1, source_target_pairs={{0,496},{16,32},{32,16},{48,64},{64,48},{80,96},{96,80},{112,128},... | collective-permute-start | bytes 49160 | tf_op jit(solution)/shard_map/ppermute | solution.py:843
  144.5 5.6 %collective-permute-start.16 = (f32[2,16,128]{2,1,0:T(8,128)S(1)}, f32[2,16,128]{2,1,0:T(8,128)S(1)}, u32[]{:S(2)}, u32[]{:S(2)}) collective-permute-start(f32[2,16,128]{2,1,0:T(8,128)S(1)} %get-tuple-element.97), channel_id=1, source_target_pairs={{0,16},{16,0},{32,48},{48,32},{64,80},{80,64},{96,112},{112,96},{1... | collective-permute-start | bytes 49160 | tf_op jit(solution)/shard_map/ppermute | solution.py:843
  151.8 9.8 %collective-permute-start.17 = (f32[2,64,128]{2,1,0:T(8,128)S(1)}, f32[2,64,128]{2,1,0:T(8,128)S(1)}, u32[]{:S(2)}, u32[]{:S(2)}) collective-permute-start(f32[2,64,128]{2,1,0:T(8,128)S(1)} %get-tuple-element.101), channel_id=1, source_target_pairs={{0,496},{16,32},{32,16},{48,64},{64,48},{80,96},{96,80},{112,128},... | collective-permute-start | bytes 196616 | tf_op jit(solution)/shard_map/ppermute | solution.py:843
  155.7 6.2 %collective-permute-start.18 = (f32[2,64,128]{2,1,0:T(8,128)S(1)}, f32[2,64,128]{2,1,0:T(8,128)S(1)}, u32[]{:S(2)}, u32[]{:S(2)}) collective-permute-start(f32[2,64,128]{2,1,0:T(8,128)S(1)} %get-tuple-element.102), channel_id=1, source_target_pairs={{0,16},{16,0},{32,48},{48,32},{64,80},{80,64},{96,112},{112,96},{1... | collective-permute-start | bytes 196616 | tf_op jit(solution)/shard_map/ppermute | solution.py:843
  163.5 9.4 %collective-permute-start.19 = (f32[64,128]{1,0:T(8,128)S(1)}, f32[64,128]{1,0:T(8,128)S(1)}, u32[]{:S(2)}, u32[]{:S(2)}) collective-permute-start(f32[64,128]{1,0:T(8,128)S(1)} %get-tuple-element.107), channel_id=1, source_target_pairs={{0,496},{16,32},{32,16},{48,64},{64,48},{80,96},{96,80},{112,128},... | collective-permute-start | bytes 98312 | tf_op jit(solution)/shard_map/ppermute | solution.py:843
  169.1 5.8 %collective-permute-start.20 = (f32[64,128]{1,0:T(8,128)S(1)}, f32[64,128]{1,0:T(8,128)S(1)}, u32[]{:S(2)}, u32[]{:S(2)}) collective-permute-start(f32[64,128]{1,0:T(8,128)S(1)} %get-tuple-element.108), channel_id=1, source_target_pairs={{0,16},{16,0},{32,48},{48,32},{64,80},{80,64},{96,112},{112,96},{1... | collective-permute-start | bytes 98312 | tf_op jit(solution)/shard_map/ppermute | solution.py:843

commit v2 on v1

--- a/solution.py
+++ b/solution.py
@@ -114,13 +114,20 @@
 C_W4 = lanes_of(cube(W4) / np.exp(kron3(TO4, TO4, TO4) @ np.log(cube(W8))))
 C_W2 = lanes_of(cube(W2) / np.exp(kron3(TO2, TO2, TO2) @ np.log(cube(W8))))
 C_M4 = lanes_of(share(4))
-FIRST = np.r_[0:64, 64:80, 128:144]
-LAST = np.r_[0:64, 112:128, 176:192]
+FIRST = np.r_[0:16, 64:80, 128:144]
+LAST = np.r_[48:64, 112:128, 176:192]
+
+
+def plane_back(plane, rows):
+    eye = np.eye(16, dtype=np.float32)
+    return np.concatenate([eye, C_G4T[plane : plane + 16, rows[16:]]], axis=1)
+
+
 CONSTANTS = {
     "bd": C_BD, "bdt": C_BDT, "bsq": C_BSQ, "sample": C_SAMPLE, "w4": C_W4, "w2": C_W2,
     "sq4": C_SQ4, "gm": C_G4, "gmt": C_G4T, "m4": C_M4, "down8": C_DOWN8, "down4": C_DOWN4,
-    "up4": C_UP4X3, "up8": C_UP8, "gm_first": C_G4[FIRST], "gmt_first": C_G4T[:16, FIRST],
-    "gm_last": C_G4[LAST], "gmt_last": C_G4T[48:, LAST],
+    "up4": C_UP4X3, "up8": C_UP8, "gm_first": C_G4[FIRST], "gmt_first": plane_back(0, FIRST),
+    "gm_last": C_G4[LAST], "gmt_last": plane_back(48, LAST),
 }
 
 
@@ -595,12 +602,19 @@
     put(back, 0, 64, dot(gmt[...], flux))
     one = pl.multiple_of(jnp.where(even, 48, 0), 8)
     two = pl.multiple_of(jnp.where(even, 0, 48), 8)
-    for out, plane in ((near_side, one), (far, two)):
+    sums = [
+        [
+            total([g4[h, 16 * k : 16 * k + 16] * float(D4[k, end]) for k in range(4)])
+            for end in (0, 3)
+        ]
+        for h in range(2)
+    ]
+    for out, plane, is_last in ((near_side, one, even), (far, two, jnp.logical_not(even))):
         for h in range(2):
-            out[h, 0:64] = g4[h, 0:64]
-            out[h, 64:80] = g4[h, pl.ds(64 + plane, 16), :]
-            out[h, 80:96] = g4[h, pl.ds(128 + plane, 16), :]
-            out[h, 96:112] = back[h, pl.ds(plane, 16), :]
+            out[h, 0:16] = jnp.where(is_last, sums[h][1], sums[h][0])
+            out[h, 16:32] = g4[h, pl.ds(64 + plane, 16), :]
+            out[h, 32:48] = g4[h, pl.ds(128 + plane, 16), :]
+            out[h, 48:64] = back[h, pl.ds(plane, 16), :]
 
 
 def column_kernel(rows, first, out):
@@ -723,10 +737,10 @@
     ext = jnp.concatenate([jnp.where(near, b[0], b[1]), jnp.where(near, b[1], b[2])], axis=1)
     rise = dot(up4[...], ext)
     even = is_even(pos, 0)
-    x, y = wide(far, 0, 112), wide(near_side, 0, 112)
+    x, y = wide(far, 0, 64), wide(near_side, 0, 64)
     below, above = jnp.where(even, x, y), jnp.where(even, y, x)
-    low = dot(gmt_last[...], dot(gm_last[...], rise[:64]) * below[:96]) + below[96:]
-    high = dot(gmt_first[...], dot(gm_first[...], rise[128:]) * above[:96]) + above[96:]
+    low = dot(gmt_last[...], dot(gm_last[...], rise[:64]) * below[:48]) + below[48:]
+    high = dot(gmt_first[...], dot(gm_first[...], rise[128:]) * above[:48]) + above[48:]
     flux = dot(gm[...], rise[64:128] + wide(wider, 64, 64)) * wide(g4, 0, 192)
     back = dot(gmt[...], flux)
     put(acc, 0, 16, back[:16] + low)
@@ -911,7 +925,7 @@
     wider, a, b = call(
         side_kernel,
         (pos, *kept4, a, b, g4, "gm", "gmt"),
-        [(2, 192, LANES)] + [(2, 112, LANES)] * 2,
+        [(2, 192, LANES)] + face8,
         [mid],
     )
     sides = exchange(a, b, "stream")

time: 177 us -> 176 us (level)
  no operation moved by 1% of the time
where the time goes in v2:
time: 176 us; the launch traced here: 175 us
  starting transfers between devices  76.5 us (43%)
  waiting for transfers between devices  47.4 us (27%)
  Pallas kernels  26.9 us (15%)
  blocking collectives  13.2 us (8%)
  local copies, waits for them, and re-layouts  10.6 us (6%)
    ppermute x10, starting transfers between devices, exchange(): lax.ppermute(far, axis, pairs_far)  47.9 us
    ppermute x10, waiting for transfers between devices, exchange(): lax.ppermute(far, axis, pairs_far)  30.9 us
    pallas_call x17, Pallas kernels, call(): pl.pallas_call(body, out_shape=[jax.ShapeDtypeStruct(s, F32) for s in out...  26.9 us
    ppermute x10, starting transfers between devices, exchange(): lax.ppermute(near, axis, pairs_near)  20.9 us
    all_to_all x1, blocking collectives, spread(): lax.all_to_all(copies, axis, 0, 0, axis_index_groups=groups)  13.2 us
    ppermute x10, waiting for transfers between devices, exchange(): lax.ppermute(near, axis, pairs_near)  10.4 us
    unnamed x40, local copies, waits for them, and re-layouts  9.95 us
    all_to_all x1, waiting for transfers between devices, spread(): lax.all_to_all(copies, axis, 0, 0, axis_index_groups=groups)  5.98 us
  transfers between devices with their start and end apart: 22, of which 16 were waited for; matrix products, arithmetic and copies ran while one was open for 0% of the time, Pallas kernels for 3%

profile of v2, /device:TPU:8, one launch (start us, length us, event | category | flops | bytes accessed | tf_op | source)
XLA Modules:
  0.0 175.1 jit_solution(9875782885095251619)
XLA Ops:
  0.1 1.1 copy-done.7
  1.2 0.9 copy-done.10
  2.2 0.7 copy-done.15
  2.8 1.2 order_kernel.1
  4.0 1.9 %collective-permute-start = (f32[1024,128]{1,0:T(8,128)S(1)}, f32[1024,128]{1,0:T(8,128)S(1)}, u32[]{:S(2)}, u32[]{:S(2)}) collective-permute-start(f32[1024,128]{1,0:T(8,128)S(1)} %get-tuple-element.59), channel_id=1, source_target_pairs={{0,15},{1,2},{2,1},{3,4},{4,3},{5,6},{6,5},{7,8},{8,7},{9,10},{10,... | collective-permute-start | bytes 1572872 | tf_op jit(solution)/shard_map/ppermute | solution.py:857
  6.0 3.4 %collective-permute-start.1 = (f32[1024,128]{1,0:T(8,128)S(1)}, f32[1024,128]{1,0:T(8,128)S(1)}, u32[]{:S(2)}, u32[]{:S(2)}) collective-permute-start(f32[1024,128]{1,0:T(8,128)S(1)} %get-tuple-element.60), channel_id=1, source_target_pairs={{0,1},{1,0},{2,3},{3,2},{4,5},{5,4},{6,7},{7,6},{8,9},{9,8},{10,11... | collective-permute-start | bytes 1572872 | tf_op jit(solution)/shard_map/ppermute | solution.py:857
  9.4 1.3 copy-done
  11.0 9.2 %collective-permute-done.refs_4_ = f32[1024,128]{1,0:T(8,128)S(1)} collective-permute-done((f32[1024,128]{1,0:T(8,128)S(1)}, f32[1024,128]{1,0:T(8,128)S(1)}, u32[]{:S(2)}, u32[]{:S(2)}) %collective-permute-start) | collective-permute-done | bytes 524320 | tf_op jit(solution)/shard_map/ppermute | solution.py:857
  20.2 1.8 %setup_kernel.1 = (f32[2,1536,128]{2,1,0:T(8,128)S(1)}, f32[2,512,128]{2,1,0:T(8,128)S(1)}, f32[2,512,128]{2,1,0:T(8,128)S(1)}, f32[2,128,128]{2,1,0:T(8,128)S(1)}, f32[2,128,128]{2,1,0:T(8,128)S(1)}) custom-call(s32[2]{0:T(128)S(1)} %pad_add_fusion.refs_0_, f32[1536,128]{1,0:T(8,128)S(1)} %get-tuple-element.57.refs_0_.refs_1_, ...), custom_call_target="tpu_custom_call" | custom-call | tf_op jit(solution)/shard_map/setup_kernel/pallas_call | solution.py:842
  21.9 13.1 %collective-permute-start.2 = (f32[2,128,128]{2,1,0:T(8,128)S(1)}, f32[2,128,128]{2,1,0:T(8,128)S(1)}, u32[]{:S(2)}, u32[]{:S(2)}) collective-permute-start(f32[2,128,128]{2,1,0:T(8,128)S(1)} %get-tuple-element.63), channel_id=1, source_target_pairs={{0,496},{16,32},{32,16},{48,64},{64,48},{80,96},{96,80},{112,128},... | collective-permute-start | bytes 393224 | tf_op jit(solution)/shard_map/ppermute | solution.py:857
  35.1 1.9 %collective-permute-start.3 = (f32[2,128,128]{2,1,0:T(8,128)S(1)}, f32[2,128,128]{2,1,0:T(8,128)S(1)}, u32[]{:S(2)}, u32[]{:S(2)}) collective-permute-start(f32[2,128,128]{2,1,0:T(8,128)S(1)} %get-tuple-element.64), channel_id=1, source_target_pairs={{0,16},{16,0},{32,48},{48,32},{64,80},{80,64},{96,112},{112,96},{1... | collective-permute-start | bytes 393224 | tf_op jit(solution)/shard_map/ppermute | solution.py:857
  37.0 1.0 collective-permute-done.2.refs_3_
  38.0 3.9 %collective-permute-done.3.refs_4_ = f32[2,128,128]{2,1,0:T(8,128)S(1)} collective-permute-done((f32[2,128,128]{2,1,0:T(8,128)S(1)}, f32[2,128,128]{2,1,0:T(8,128)S(1)}, u32[]{:S(2)}, u32[]{:S(2)}) %collective-permute-start.3) | collective-permute-done | bytes 131104 | tf_op jit(solution)/shard_map/ppermute | solution.py:857
  41.9 1.6 first_kernel.1
  43.5 3.6 %collective-permute-start.4 = (f32[2,64,128]{2,1,0:T(8,128)S(1)}, f32[2,64,128]{2,1,0:T(8,128)S(1)}, u32[]{:S(2)}, u32[]{:S(2)}) collective-permute-start(f32[2,64,128]{2,1,0:T(8,128)S(1)} %get-tuple-element.70), channel_id=1, source_target_pairs={{0,496},{16,32},{32,16},{48,64},{64,48},{80,96},{96,80},{112,128},... | collective-permute-start | bytes 196616 | tf_op jit(solution)/shard_map/ppermute | solution.py:857
  47.1 1.9 %collective-permute-start.5 = (f32[2,64,128]{2,1,0:T(8,128)S(1)}, f32[2,64,128]{2,1,0:T(8,128)S(1)}, u32[]{:S(2)}, u32[]{:S(2)}) collective-permute-start(f32[2,64,128]{2,1,0:T(8,128)S(1)} %get-tuple-element.71), channel_id=1, source_target_pairs={{0,16},{16,0},{32,48},{48,32},{64,80},{80,64},{96,112},{112,96},{1... | collective-permute-start | bytes 196616 | tf_op jit(solution)/shard_map/ppermute | solution.py:857
  49.1 1.4 coarsen_kernel.1
  50.5 0.8 inner_kernel.2.refs_3_
  51.3 2.0 %collective-permute-done.4.refs_4_ = f32[2,64,128]{2,1,0:T(8,128)S(1)} collective-permute-done((f32[2,64,128]{2,1,0:T(8,128)S(1)}, f32[2,64,128]{2,1,0:T(8,128)S(1)}, u32[]{:S(2)}, u32[]{:S(2)}) %collective-permute-start.4) | collective-permute-done | bytes 65568 | tf_op jit(solution)/shard_map/ppermute | solution.py:857
  53.3 2.2 %second_kernel.1 = (f32[2,1536,128]{2,1,0:T(8,128)S(1)}, f32[2,64,128]{2,1,0:T(8,128)S(1)}, f32[2,40,128]{2,1,0:T(8,128)S(1)}, f32[2,40,128]{2,1,0:T(8,128)S(1)}) custom-call(s32[2]{0:T(128)S(1)} %pad_add_fusion.refs_0_, f32[2,512,128]{2,1,0:T(8,128)S(1)} %get-tuple-element.66.refs_1_, f32[2,512,128]{2,1,0:T(8,128)S(1)} %get-tuple-element.67.refs_2_.refs_6_.refs_5_.refs_7_, ...), custom_call_target="tpu_custom_call" | custom-call | tf_op jit(solution)/shard_map/second_kernel/pallas_call | solution.py:842
  55.6 5.8 %collective-permute-start.6 = (f32[2,40,128]{2,1,0:T(8,128)S(1)}, f32[2,40,128]{2,1,0:T(8,128)S(1)}, u32[]{:S(2)}, u32[]{:S(2)}) collective-permute-start(f32[2,40,128]{2,1,0:T(8,128)S(1)} %get-tuple-element.77), channel_id=1, source_target_pairs={{0,496},{16,32},{32,16},{48,64},{64,48},{80,96},{96,80},{112,128},... | collective-permute-start | bytes 122888 | tf_op jit(solution)/shard_map/ppermute | solution.py:857
  61.4 1.9 %collective-permute-start.7 = (f32[2,40,128]{2,1,0:T(8,128)S(1)}, f32[2,40,128]{2,1,0:T(8,128)S(1)}, u32[]{:S(2)}, u32[]{:S(2)}) collective-permute-start(f32[2,40,128]{2,1,0:T(8,128)S(1)} %get-tuple-element.78), channel_id=1, source_target_pairs={{0,16},{16,0},{32,48},{48,32},{64,80},{80,64},{96,112},{112,96},{1... | collective-permute-start | bytes 122888 | tf_op jit(solution)/shard_map/ppermute | solution.py:857
  63.4 1.7 collective-permute-done.6.refs_4_
  65.1 2.2 %collective-permute-done.7.refs_5_ = f32[2,40,128]{2,1,0:T(8,128)S(1)} collective-permute-done((f32[2,40,128]{2,1,0:T(8,128)S(1)}, f32[2,40,128]{2,1,0:T(8,128)S(1)}, u32[]{:S(2)}, u32[]{:S(2)}) %collective-permute-start.7) | collective-permute-done | bytes 40992 | tf_op jit(solution)/shard_map/ppermute | solution.py:857
  67.3 1.2 third_kernel.1
  68.5 3.6 %collective-permute-start.8 = (f32[2,16,128]{2,1,0:T(8,128)S(1)}, f32[2,16,128]{2,1,0:T(8,128)S(1)}, u32[]{:S(2)}, u32[]{:S(2)}) collective-permute-start(f32[2,16,128]{2,1,0:T(8,128)S(1)} %get-tuple-element.84), channel_id=1, source_target_pairs={{0,496},{16,32},{32,16},{48,64},{64,48},{80,96},{96,80},{112,128},... | collective-permute-start | bytes 49160 | tf_op jit(solution)/shard_map/ppermute | solution.py:857
  72.1 1.9 %collective-permute-start.9 = (f32[2,16,128]{2,1,0:T(8,128)S(1)}, f32[2,16,128]{2,1,0:T(8,128)S(1)}, u32[]{:S(2)}, u32[]{:S(2)}) collective-permute-start(f32[2,16,128]{2,1,0:T(8,128)S(1)} %get-tuple-element.85), channel_id=1, source_target_pairs={{0,16},{16,0},{32,48},{48,32},{64,80},{80,64},{96,112},{112,96},{1... | collective-permute-start | bytes 49160 | tf_op jit(solution)/shard_map/ppermute | solution.py:857
  74.1 3.7 %collective-permute-done.8.refs_5_ = f32[2,16,128]{2,1,0:T(8,128)S(1)} collective-permute-done((f32[2,16,128]{2,1,0:T(8,128)S(1)}, f32[2,16,128]{2,1,0:T(8,128)S(1)}, u32[]{:S(2)}, u32[]{:S(2)}) %collective-permute-start.8) | collective-permute-done | bytes 16416 | tf_op jit(solution)/shard_map/ppermute | solution.py:857
  77.8 1.3 fourth_kernel.1
  79.8 0.6 copy-done.13
  80.4 0.7 broadcast_in_dim.4
  81.1 5.7 %all-to-all-start = ((f32[32,8,128]{2,1,0:T(8,128)}), f32[32,8,128]{2,1,0:T(8,128)}, u32[]{:S(2)}, u32[]{:S(2)}) async-start(f32[32,8,128]{2,1,0:T(8,128)} %broadcast_in_dim.4), calls=%async_computation | async-start | bytes 262144 | tf_op jit(solution)/shard_map/all_to_all | solution.py:863
  86.8 1.9 %collective-permute-start.10 = (f32[192,128]{1,0:T(8,128)}, f32[192,128]{1,0:T(8,128)S(1)}, u32[]{:S(2)}, u32[]{:S(2)}) collective-permute-start(f32[192,128]{1,0:T(8,128)} %copy-done.11), channel_id=1, source_target_pairs={{0,15},{1,2},{2,1},{3,4},{4,3},{5,6},{6,5},{7,8},{8,7},{9,10},{10,... | collective-permute-start | bytes 294920 | tf_op jit(solution)/shard_map/ppermute | solution.py:857
  88.7 1.9 %collective-permute-start.11 = (f32[192,128]{1,0:T(8,128)}, f32[192,128]{1,0:T(8,128)S(1)}, u32[]{:S(2)}, u32[]{:S(2)}) collective-permute-start(f32[192,128]{1,0:T(8,128)} %copy-done.13), channel_id=1, source_target_pairs={{0,1},{1,0},{2,3},{3,2},{4,5},{5,4},{6,7},{7,6},{8,9},{9,8},{10,11... | collective-permute-start | bytes 294920 | tf_op jit(solution)/shard_map/ppermute | solution.py:857
  90.7 2.5 %collective-permute-done.10.refs_3_ = f32[192,128]{1,0:T(8,128)S(1)} collective-permute-done((f32[192,128]{1,0:T(8,128)}, f32[192,128]{1,0:T(8,128)S(1)}, u32[]{:S(2)}, u32[]{:S(2)}) %collective-permute-start.10) | collective-permute-done | bytes 98336 | tf_op jit(solution)/shard_map/ppermute | solution.py:857
  93.1 0.9 copy-done.12
  94.0 0.9 copy-done.14
  94.9 1.0 side_kernel.1
  96.0 0.7 copy-done.4
  97.9 6.0 %all-to-all-done = f32[32,8,128]{2,1,0:T(8,128)} async-done(((f32[32,8,128]{2,1,0:T(8,128)}), f32[32,8,128]{2,1,0:T(8,128)}, u32[]{:S(2)}, u32[]{:S(2)}) %all-to-all-start) | async-done | bytes 131104 | tf_op jit(solution)/shard_map/all_to_all | solution.py:863
  103.8 0.9 copy-done.5
  104.8 1.1 column_kernel.1
  105.9 13.2 %all_to_all.10 = f32[8,136,128]{2,1,0:T(8,128)S(1)} all-to-all(f32[8,136,128]{2,1,0:T(8,128)S(1)} %broadcast_in_dim.5), channel_id=1, replica_groups={{0,2,4,6,8,10,12,14},{1,3,5,7,9,11,13,15},{16,18,20,22,24,26,28,30},{17..., dimensions={0} | all-to-all | bytes 1114112 | tf_op jit(solution)/shard_map/all_to_all | solution.py:863
  119.2 2.0 %collective-permute-start.12 = (f32[1088,128]{1,0:T(8,128)S(1)}, f32[1088,128]{1,0:T(8,128)S(1)}, u32[]{:S(2)}, u32[]{:S(2)}) collective-permute-start(f32[1088,128]{1,0:T(8,128)S(1)} %bitcast.9), channel_id=1, source_target_pairs={{0,1},{1,0},{2,3},{3,2},{4,5},{5,4},{6,7},{7,6},{8,9},{9,8},{10,11... | collective-permute-start | bytes 1671176 | tf_op jit(solution)/shard_map/ppermute | solution.py:938
  121.2 2.8 %collective-permute-start.13 = (f32[2,64,128]{2,1,0:T(8,128)S(1)}, f32[2,64,128]{2,1,0:T(8,128)S(1)}, u32[]{:S(2)}, u32[]{:S(2)}) collective-permute-start(f32[2,64,128]{2,1,0:T(8,128)S(1)} %copy-done.19), channel_id=1, source_target_pairs={{0,496},{16,32},{32,16},{48,64},{64,48},{80,96},{96,80},{112,128},... | collective-permute-start | bytes 196616 | tf_op jit(solution)/shard_map/ppermute | solution.py:857
  124.0 2.1 %collective-permute-start.14 = (f32[2,64,128]{2,1,0:T(8,128)S(1)}, f32[2,64,128]{2,1,0:T(8,128)S(1)}, u32[]{:S(2)}, u32[]{:S(2)}) collective-permute-start(f32[2,64,128]{2,1,0:T(8,128)S(1)} %copy-done.17), channel_id=1, source_target_pairs={{0,16},{16,0},{32,48},{48,32},{64,80},{80,64},{96,112},{112,96},{1... | collective-permute-start | bytes 196616 | tf_op jit(solution)/shard_map/ppermute | solution.py:857
  126.1 5.1 %collective-permute-done.13.refs_4_ = f32[2,64,128]{2,1,0:T(8,128)S(1)} collective-permute-done((f32[2,64,128]{2,1,0:T(8,128)S(1)}, f32[2,64,128]{2,1,0:T(8,128)S(1)}, u32[]{:S(2)}, u32[]{:S(2)}) %collective-permute-start.13) | collective-permute-done | bytes 65568 | tf_op jit(solution)/shard_map/ppermute | solution.py:857
  131.3 6.5 %coarse_kernel.1 = (f32[2,64,128]{2,1,0:T(8,128)S(1)}, f32[2,64,128]{2,1,0:T(8,128)S(1)}, f32[2,64,128]{2,1,0:T(8,128)S(1)}, f32[2,64,128]{2,1,0:T(8,128)S(1)}, ...) custom-call(s32[2]{0:T(128)S(1)} %pad_add_fusion.refs_0_, f32[1088,128]{1,0:T(8,128)S(1)} %bitcast.10, ...), custom_call_target="tpu_custom_call" | custom-call | tf_op jit(solution)/shard_map/coarse_kernel/pallas_call | solution.py:842
  137.8 5.6 %collective-permute-start.15 = (f32[2,16,128]{2,1,0:T(8,128)S(1)}, f32[2,16,128]{2,1,0:T(8,128)S(1)}, u32[]{:S(2)}, u32[]{:S(2)}) collective-permute-start(f32[2,16,128]{2,1,0:T(8,128)S(1)} %get-tuple-element.96), channel_id=1, source_target_pairs={{0,496},{16,32},{32,16},{48,64},{64,48},{80,96},{96,80},{112,128},... | collective-permute-start | bytes 49160 | tf_op jit(solution)/shard_map/ppermute | solution.py:857
  143.4 1.9 %collective-permute-start.16 = (f32[2,16,128]{2,1,0:T(8,128)S(1)}, f32[2,16,128]{2,1,0:T(8,128)S(1)}, u32[]{:S(2)}, u32[]{:S(2)}) collective-permute-start(f32[2,16,128]{2,1,0:T(8,128)S(1)} %get-tuple-element.97), channel_id=1, source_target_pairs={{0,16},{16,0},{32,48},{48,32},{64,80},{80,64},{96,112},{112,96},{1... | collective-permute-start | bytes 49160 | tf_op jit(solution)/shard_map/ppermute | solution.py:857
  145.3 1.7 collective-permute-done.15.refs_5_
  147.0 2.0 %collective-permute-done.16.refs_6_ = f32[2,16,128]{2,1,0:T(8,128)S(1)} collective-permute-done((f32[2,16,128]{2,1,0:T(8,128)S(1)}, f32[2,16,128]{2,1,0:T(8,128)S(1)}, u32[]{:S(2)}, u32[]{:S(2)}) %collective-permute-start.16) | collective-permute-done | bytes 16416 | tf_op jit(solution)/shard_map/ppermute | solution.py:857
  149.0 1.6 sixth_kernel.1
  150.7 3.8 %collective-permute-start.17 = (f32[2,64,128]{2,1,0:T(8,128)S(1)}, f32[2,64,128]{2,1,0:T(8,128)S(1)}, u32[]{:S(2)}, u32[]{:S(2)}) collective-permute-start(f32[2,64,128]{2,1,0:T(8,128)S(1)} %get-tuple-element.101), channel_id=1, source_target_pairs={{0,496},{16,32},{32,16},{48,64},{64,48},{80,96},{96,80},{112,128},... | collective-permute-start | bytes 196616 | tf_op jit(solution)/shard_map/ppermute | solution.py:857
  154.5 1.9 %collective-permute-start.18 = (f32[2,64,128]{2,1,0:T(8,128)S(1)}, f32[2,64,128]{2,1,0:T(8,128)S(1)}, u32[]{:S(2)}, u32[]{:S(2)}) collective-permute-start(f32[2,64,128]{2,1,0:T(8,128)S(1)} %get-tuple-element.102), channel_id=1, source_target_pairs={{0,16},{16,0},{32,48},{48,32},{64,80},{80,64},{96,112},{112,96},{1... | collective-permute-start | bytes 196616 | tf_op jit(solution)/shard_map/ppermute | solution.py:857
  156.4 0.8 inner_kernel.3.refs_3_
  157.3 3.2 %collective-permute-done.17.refs_4_ = f32[2,64,128]{2,1,0:T(8,128)S(1)} collective-permute-done((f32[2,64,128]{2,1,0:T(8,128)S(1)}, f32[2,64,128]{2,1,0:T(8,128)S(1)}, u32[]{:S(2)}, u32[]{:S(2)}) %collective-permute-start.17) | collective-permute-done | bytes 65568 | tf_op jit(solution)/shard_map/ppermute | solution.py:857
  160.7 1.7 seventh_kernel.1
  162.3 5.6 %collective-permute-start.19 = (f32[64,128]{1,0:T(8,128)S(1)}, f32[64,128]{1,0:T(8,128)S(1)}, u32[]{:S(2)}, u32[]{:S(2)}) collective-permute-start(f32[64,128]{1,0:T(8,128)S(1)} %get-tuple-element.107), channel_id=1, source_target_pairs={{0,496},{16,32},{32,16},{48,64},{64,48},{80,96},{96,80},{112,128},... | collective-permute-start | bytes 98312 | tf_op jit(solution)/shard_map/ppermute | solution.py:857
  168.0 1.9 %collective-permute-start.20 = (f32[64,128]{1,0:T(8,128)S(1)}, f32[64,128]{1,0:T(8,128)S(1)}, u32[]{:S(2)}, u32[]{:S(2)}) collective-permute-start(f32[64,128]{1,0:T(8,128)S(1)} %get-tuple-element.108), channel_id=1, source_target_pairs={{0,16},{16,0},{32,48},{48,32},{64,80},{80,64},{96,112},{112,96},{1... | collective-permute-start | bytes 98312 | tf_op jit(solution)/shard_map/ppermute | solution.py:857
  169.9 0.9 inner_last_kernel.1.refs_8_
  170.8 0.9 collective-permute-done.19.refs_5_
  171.8 2.0 %collective-permute-done.20.refs_6_ = f32[64,128]{1,0:T(8,128)S(1)} collective-permute-done((f32[64,128]{1,0:T(8,128)S(1)}, f32[64,128]{1,0:T(8,128)S(1)}, u32[]{:S(2)}, u32[]{:S(2)}) %collective-permute-start.20) | collective-permute-done | bytes 32800 | tf_op jit(solution)/shard_map/ppermute | solution.py:857
  173.8 1.4 last_kernel.1
  (41 shorter events, 2.6 us)
Async XLA Ops:
  0.1 1.1 copy-start.7
  1.2 0.9 copy-start.10
  2.2 0.7 copy-start.15
  4.0 16.1 %collective-permute-start = (f32[1024,128]{1,0:T(8,128)S(1)}, f32[1024,128]{1,0:T(8,128)S(1)}, u32[]{:S(2)}, u32[]{:S(2)}) collective-permute-start(f32[1024,128]{1,0:T(8,128)S(1)} %get-tuple-element.59), channel_id=1, source_target_pairs={{0,15},{1,2},{2,1},{3,4},{4,3},{5,6},{6,5},{7,8},{8,7},{9,10},{10,... | collective-permute-start | bytes 1572872 | tf_op jit(solution)/shard_map/ppermute | solution.py:857
  6.0 14.2 %collective-permute-start.1 = (f32[1024,128]{1,0:T(8,128)S(1)}, f32[1024,128]{1,0:T(8,128)S(1)}, u32[]{:S(2)}, u32[]{:S(2)}) collective-permute-start(f32[1024,128]{1,0:T(8,128)S(1)} %get-tuple-element.60), channel_id=1, source_target_pairs={{0,1},{1,0},{2,3},{3,2},{4,5},{5,4},{6,7},{7,6},{8,9},{9,8},{10,11... | collective-permute-start | bytes 1572872 | tf_op jit(solution)/shard_map/ppermute | solution.py:857
  9.4 1.3 copy-start
  10.6 9.5 %copy-start.1 = (f32[2352,128]{1,0:T(8,128)S(1)}, f32[2352,128]{1,0:T(8,128)}, u32[]{:S(2)}) copy-start(f32[2352,128]{1,0:T(8,128)} %constant.11.clone.refs_1_.refs_6_.refs_3_.refs_9_.refs_7_.refs_8_.refs_10_) | copy-start | bytes 3612676
  21.9 16.1 %collective-permute-start.2 = (f32[2,128,128]{2,1,0:T(8,128)S(1)}, f32[2,128,128]{2,1,0:T(8,128)S(1)}, u32[]{:S(2)}, u32[]{:S(2)}) collective-permute-start(f32[2,128,128]{2,1,0:T(8,128)S(1)} %get-tuple-element.63), channel_id=1, source_target_pairs={{0,496},{16,32},{32,16},{48,64},{64,48},{80,96},{96,80},{112,128},... | collective-permute-start | bytes 393224 | tf_op jit(solution)/shard_map/ppermute | solution.py:857
  35.1 6.9 %collective-permute-start.3 = (f32[2,128,128]{2,1,0:T(8,128)S(1)}, f32[2,128,128]{2,1,0:T(8,128)S(1)}, u32[]{:S(2)}, u32[]{:S(2)}) collective-permute-start(f32[2,128,128]{2,1,0:T(8,128)S(1)} %get-tuple-element.64), channel_id=1, source_target_pairs={{0,16},{16,0},{32,48},{48,32},{64,80},{80,64},{96,112},{112,96},{1... | collective-permute-start | bytes 393224 | tf_op jit(solution)/shard_map/ppermute | solution.py:857
  43.5 9.8 %collective-permute-start.4 = (f32[2,64,128]{2,1,0:T(8,128)S(1)}, f32[2,64,128]{2,1,0:T(8,128)S(1)}, u32[]{:S(2)}, u32[]{:S(2)}) collective-permute-start(f32[2,64,128]{2,1,0:T(8,128)S(1)} %get-tuple-element.70), channel_id=1, source_target_pairs={{0,496},{16,32},{32,16},{48,64},{64,48},{80,96},{96,80},{112,128},... | collective-permute-start | bytes 196616 | tf_op jit(solution)/shard_map/ppermute | solution.py:857
  47.1 6.2 %collective-permute-start.5 = (f32[2,64,128]{2,1,0:T(8,128)S(1)}, f32[2,64,128]{2,1,0:T(8,128)S(1)}, u32[]{:S(2)}, u32[]{:S(2)}) collective-permute-start(f32[2,64,128]{2,1,0:T(8,128)S(1)} %get-tuple-element.71), channel_id=1, source_target_pairs={{0,16},{16,0},{32,48},{48,32},{64,80},{80,64},{96,112},{112,96},{1... | collective-permute-start | bytes 196616 | tf_op jit(solution)/shard_map/ppermute | solution.py:857
  55.6 23.6 %copy-start.2 = (f32[2,1536,128]{2,1,0:T(8,128)}, f32[2,1536,128]{2,1,0:T(8,128)S(1)}, u32[]{:S(2)}) copy-start(f32[2,1536,128]{2,1,0:T(8,128)S(1)} %get-tuple-element.74.refs_8_.refs_1_) | copy-start | bytes 4718596
  55.6 9.5 %collective-permute-start.6 = (f32[2,40,128]{2,1,0:T(8,128)S(1)}, f32[2,40,128]{2,1,0:T(8,128)S(1)}, u32[]{:S(2)}, u32[]{:S(2)}) collective-permute-start(f32[2,40,128]{2,1,0:T(8,128)S(1)} %get-tuple-element.77), channel_id=1, source_target_pairs={{0,496},{16,32},{32,16},{48,64},{64,48},{80,96},{96,80},{112,128},... | collective-permute-start | bytes 122888 | tf_op jit(solution)/shard_map/ppermute | solution.py:857
  61.4 5.9 %collective-permute-start.7 = (f32[2,40,128]{2,1,0:T(8,128)S(1)}, f32[2,40,128]{2,1,0:T(8,128)S(1)}, u32[]{:S(2)}, u32[]{:S(2)}) collective-permute-start(f32[2,40,128]{2,1,0:T(8,128)S(1)} %get-tuple-element.78), channel_id=1, source_target_pairs={{0,16},{16,0},{32,48},{48,32},{64,80},{80,64},{96,112},{112,96},{1... | collective-permute-start | bytes 122888 | tf_op jit(solution)/shard_map/ppermute | solution.py:857
  68.5 11.9 %copy-start.8 = (f32[2,64,128]{2,1,0:T(8,128)}, f32[2,64,128]{2,1,0:T(8,128)S(1)}, u32[]{:S(2)}) copy-start(f32[2,64,128]{2,1,0:T(8,128)S(1)} %get-tuple-element.82.refs_3_.refs_7_) | copy-start | bytes 196612
  68.5 9.2 %collective-permute-start.8 = (f32[2,16,128]{2,1,0:T(8,128)S(1)}, f32[2,16,128]{2,1,0:T(8,128)S(1)}, u32[]{:S(2)}, u32[]{:S(2)}) collective-permute-start(f32[2,16,128]{2,1,0:T(8,128)S(1)} %get-tuple-element.84), channel_id=1, source_target_pairs={{0,496},{16,32},{32,16},{48,64},{64,48},{80,96},{96,80},{112,128},... | collective-permute-start | bytes 49160 | tf_op jit(solution)/shard_map/ppermute | solution.py:857
  72.1 5.6 %collective-permute-start.9 = (f32[2,16,128]{2,1,0:T(8,128)S(1)}, f32[2,16,128]{2,1,0:T(8,128)S(1)}, u32[]{:S(2)}, u32[]{:S(2)}) collective-permute-start(f32[2,16,128]{2,1,0:T(8,128)S(1)} %get-tuple-element.85), channel_id=1, source_target_pairs={{0,16},{16,0},{32,48},{48,32},{64,80},{80,64},{96,112},{112,96},{1... | collective-permute-start | bytes 49160 | tf_op jit(solution)/shard_map/ppermute | solution.py:857
  79.1 0.6 copy-start.11
  79.8 0.6 copy-start.13
  81.1 22.8 %all-to-all-start = ((f32[32,8,128]{2,1,0:T(8,128)}), f32[32,8,128]{2,1,0:T(8,128)}, u32[]{:S(2)}, u32[]{:S(2)}) async-start(f32[32,8,128]{2,1,0:T(8,128)} %broadcast_in_dim.4), calls=%async_computation | async-start | bytes 262144 | tf_op jit(solution)/shard_map/all_to_all | solution.py:863
  86.8 6.3 %collective-permute-start.10 = (f32[192,128]{1,0:T(8,128)}, f32[192,128]{1,0:T(8,128)S(1)}, u32[]{:S(2)}, u32[]{:S(2)}) collective-permute-start(f32[192,128]{1,0:T(8,128)} %copy-done.11), channel_id=1, source_target_pairs={{0,15},{1,2},{2,1},{3,4},{4,3},{5,6},{6,5},{7,8},{8,7},{9,10},{10,... | collective-permute-start | bytes 294920 | tf_op jit(solution)/shard_map/ppermute | solution.py:857
  88.7 4.4 %collective-permute-start.11 = (f32[192,128]{1,0:T(8,128)}, f32[192,128]{1,0:T(8,128)S(1)}, u32[]{:S(2)}, u32[]{:S(2)}) collective-permute-start(f32[192,128]{1,0:T(8,128)} %copy-done.13), channel_id=1, source_target_pairs={{0,1},{1,0},{2,3},{3,2},{4,5},{5,4},{6,7},{7,6},{8,9},{9,8},{10,11... | collective-permute-start | bytes 294920 | tf_op jit(solution)/shard_map/ppermute | solution.py:857
  93.1 0.9 copy-start.12
  94.0 0.9 copy-start.14
  95.9 0.7 copy-start.4
  96.6 0.6 copy-start.16
  97.2 0.6 copy-start.18
  103.8 0.9 copy-start.5
  104.8 16.5 %copy-start.19 = (f32[2,64,128]{2,1,0:T(8,128)S(1)}, f32[2,64,128]{2,1,0:T(8,128)}, u32[]{:S(2)}) copy-start(f32[2,64,128]{2,1,0:T(8,128)} %copy-done.18) | copy-start | bytes 196612
  104.8 19.2 %copy-start.17 = (f32[2,64,128]{2,1,0:T(8,128)S(1)}, f32[2,64,128]{2,1,0:T(8,128)}, u32[]{:S(2)}) copy-start(f32[2,64,128]{2,1,0:T(8,128)} %copy-done.16) | copy-start | bytes 196612
  104.8 26.5 %copy-start.6 = (f32[2,192,128]{2,1,0:T(8,128)S(1)}, f32[2,192,128]{2,1,0:T(8,128)}, u32[]{:S(2)}) copy-start(f32[2,192,128]{2,1,0:T(8,128)} %copy-done.4) | copy-start | bytes 589828
  104.8 26.5 %copy-start.9 = (f32[2,64,128]{2,1,0:T(8,128)S(1)}, f32[2,64,128]{2,1,0:T(8,128)}, u32[]{:S(2)}) copy-start(f32[2,64,128]{2,1,0:T(8,128)} %copy-done.8) | copy-start | bytes 196612
  119.2 29.8 %copy-start.3 = (f32[2,1536,128]{2,1,0:T(8,128)S(1)}, f32[2,1536,128]{2,1,0:T(8,128)}, u32[]{:S(2)}) copy-start(f32[2,1536,128]{2,1,0:T(8,128)} %copy-done.2) | copy-start | bytes 4718596
  119.2 12.1 %collective-permute-start.12 = (f32[1088,128]{1,0:T(8,128)S(1)}, f32[1088,128]{1,0:T(8,128)S(1)}, u32[]{:S(2)}, u32[]{:S(2)}) collective-permute-start(f32[1088,128]{1,0:T(8,128)S(1)} %bitcast.9), channel_id=1, source_target_pairs={{0,1},{1,0},{2,3},{3,2},{4,5},{5,4},{6,7},{7,6},{8,9},{9,8},{10,11... | collective-permute-start | bytes 1671176 | tf_op jit(solution)/shard_map/ppermute | solution.py:938
  121.2 10.0 %collective-permute-start.13 = (f32[2,64,128]{2,1,0:T(8,128)S(1)}, f32[2,64,128]{2,1,0:T(8,128)S(1)}, u32[]{:S(2)}, u32[]{:S(2)}) collective-permute-start(f32[2,64,128]{2,1,0:T(8,128)S(1)} %copy-done.19), channel_id=1, source_target_pairs={{0,496},{16,32},{32,16},{48,64},{64,48},{80,96},{96,80},{112,128},... | collective-permute-start | bytes 196616 | tf_op jit(solution)/shard_map/ppermute | solution.py:857
  124.0 7.2 %collective-permute-start.14 = (f32[2,64,128]{2,1,0:T(8,128)S(1)}, f32[2,64,128]{2,1,0:T(8,128)S(1)}, u32[]{:S(2)}, u32[]{:S(2)}) collective-permute-start(f32[2,64,128]{2,1,0:T(8,128)S(1)} %copy-done.17), channel_id=1, source_target_pairs={{0,16},{16,0},{32,48},{48,32},{64,80},{80,64},{96,112},{112,96},{1... | collective-permute-start | bytes 196616 | tf_op jit(solution)/shard_map/ppermute | solution.py:857
  137.8 9.2 %collective-permute-start.15 = (f32[2,16,128]{2,1,0:T(8,128)S(1)}, f32[2,16,128]{2,1,0:T(8,128)S(1)}, u32[]{:S(2)}, u32[]{:S(2)}) collective-permute-start(f32[2,16,128]{2,1,0:T(8,128)S(1)} %get-tuple-element.96), channel_id=1, source_target_pairs={{0,496},{16,32},{32,16},{48,64},{64,48},{80,96},{96,80},{112,128},... | collective-permute-start | bytes 49160 | tf_op jit(solution)/shard_map/ppermute | solution.py:857
  143.4 5.6 %collective-permute-start.16 = (f32[2,16,128]{2,1,0:T(8,128)S(1)}, f32[2,16,128]{2,1,0:T(8,128)S(1)}, u32[]{:S(2)}, u32[]{:S(2)}) collective-permute-start(f32[2,16,128]{2,1,0:T(8,128)S(1)} %get-tuple-element.97), channel_id=1, source_target_pairs={{0,16},{16,0},{32,48},{48,32},{64,80},{80,64},{96,112},{112,96},{1... | collective-permute-start | bytes 49160 | tf_op jit(solution)/shard_map/ppermute | solution.py:857
  150.7 9.8 %collective-permute-start.17 = (f32[2,64,128]{2,1,0:T(8,128)S(1)}, f32[2,64,128]{2,1,0:T(8,128)S(1)}, u32[]{:S(2)}, u32[]{:S(2)}) collective-permute-start(f32[2,64,128]{2,1,0:T(8,128)S(1)} %get-tuple-element.101), channel_id=1, source_target_pairs={{0,496},{16,32},{32,16},{48,64},{64,48},{80,96},{96,80},{112,128},... | collective-permute-start | bytes 196616 | tf_op jit(solution)/shard_map/ppermute | solution.py:857
  154.5 6.2 %collective-permute-start.18 = (f32[2,64,128]{2,1,0:T(8,128)S(1)}, f32[2,64,128]{2,1,0:T(8,128)S(1)}, u32[]{:S(2)}, u32[]{:S(2)}) collective-permute-start(f32[2,64,128]{2,1,0:T(8,128)S(1)} %get-tuple-element.102), channel_id=1, source_target_pairs={{0,16},{16,0},{32,48},{48,32},{64,80},{80,64},{96,112},{112,96},{1... | collective-permute-start | bytes 196616 | tf_op jit(solution)/shard_map/ppermute | solution.py:857
  162.3 9.4 %collective-permute-start.19 = (f32[64,128]{1,0:T(8,128)S(1)}, f32[64,128]{1,0:T(8,128)S(1)}, u32[]{:S(2)}, u32[]{:S(2)}) collective-permute-start(f32[64,128]{1,0:T(8,128)S(1)} %get-tuple-element.107), channel_id=1, source_target_pairs={{0,496},{16,32},{32,16},{48,64},{64,48},{80,96},{96,80},{112,128},... | collective-permute-start | bytes 98312 | tf_op jit(solution)/shard_map/ppermute | solution.py:857
  168.0 5.8 %collective-permute-start.20 = (f32[64,128]{1,0:T(8,128)S(1)}, f32[64,128]{1,0:T(8,128)S(1)}, u32[]{:S(2)}, u32[]{:S(2)}) collective-permute-start(f32[64,128]{1,0:T(8,128)S(1)} %get-tuple-element.108), channel_id=1, source_target_pairs={{0,16},{16,0},{32,48},{48,32},{64,80},{80,64},{96,112},{112,96},{1... | collective-permute-start | bytes 98312 | tf_op jit(solution)/shard_map/ppermute | solution.py:857

commit v3 on v2

--- a/solution.py
+++ b/solution.py
@@ -639,7 +639,7 @@
 
 
 def coarse_kernel(
-    pos, columns, others, wider, far, near_side, g4, inv4, gm, gmt, up4, gm_first, gmt_first,
+    pos, columns, wider, far, near_side, g4, inv4, gm, gmt, up4, gm_first, gmt_first,
     gm_last, gmt_last,
     res, u, sol, acc, face_a, face_b, vals, x2, es, ea, er, es0, ea0, er0, dg, ri,
 ):
@@ -652,9 +652,7 @@
     even_a = is_even(pos, 1)
 
     def rows_of(d, start, count):
-        at = d // 2 * size + start
-        x, y = columns[at : at + count], others[at : at + count]
-        return jnp.where(even_a, x, y) if d % 2 == 0 else jnp.where(even_a, y, x)
+        return columns[d * size + start : d * size + start + count]
 
     def field(k):
         return [rows_of(d, k * ns, ns) for d in range(na)]
@@ -857,10 +855,10 @@
     return lax.ppermute(far, axis, pairs_far), lax.ppermute(near, axis, pairs_near)
 
 
-def spread(x, axis, groups=None):
-    size = len(groups[0]) if groups else lax.axis_size(axis)
+def spread(x, axis):
+    size = lax.axis_size(axis)
     copies = jnp.broadcast_to(x[None], (size,) + x.shape)
-    return lax.all_to_all(copies, axis, 0, 0, axis_index_groups=groups).reshape(-1, LANES)
+    return lax.all_to_all(copies, axis, 0, 0).reshape(-1, LANES)
 
 
 def on_device(element_load, metric, element_order):
@@ -933,16 +931,13 @@
     (columns,) = call(
         column_kernel, (columns, wider), [(size, LANES)], (), 0
     )
-    cores = [list(range(core, na, 2)) for core in range(2)]
-    columns = spread(columns, "azim", cores)
-    others = lax.ppermute(columns, "azim", [(i, i ^ 1) for i in range(na)])
+    columns = spread(columns, "azim")
     whole = (ns, na * LANES)
     res4, u4, sol4, acc, a, b = call(
         coarse_kernel,
         (
             pos,
             columns,
-            others,
             wider,
             *sides,
             g4,

time: 176 us -> 176 us (level)
  blocking collectives: 13.2 us -> 0 us
  waiting for transfers between devices: 47.4 us -> 53.7 us
  local copies, waits for them, and re-layouts: 10.6 us -> 16.4 us
    all_to_all x1 -> x0, blocking collectives: 13.2 us -> none  [spread(): lax.all_to_all(copies, axis, 0, 0, axis_index_groups=groups)]
    all_to_all x1 -> x2, starting transfers between devices: 5.73 us -> 11.5 us  [spread(): return lax.all_to_all(copies, axis, 0, 0).reshape(-1, LANES)]
    unnamed x40 -> x44, local copies, waits for them, and re-layouts: 9.95 us -> 14.6 us
    ppermute x10, starting transfers between devices: 47.9 us -> 43.3 us  [exchange(): lax.ppermute(far, axis, pairs_far)]
    all_to_all x1 -> x2, waiting for transfers between devices: 5.98 us -> 10.2 us  [spread(): return lax.all_to_all(copies, axis, 0, 0).reshape(-1, LANES)]
    ppermute x10, waiting for transfers between devices: 30.9 us -> 35.1 us  [exchange(): lax.ppermute(far, axis, pairs_far)]
    ppermute x1 -> x0, starting transfers between devices: 2.04 us -> none  [on_device(): others = lax.ppermute(columns, 'azim', [(i, i ^ 1) for i in range(na)])]
    ppermute x10, waiting for transfers between devices: 10.4 us -> 8.43 us  [exchange(): lax.ppermute(near, axis, pairs_near)]
  transfers between devices with their start and end apart: 22 -> 22, of which waited for: 16 -> 15; matrix products, arithmetic and copies ran while one was open for 0% -> 0% of each run, Pallas kernels for 3% -> 3%
where the time goes in v3:
time: 176 us; the launch traced here: 175 us
  starting transfers between devices  76.8 us (44%)
  waiting for transfers between devices  53.7 us (31%)
  Pallas kernels  27.7 us (16%)
  local copies, waits for them, and re-layouts  16.4 us (9%)
    ppermute x10, starting transfers between devices, exchange(): lax.ppermute(far, axis, pairs_far)  43.3 us
    ppermute x10, waiting for transfers between devices, exchange(): lax.ppermute(far, axis, pairs_far)  35.1 us
    pallas_call x17, Pallas kernels, call(): pl.pallas_call(body, out_shape=[jax.ShapeDtypeStruct(s, F32) for s in out...  27.7 us
    ppermute x10, starting transfers between devices, exchange(): lax.ppermute(near, axis, pairs_near)  22 us
    unnamed x44, local copies, waits for them, and re-layouts  14.6 us
    all_to_all x2, starting transfers between devices, spread(): return lax.all_to_all(copies, axis, 0, 0).reshape(-1, LANES)  11.5 us
    all_to_all x2, waiting for transfers between devices, spread(): return lax.all_to_all(copies, axis, 0, 0).reshape(-1, LANES)  10.2 us
    ppermute x10, waiting for transfers between devices, exchange(): lax.ppermute(near, axis, pairs_near)  8.43 us
  transfers between devices with their start and end apart: 22, of which 15 were waited for; matrix products, arithmetic and copies ran while one was open for 0% of the time, Pallas kernels for 3%

profile of v3, /device:TPU:8, one launch (start us, length us, event | category | flops | bytes accessed | tf_op | source)
XLA Modules:
  0.0 175.0 jit_solution(1121982894290385397)
XLA Ops:
  0.1 1.1 copy-done.7
  1.2 0.9 copy-done.10
  2.8 1.2 order_kernel.1
  4.0 1.9 %collective-permute-start = (f32[1024,128]{1,0:T(8,128)S(1)}, f32[1024,128]{1,0:T(8,128)S(1)}, u32[]{:S(2)}, u32[]{:S(2)}) collective-permute-start(f32[1024,128]{1,0:T(8,128)S(1)} %get-tuple-element.59), channel_id=1, source_target_pairs={{0,15},{1,2},{2,1},{3,4},{4,3},{5,6},{6,5},{7,8},{8,7},{9,10},{10,... | collective-permute-start | bytes 1572872 | tf_op jit(solution)/shard_map/ppermute | solution.py:855
  6.0 3.4 %collective-permute-start.1 = (f32[1024,128]{1,0:T(8,128)S(1)}, f32[1024,128]{1,0:T(8,128)S(1)}, u32[]{:S(2)}, u32[]{:S(2)}) collective-permute-start(f32[1024,128]{1,0:T(8,128)S(1)} %get-tuple-element.60), channel_id=1, source_target_pairs={{0,1},{1,0},{2,3},{3,2},{4,5},{5,4},{6,7},{7,6},{8,9},{9,8},{10,11... | collective-permute-start | bytes 1572872 | tf_op jit(solution)/shard_map/ppermute | solution.py:855
  9.4 1.3 copy-done
  11.0 9.2 %collective-permute-done.refs_4_ = f32[1024,128]{1,0:T(8,128)S(1)} collective-permute-done((f32[1024,128]{1,0:T(8,128)S(1)}, f32[1024,128]{1,0:T(8,128)S(1)}, u32[]{:S(2)}, u32[]{:S(2)}) %collective-permute-start) | collective-permute-done | bytes 524320 | tf_op jit(solution)/shard_map/ppermute | solution.py:855
  20.2 1.8 %setup_kernel.1 = (f32[2,1536,128]{2,1,0:T(8,128)S(1)}, f32[2,512,128]{2,1,0:T(8,128)S(1)}, f32[2,512,128]{2,1,0:T(8,128)S(1)}, f32[2,128,128]{2,1,0:T(8,128)S(1)}, f32[2,128,128]{2,1,0:T(8,128)S(1)}) custom-call(s32[2]{0:T(128)S(1)} %pad_add_fusion.refs_0_, f32[1536,128]{1,0:T(8,128)S(1)} %get-tuple-element.57.refs_0_.refs_1_, ...), custom_call_target="tpu_custom_call" | custom-call | tf_op jit(solution)/shard_map/setup_kernel/pallas_call | solution.py:840
  21.9 13.1 %collective-permute-start.2 = (f32[2,128,128]{2,1,0:T(8,128)S(1)}, f32[2,128,128]{2,1,0:T(8,128)S(1)}, u32[]{:S(2)}, u32[]{:S(2)}) collective-permute-start(f32[2,128,128]{2,1,0:T(8,128)S(1)} %get-tuple-element.63), channel_id=1, source_target_pairs={{0,496},{16,32},{32,16},{48,64},{64,48},{80,96},{96,80},{112,128},... | collective-permute-start | bytes 393224 | tf_op jit(solution)/shard_map/ppermute | solution.py:855
  35.1 1.9 %collective-permute-start.3 = (f32[2,128,128]{2,1,0:T(8,128)S(1)}, f32[2,128,128]{2,1,0:T(8,128)S(1)}, u32[]{:S(2)}, u32[]{:S(2)}) collective-permute-start(f32[2,128,128]{2,1,0:T(8,128)S(1)} %get-tuple-element.64), channel_id=1, source_target_pairs={{0,16},{16,0},{32,48},{48,32},{64,80},{80,64},{96,112},{112,96},{1... | collective-permute-start | bytes 393224 | tf_op jit(solution)/shard_map/ppermute | solution.py:855
  37.0 1.0 collective-permute-done.2.refs_3_
  38.0 3.9 %collective-permute-done.3.refs_4_ = f32[2,128,128]{2,1,0:T(8,128)S(1)} collective-permute-done((f32[2,128,128]{2,1,0:T(8,128)S(1)}, f32[2,128,128]{2,1,0:T(8,128)S(1)}, u32[]{:S(2)}, u32[]{:S(2)}) %collective-permute-start.3) | collective-permute-done | bytes 131104 | tf_op jit(solution)/shard_map/ppermute | solution.py:855
  41.9 1.6 first_kernel.1
  43.5 3.6 %collective-permute-start.4 = (f32[2,64,128]{2,1,0:T(8,128)S(1)}, f32[2,64,128]{2,1,0:T(8,128)S(1)}, u32[]{:S(2)}, u32[]{:S(2)}) collective-permute-start(f32[2,64,128]{2,1,0:T(8,128)S(1)} %get-tuple-element.70), channel_id=1, source_target_pairs={{0,496},{16,32},{32,16},{48,64},{64,48},{80,96},{96,80},{112,128},... | collective-permute-start | bytes 196616 | tf_op jit(solution)/shard_map/ppermute | solution.py:855
  47.1 1.9 %collective-permute-start.5 = (f32[2,64,128]{2,1,0:T(8,128)S(1)}, f32[2,64,128]{2,1,0:T(8,128)S(1)}, u32[]{:S(2)}, u32[]{:S(2)}) collective-permute-start(f32[2,64,128]{2,1,0:T(8,128)S(1)} %get-tuple-element.71), channel_id=1, source_target_pairs={{0,16},{16,0},{32,48},{48,32},{64,80},{80,64},{96,112},{112,96},{1... | collective-permute-start | bytes 196616 | tf_op jit(solution)/shard_map/ppermute | solution.py:855
  49.1 1.4 coarsen_kernel.1
  50.5 0.8 inner_kernel.2.refs_3_
  51.3 2.0 %collective-permute-done.4.refs_4_ = f32[2,64,128]{2,1,0:T(8,128)S(1)} collective-permute-done((f32[2,64,128]{2,1,0:T(8,128)S(1)}, f32[2,64,128]{2,1,0:T(8,128)S(1)}, u32[]{:S(2)}, u32[]{:S(2)}) %collective-permute-start.4) | collective-permute-done | bytes 65568 | tf_op jit(solution)/shard_map/ppermute | solution.py:855
  53.3 2.2 %second_kernel.1 = (f32[2,1536,128]{2,1,0:T(8,128)S(1)}, f32[2,64,128]{2,1,0:T(8,128)S(1)}, f32[2,40,128]{2,1,0:T(8,128)S(1)}, f32[2,40,128]{2,1,0:T(8,128)S(1)}) custom-call(s32[2]{0:T(128)S(1)} %pad_add_fusion.refs_0_, f32[2,512,128]{2,1,0:T(8,128)S(1)} %get-tuple-element.66.refs_1_, f32[2,512,128]{2,1,0:T(8,128)S(1)} %get-tuple-element.67.refs_2_.refs_6_.refs_5_.refs_7_, ...), custom_call_target="tpu_custom_call" | custom-call | tf_op jit(solution)/shard_map/second_kernel/pallas_call | solution.py:840
  55.6 5.8 %collective-permute-start.6 = (f32[2,40,128]{2,1,0:T(8,128)S(1)}, f32[2,40,128]{2,1,0:T(8,128)S(1)}, u32[]{:S(2)}, u32[]{:S(2)}) collective-permute-start(f32[2,40,128]{2,1,0:T(8,128)S(1)} %get-tuple-element.77), channel_id=1, source_target_pairs={{0,496},{16,32},{32,16},{48,64},{64,48},{80,96},{96,80},{112,128},... | collective-permute-start | bytes 122888 | tf_op jit(solution)/shard_map/ppermute | solution.py:855
  61.4 1.9 %collective-permute-start.7 = (f32[2,40,128]{2,1,0:T(8,128)S(1)}, f32[2,40,128]{2,1,0:T(8,128)S(1)}, u32[]{:S(2)}, u32[]{:S(2)}) collective-permute-start(f32[2,40,128]{2,1,0:T(8,128)S(1)} %get-tuple-element.78), channel_id=1, source_target_pairs={{0,16},{16,0},{32,48},{48,32},{64,80},{80,64},{96,112},{112,96},{1... | collective-permute-start | bytes 122888 | tf_op jit(solution)/shard_map/ppermute | solution.py:855
  63.4 1.7 collective-permute-done.6.refs_4_
  65.1 2.2 %collective-permute-done.7.refs_5_ = f32[2,40,128]{2,1,0:T(8,128)S(1)} collective-permute-done((f32[2,40,128]{2,1,0:T(8,128)S(1)}, f32[2,40,128]{2,1,0:T(8,128)S(1)}, u32[]{:S(2)}, u32[]{:S(2)}) %collective-permute-start.7) | collective-permute-done | bytes 40992 | tf_op jit(solution)/shard_map/ppermute | solution.py:855
  67.3 1.2 third_kernel.1
  68.5 3.6 %collective-permute-start.8 = (f32[2,16,128]{2,1,0:T(8,128)S(1)}, f32[2,16,128]{2,1,0:T(8,128)S(1)}, u32[]{:S(2)}, u32[]{:S(2)}) collective-permute-start(f32[2,16,128]{2,1,0:T(8,128)S(1)} %get-tuple-element.84), channel_id=1, source_target_pairs={{0,496},{16,32},{32,16},{48,64},{64,48},{80,96},{96,80},{112,128},... | collective-permute-start | bytes 49160 | tf_op jit(solution)/shard_map/ppermute | solution.py:855
  72.1 1.9 %collective-permute-start.9 = (f32[2,16,128]{2,1,0:T(8,128)S(1)}, f32[2,16,128]{2,1,0:T(8,128)S(1)}, u32[]{:S(2)}, u32[]{:S(2)}) collective-permute-start(f32[2,16,128]{2,1,0:T(8,128)S(1)} %get-tuple-element.85), channel_id=1, source_target_pairs={{0,16},{16,0},{32,48},{48,32},{64,80},{80,64},{96,112},{112,96},{1... | collective-permute-start | bytes 49160 | tf_op jit(solution)/shard_map/ppermute | solution.py:855
  74.1 3.7 %collective-permute-done.8.refs_5_ = f32[2,16,128]{2,1,0:T(8,128)S(1)} collective-permute-done((f32[2,16,128]{2,1,0:T(8,128)S(1)}, f32[2,16,128]{2,1,0:T(8,128)S(1)}, u32[]{:S(2)}, u32[]{:S(2)}) %collective-permute-start.8) | collective-permute-done | bytes 16416 | tf_op jit(solution)/shard_map/ppermute | solution.py:855
  77.8 1.3 fourth_kernel.1
  81.1 5.7 %all-to-all-start = ((f32[32,8,128]{2,1,0:T(8,128)}), f32[32,8,128]{2,1,0:T(8,128)}, u32[]{:S(2)}, u32[]{:S(2)}) async-start(f32[32,8,128]{2,1,0:T(8,128)} %broadcast_in_dim.4), calls=%async_computation | async-start | bytes 262144 | tf_op jit(solution)/shard_map/all_to_all | solution.py:861
  86.8 1.9 %collective-permute-start.10 = (f32[192,128]{1,0:T(8,128)}, f32[192,128]{1,0:T(8,128)S(1)}, u32[]{:S(2)}, u32[]{:S(2)}) collective-permute-start(f32[192,128]{1,0:T(8,128)} %copy-done.11), channel_id=1, source_target_pairs={{0,15},{1,2},{2,1},{3,4},{4,3},{5,6},{6,5},{7,8},{8,7},{9,10},{10,... | collective-permute-start | bytes 294920 | tf_op jit(solution)/shard_map/ppermute | solution.py:855
  88.8 1.9 %collective-permute-start.11 = (f32[192,128]{1,0:T(8,128)}, f32[192,128]{1,0:T(8,128)S(1)}, u32[]{:S(2)}, u32[]{:S(2)}) collective-permute-start(f32[192,128]{1,0:T(8,128)} %copy-done.13), channel_id=1, source_target_pairs={{0,1},{1,0},{2,3},{3,2},{4,5},{5,4},{6,7},{7,6},{8,9},{9,8},{10,11... | collective-permute-start | bytes 294920 | tf_op jit(solution)/shard_map/ppermute | solution.py:855
  90.7 2.5 %collective-permute-done.10.refs_3_ = f32[192,128]{1,0:T(8,128)S(1)} collective-permute-done((f32[192,128]{1,0:T(8,128)}, f32[192,128]{1,0:T(8,128)S(1)}, u32[]{:S(2)}, u32[]{:S(2)}) %collective-permute-start.10) | collective-permute-done | bytes 98336 | tf_op jit(solution)/shard_map/ppermute | solution.py:855
  93.2 0.9 copy-done.12
  94.1 0.9 copy-done.14
  94.9 1.0 side_kernel.1
  97.9 6.0 %all-to-all-done = f32[32,8,128]{2,1,0:T(8,128)} async-done(((f32[32,8,128]{2,1,0:T(8,128)}), f32[32,8,128]{2,1,0:T(8,128)}, u32[]{:S(2)}, u32[]{:S(2)}) %all-to-all-start) | async-done | bytes 131104 | tf_op jit(solution)/shard_map/all_to_all | solution.py:861
  103.9 0.9 copy-done.5
  104.8 1.1 column_kernel.1
  105.8 1.1 broadcast_in_dim.5
  106.9 5.8 %all-to-all-start.1 = ((f32[16,136,128]{2,1,0:T(8,128)}), f32[16,136,128]{2,1,0:T(8,128)}, u32[]{:S(2)}, u32[]{:S(2)}) async-start(f32[16,136,128]{2,1,0:T(8,128)} %broadcast_in_dim.5), calls=%async_computation.1 | async-start | bytes 2228224 | tf_op jit(solution)/shard_map/all_to_all | solution.py:861
  112.7 1.9 %collective-permute-start.12 = (f32[2,64,128]{2,1,0:T(8,128)}, f32[2,64,128]{2,1,0:T(8,128)S(1)}, u32[]{:S(2)}, u32[]{:S(2)}) collective-permute-start(f32[2,64,128]{2,1,0:T(8,128)} %copy-done.21), channel_id=1, source_target_pairs={{0,496},{16,32},{32,16},{48,64},{64,48},{80,96},{96,80},{112,128},... | collective-permute-start | bytes 196616 | tf_op jit(solution)/shard_map/ppermute | solution.py:855
  114.6 2.9 %collective-permute-start.13 = (f32[2,64,128]{2,1,0:T(8,128)}, f32[2,64,128]{2,1,0:T(8,128)S(1)}, u32[]{:S(2)}, u32[]{:S(2)}) collective-permute-start(f32[2,64,128]{2,1,0:T(8,128)} %copy-done.20), channel_id=1, source_target_pairs={{0,16},{16,0},{32,48},{48,32},{64,80},{80,64},{96,112},{112,96},{1... | collective-permute-start | bytes 196616 | tf_op jit(solution)/shard_map/ppermute | solution.py:855
  117.5 6.0 %collective-permute-done.12.refs_3_ = f32[2,64,128]{2,1,0:T(8,128)S(1)} collective-permute-done((f32[2,64,128]{2,1,0:T(8,128)}, f32[2,64,128]{2,1,0:T(8,128)S(1)}, u32[]{:S(2)}, u32[]{:S(2)}) %collective-permute-start.12) | collective-permute-done | bytes 65568 | tf_op jit(solution)/shard_map/ppermute | solution.py:855
  124.7 4.2 %all-to-all-done.1 = f32[16,136,128]{2,1,0:T(8,128)} async-done(((f32[16,136,128]{2,1,0:T(8,128)}), f32[16,136,128]{2,1,0:T(8,128)}, u32[]{:S(2)}, u32[]{:S(2)}) %all-to-all-start.1) | async-done | bytes 1114144 | tf_op jit(solution)/shard_map/all_to_all | solution.py:861
  128.9 0.9 copy-done.6
  129.8 0.8 copy-done.9
  130.7 0.8 copy-done.16
  131.5 0.8 copy-done.18
  132.3 7.3 %coarse_kernel.1 = (f32[2,64,128]{2,1,0:T(8,128)S(1)}, f32[2,64,128]{2,1,0:T(8,128)S(1)}, f32[2,64,128]{2,1,0:T(8,128)S(1)}, f32[2,64,128]{2,1,0:T(8,128)S(1)}, ...) custom-call(s32[2]{0:T(128)S(1)} %pad_add_fusion.refs_0_, f32[2176,128]{1,0:T(8,128)} %bitcast.5.refs_1_, ...), custom_call_target="tpu_custom_call" | custom-call | tf_op jit(solution)/shard_map/coarse_kernel/pallas_call | solution.py:840
  139.6 1.9 %collective-permute-start.14 = (f32[2,16,128]{2,1,0:T(8,128)S(1)}, f32[2,16,128]{2,1,0:T(8,128)S(1)}, u32[]{:S(2)}, u32[]{:S(2)}) collective-permute-start(f32[2,16,128]{2,1,0:T(8,128)S(1)} %get-tuple-element.96), channel_id=1, source_target_pairs={{0,496},{16,32},{32,16},{48,64},{64,48},{80,96},{96,80},{112,128},... | collective-permute-start | bytes 49160 | tf_op jit(solution)/shard_map/ppermute | solution.py:855
  141.6 2.3 %collective-permute-start.15 = (f32[2,16,128]{2,1,0:T(8,128)S(1)}, f32[2,16,128]{2,1,0:T(8,128)S(1)}, u32[]{:S(2)}, u32[]{:S(2)}) collective-permute-start(f32[2,16,128]{2,1,0:T(8,128)S(1)} %get-tuple-element.97), channel_id=1, source_target_pairs={{0,16},{16,0},{32,48},{48,32},{64,80},{80,64},{96,112},{112,96},{1... | collective-permute-start | bytes 49160 | tf_op jit(solution)/shard_map/ppermute | solution.py:855
  143.8 5.0 %collective-permute-done.14.refs_5_ = f32[2,16,128]{2,1,0:T(8,128)S(1)} collective-permute-done((f32[2,16,128]{2,1,0:T(8,128)S(1)}, f32[2,16,128]{2,1,0:T(8,128)S(1)}, u32[]{:S(2)}, u32[]{:S(2)}) %collective-permute-start.14) | collective-permute-done | bytes 16416 | tf_op jit(solution)/shard_map/ppermute | solution.py:855
  148.9 1.6 sixth_kernel.1
  150.5 5.9 %collective-permute-start.16 = (f32[2,64,128]{2,1,0:T(8,128)S(1)}, f32[2,64,128]{2,1,0:T(8,128)S(1)}, u32[]{:S(2)}, u32[]{:S(2)}) collective-permute-start(f32[2,64,128]{2,1,0:T(8,128)S(1)} %get-tuple-element.101), channel_id=1, source_target_pairs={{0,496},{16,32},{32,16},{48,64},{64,48},{80,96},{96,80},{112,128},... | collective-permute-start | bytes 196616 | tf_op jit(solution)/shard_map/ppermute | solution.py:855
  156.4 1.9 %collective-permute-start.17 = (f32[2,64,128]{2,1,0:T(8,128)S(1)}, f32[2,64,128]{2,1,0:T(8,128)S(1)}, u32[]{:S(2)}, u32[]{:S(2)}) collective-permute-start(f32[2,64,128]{2,1,0:T(8,128)S(1)} %get-tuple-element.102), channel_id=1, source_target_pairs={{0,16},{16,0},{32,48},{48,32},{64,80},{80,64},{96,112},{112,96},{1... | collective-permute-start | bytes 196616 | tf_op jit(solution)/shard_map/ppermute | solution.py:855
  158.3 0.8 inner_kernel.3.refs_3_
  159.1 1.2 collective-permute-done.16.refs_4_
  160.3 2.2 %collective-permute-done.17.refs_5_ = f32[2,64,128]{2,1,0:T(8,128)S(1)} collective-permute-done((f32[2,64,128]{2,1,0:T(8,128)S(1)}, f32[2,64,128]{2,1,0:T(8,128)S(1)}, u32[]{:S(2)}, u32[]{:S(2)}) %collective-permute-start.17) | collective-permute-done | bytes 65568 | tf_op jit(solution)/shard_map/ppermute | solution.py:855
  162.5 1.7 seventh_kernel.1
  164.2 3.6 %collective-permute-start.18 = (f32[64,128]{1,0:T(8,128)S(1)}, f32[64,128]{1,0:T(8,128)S(1)}, u32[]{:S(2)}, u32[]{:S(2)}) collective-permute-start(f32[64,128]{1,0:T(8,128)S(1)} %get-tuple-element.107), channel_id=1, source_target_pairs={{0,496},{16,32},{32,16},{48,64},{64,48},{80,96},{96,80},{112,128},... | collective-permute-start | bytes 98312 | tf_op jit(solution)/shard_map/ppermute | solution.py:855
  167.8 1.9 %collective-permute-start.19 = (f32[64,128]{1,0:T(8,128)S(1)}, f32[64,128]{1,0:T(8,128)S(1)}, u32[]{:S(2)}, u32[]{:S(2)}) collective-permute-start(f32[64,128]{1,0:T(8,128)S(1)} %get-tuple-element.108), channel_id=1, source_target_pairs={{0,16},{16,0},{32,48},{48,32},{64,80},{80,64},{96,112},{112,96},{1... | collective-permute-start | bytes 98312 | tf_op jit(solution)/shard_map/ppermute | solution.py:855
  169.7 0.9 inner_last_kernel.1.refs_8_
  170.7 2.9 %collective-permute-done.18.refs_5_ = f32[64,128]{1,0:T(8,128)S(1)} collective-permute-done((f32[64,128]{1,0:T(8,128)S(1)}, f32[64,128]{1,0:T(8,128)S(1)}, u32[]{:S(2)}, u32[]{:S(2)}) %collective-permute-start.18) | collective-permute-done | bytes 32800 | tf_op jit(solution)/shard_map/ppermute | solution.py:855
  173.6 1.4 last_kernel.1
  (44 shorter events, 6.2 us)
Async XLA Ops:
  0.1 1.1 copy-start.7
  1.2 0.9 copy-start.10
  2.2 0.7 copy-start.19
  4.0 16.1 %collective-permute-start = (f32[1024,128]{1,0:T(8,128)S(1)}, f32[1024,128]{1,0:T(8,128)S(1)}, u32[]{:S(2)}, u32[]{:S(2)}) collective-permute-start(f32[1024,128]{1,0:T(8,128)S(1)} %get-tuple-element.59), channel_id=1, source_target_pairs={{0,15},{1,2},{2,1},{3,4},{4,3},{5,6},{6,5},{7,8},{8,7},{9,10},{10,... | collective-permute-start | bytes 1572872 | tf_op jit(solution)/shard_map/ppermute | solution.py:855
  6.0 14.2 %collective-permute-start.1 = (f32[1024,128]{1,0:T(8,128)S(1)}, f32[1024,128]{1,0:T(8,128)S(1)}, u32[]{:S(2)}, u32[]{:S(2)}) collective-permute-start(f32[1024,128]{1,0:T(8,128)S(1)} %get-tuple-element.60), channel_id=1, source_target_pairs={{0,1},{1,0},{2,3},{3,2},{4,5},{5,4},{6,7},{7,6},{8,9},{9,8},{10,11... | collective-permute-start | bytes 1572872 | tf_op jit(solution)/shard_map/ppermute | solution.py:855
  9.4 1.3 copy-start
  10.6 9.5 %copy-start.1 = (f32[2352,128]{1,0:T(8,128)S(1)}, f32[2352,128]{1,0:T(8,128)}, u32[]{:S(2)}) copy-start(f32[2352,128]{1,0:T(8,128)} %constant.11.clone.refs_1_.refs_6_.refs_3_.refs_9_.refs_7_.refs_8_.refs_10_) | copy-start | bytes 3612676
  21.9 16.1 %collective-permute-start.2 = (f32[2,128,128]{2,1,0:T(8,128)S(1)}, f32[2,128,128]{2,1,0:T(8,128)S(1)}, u32[]{:S(2)}, u32[]{:S(2)}) collective-permute-start(f32[2,128,128]{2,1,0:T(8,128)S(1)} %get-tuple-element.63), channel_id=1, source_target_pairs={{0,496},{16,32},{32,16},{48,64},{64,48},{80,96},{96,80},{112,128},... | collective-permute-start | bytes 393224 | tf_op jit(solution)/shard_map/ppermute | solution.py:855
  35.1 6.9 %collective-permute-start.3 = (f32[2,128,128]{2,1,0:T(8,128)S(1)}, f32[2,128,128]{2,1,0:T(8,128)S(1)}, u32[]{:S(2)}, u32[]{:S(2)}) collective-permute-start(f32[2,128,128]{2,1,0:T(8,128)S(1)} %get-tuple-element.64), channel_id=1, source_target_pairs={{0,16},{16,0},{32,48},{48,32},{64,80},{80,64},{96,112},{112,96},{1... | collective-permute-start | bytes 393224 | tf_op jit(solution)/shard_map/ppermute | solution.py:855
  43.5 9.8 %collective-permute-start.4 = (f32[2,64,128]{2,1,0:T(8,128)S(1)}, f32[2,64,128]{2,1,0:T(8,128)S(1)}, u32[]{:S(2)}, u32[]{:S(2)}) collective-permute-start(f32[2,64,128]{2,1,0:T(8,128)S(1)} %get-tuple-element.70), channel_id=1, source_target_pairs={{0,496},{16,32},{32,16},{48,64},{64,48},{80,96},{96,80},{112,128},... | collective-permute-start | bytes 196616 | tf_op jit(solution)/shard_map/ppermute | solution.py:855
  47.1 6.2 %collective-permute-start.5 = (f32[2,64,128]{2,1,0:T(8,128)S(1)}, f32[2,64,128]{2,1,0:T(8,128)S(1)}, u32[]{:S(2)}, u32[]{:S(2)}) collective-permute-start(f32[2,64,128]{2,1,0:T(8,128)S(1)} %get-tuple-element.71), channel_id=1, source_target_pairs={{0,16},{16,0},{32,48},{48,32},{64,80},{80,64},{96,112},{112,96},{1... | collective-permute-start | bytes 196616 | tf_op jit(solution)/shard_map/ppermute | solution.py:855
  55.6 23.6 %copy-start.2 = (f32[2,1536,128]{2,1,0:T(8,128)}, f32[2,1536,128]{2,1,0:T(8,128)S(1)}, u32[]{:S(2)}) copy-start(f32[2,1536,128]{2,1,0:T(8,128)S(1)} %get-tuple-element.74.refs_8_.refs_1_) | copy-start | bytes 4718596
  55.6 9.5 %collective-permute-start.6 = (f32[2,40,128]{2,1,0:T(8,128)S(1)}, f32[2,40,128]{2,1,0:T(8,128)S(1)}, u32[]{:S(2)}, u32[]{:S(2)}) collective-permute-start(f32[2,40,128]{2,1,0:T(8,128)S(1)} %get-tuple-element.77), channel_id=1, source_target_pairs={{0,496},{16,32},{32,16},{48,64},{64,48},{80,96},{96,80},{112,128},... | collective-permute-start | bytes 122888 | tf_op jit(solution)/shard_map/ppermute | solution.py:855
  61.4 5.9 %collective-permute-start.7 = (f32[2,40,128]{2,1,0:T(8,128)S(1)}, f32[2,40,128]{2,1,0:T(8,128)S(1)}, u32[]{:S(2)}, u32[]{:S(2)}) collective-permute-start(f32[2,40,128]{2,1,0:T(8,128)S(1)} %get-tuple-element.78), channel_id=1, source_target_pairs={{0,16},{16,0},{32,48},{48,32},{64,80},{80,64},{96,112},{112,96},{1... | collective-permute-start | bytes 122888 | tf_op jit(solution)/shard_map/ppermute | solution.py:855
  68.5 11.9 %copy-start.8 = (f32[2,64,128]{2,1,0:T(8,128)}, f32[2,64,128]{2,1,0:T(8,128)S(1)}, u32[]{:S(2)}) copy-start(f32[2,64,128]{2,1,0:T(8,128)S(1)} %get-tuple-element.82.refs_3_.refs_6_.refs_7_) | copy-start | bytes 196612
  68.5 9.2 %collective-permute-start.8 = (f32[2,16,128]{2,1,0:T(8,128)S(1)}, f32[2,16,128]{2,1,0:T(8,128)S(1)}, u32[]{:S(2)}, u32[]{:S(2)}) collective-permute-start(f32[2,16,128]{2,1,0:T(8,128)S(1)} %get-tuple-element.84), channel_id=1, source_target_pairs={{0,496},{16,32},{32,16},{48,64},{64,48},{80,96},{96,80},{112,128},... | collective-permute-start | bytes 49160 | tf_op jit(solution)/shard_map/ppermute | solution.py:855
  72.1 5.6 %collective-permute-start.9 = (f32[2,16,128]{2,1,0:T(8,128)S(1)}, f32[2,16,128]{2,1,0:T(8,128)S(1)}, u32[]{:S(2)}, u32[]{:S(2)}) collective-permute-start(f32[2,16,128]{2,1,0:T(8,128)S(1)} %get-tuple-element.85), channel_id=1, source_target_pairs={{0,16},{16,0},{32,48},{48,32},{64,80},{80,64},{96,112},{112,96},{1... | collective-permute-start | bytes 49160 | tf_op jit(solution)/shard_map/ppermute | solution.py:855
  79.1 0.6 copy-start.11
  79.8 0.6 copy-start.13
  81.1 22.8 %all-to-all-start = ((f32[32,8,128]{2,1,0:T(8,128)}), f32[32,8,128]{2,1,0:T(8,128)}, u32[]{:S(2)}, u32[]{:S(2)}) async-start(f32[32,8,128]{2,1,0:T(8,128)} %broadcast_in_dim.4), calls=%async_computation | async-start | bytes 262144 | tf_op jit(solution)/shard_map/all_to_all | solution.py:861
  86.8 6.3 %collective-permute-start.10 = (f32[192,128]{1,0:T(8,128)}, f32[192,128]{1,0:T(8,128)S(1)}, u32[]{:S(2)}, u32[]{:S(2)}) collective-permute-start(f32[192,128]{1,0:T(8,128)} %copy-done.11), channel_id=1, source_target_pairs={{0,15},{1,2},{2,1},{3,4},{4,3},{5,6},{6,5},{7,8},{8,7},{9,10},{10,... | collective-permute-start | bytes 294920 | tf_op jit(solution)/shard_map/ppermute | solution.py:855
  88.8 4.4 %collective-permute-start.11 = (f32[192,128]{1,0:T(8,128)}, f32[192,128]{1,0:T(8,128)S(1)}, u32[]{:S(2)}, u32[]{:S(2)}) collective-permute-start(f32[192,128]{1,0:T(8,128)} %copy-done.13), channel_id=1, source_target_pairs={{0,1},{1,0},{2,3},{3,2},{4,5},{5,4},{6,7},{7,6},{8,9},{9,8},{10,11... | collective-permute-start | bytes 294920 | tf_op jit(solution)/shard_map/ppermute | solution.py:855
  93.2 0.9 copy-start.12
  94.1 0.9 copy-start.14
  96.0 0.7 copy-start.4
  96.6 0.6 copy-start.20
  97.3 0.6 copy-start.21
  103.9 0.9 copy-start.5
  106.9 22.0 %all-to-all-start.1 = ((f32[16,136,128]{2,1,0:T(8,128)}), f32[16,136,128]{2,1,0:T(8,128)}, u32[]{:S(2)}, u32[]{:S(2)}) async-start(f32[16,136,128]{2,1,0:T(8,128)} %broadcast_in_dim.5), calls=%async_computation.1 | async-start | bytes 2228224 | tf_op jit(solution)/shard_map/all_to_all | solution.py:861
  112.7 10.8 %collective-permute-start.12 = (f32[2,64,128]{2,1,0:T(8,128)}, f32[2,64,128]{2,1,0:T(8,128)S(1)}, u32[]{:S(2)}, u32[]{:S(2)}) collective-permute-start(f32[2,64,128]{2,1,0:T(8,128)} %copy-done.21), channel_id=1, source_target_pairs={{0,496},{16,32},{32,16},{48,64},{64,48},{80,96},{96,80},{112,128},... | collective-permute-start | bytes 196616 | tf_op jit(solution)/shard_map/ppermute | solution.py:855
  114.6 9.5 %collective-permute-start.13 = (f32[2,64,128]{2,1,0:T(8,128)}, f32[2,64,128]{2,1,0:T(8,128)S(1)}, u32[]{:S(2)}, u32[]{:S(2)}) collective-permute-start(f32[2,64,128]{2,1,0:T(8,128)} %copy-done.20), channel_id=1, source_target_pairs={{0,16},{16,0},{32,48},{48,32},{64,80},{80,64},{96,112},{112,96},{1... | collective-permute-start | bytes 196616 | tf_op jit(solution)/shard_map/ppermute | solution.py:855
  123.4 0.6 copy-start.15
  124.1 0.6 copy-start.17
  128.9 0.9 copy-start.6
  129.8 0.8 copy-start.9
  130.7 0.8 copy-start.16
  131.5 0.8 copy-start.18
  132.3 16.5 %copy-start.3 = (f32[2,1536,128]{2,1,0:T(8,128)S(1)}, f32[2,1536,128]{2,1,0:T(8,128)}, u32[]{:S(2)}) copy-start(f32[2,1536,128]{2,1,0:T(8,128)} %copy-done.2) | copy-start | bytes 4718596
  139.6 9.2 %collective-permute-start.14 = (f32[2,16,128]{2,1,0:T(8,128)S(1)}, f32[2,16,128]{2,1,0:T(8,128)S(1)}, u32[]{:S(2)}, u32[]{:S(2)}) collective-permute-start(f32[2,16,128]{2,1,0:T(8,128)S(1)} %get-tuple-element.96), channel_id=1, source_target_pairs={{0,496},{16,32},{32,16},{48,64},{64,48},{80,96},{96,80},{112,128},... | collective-permute-start | bytes 49160 | tf_op jit(solution)/shard_map/ppermute | solution.py:855
  141.6 7.3 %collective-permute-start.15 = (f32[2,16,128]{2,1,0:T(8,128)S(1)}, f32[2,16,128]{2,1,0:T(8,128)S(1)}, u32[]{:S(2)}, u32[]{:S(2)}) collective-permute-start(f32[2,16,128]{2,1,0:T(8,128)S(1)} %get-tuple-element.97), channel_id=1, source_target_pairs={{0,16},{16,0},{32,48},{48,32},{64,80},{80,64},{96,112},{112,96},{1... | collective-permute-start | bytes 49160 | tf_op jit(solution)/shard_map/ppermute | solution.py:855
  150.5 9.8 %collective-permute-start.16 = (f32[2,64,128]{2,1,0:T(8,128)S(1)}, f32[2,64,128]{2,1,0:T(8,128)S(1)}, u32[]{:S(2)}, u32[]{:S(2)}) collective-permute-start(f32[2,64,128]{2,1,0:T(8,128)S(1)} %get-tuple-element.101), channel_id=1, source_target_pairs={{0,496},{16,32},{32,16},{48,64},{64,48},{80,96},{96,80},{112,128},... | collective-permute-start | bytes 196616 | tf_op jit(solution)/shard_map/ppermute | solution.py:855
  156.4 6.2 %collective-permute-start.17 = (f32[2,64,128]{2,1,0:T(8,128)S(1)}, f32[2,64,128]{2,1,0:T(8,128)S(1)}, u32[]{:S(2)}, u32[]{:S(2)}) collective-permute-start(f32[2,64,128]{2,1,0:T(8,128)S(1)} %get-tuple-element.102), channel_id=1, source_target_pairs={{0,16},{16,0},{32,48},{48,32},{64,80},{80,64},{96,112},{112,96},{1... | collective-permute-start | bytes 196616 | tf_op jit(solution)/shard_map/ppermute | solution.py:855
  164.2 9.4 %collective-permute-start.18 = (f32[64,128]{1,0:T(8,128)S(1)}, f32[64,128]{1,0:T(8,128)S(1)}, u32[]{:S(2)}, u32[]{:S(2)}) collective-permute-start(f32[64,128]{1,0:T(8,128)S(1)} %get-tuple-element.107), channel_id=1, source_target_pairs={{0,496},{16,32},{32,16},{48,64},{64,48},{80,96},{96,80},{112,128},... | collective-permute-start | bytes 98312 | tf_op jit(solution)/shard_map/ppermute | solution.py:855
  167.8 5.8 %collective-permute-start.19 = (f32[64,128]{1,0:T(8,128)S(1)}, f32[64,128]{1,0:T(8,128)S(1)}, u32[]{:S(2)}, u32[]{:S(2)}) collective-permute-start(f32[64,128]{1,0:T(8,128)S(1)} %get-tuple-element.108), channel_id=1, source_target_pairs={{0,16},{16,0},{32,48},{48,32},{64,80},{80,64},{96,112},{112,96},{1... | collective-permute-start | bytes 98312 | tf_op jit(solution)/shard_map/ppermute | solution.py:855

commit v4 on v2

--- a/solution.py
+++ b/solution.py
@@ -617,7 +617,7 @@
             out[h, 48:64] = back[h, pl.ds(plane, 16), :]
 
 
-def column_kernel(rows, first, out):
+def column_kernel(rows, out):
     ns = rows.shape[0] // 8
     n = ns // groups(ns)
 
@@ -931,7 +931,7 @@
     sides = exchange(a, b, "stream")
     size = 4 * ns + ns // groups(ns)
     (columns,) = call(
-        column_kernel, (columns, wider), [(size, LANES)], (), 0
+        column_kernel, (columns,), [(size, LANES)], (), 0
     )
     cores = [list(range(core, na, 2)) for core in range(2)]
     columns = spread(columns, "azim", cores)

time: 176 us -> 180 us (1.023)
  blocking collectives: 13.2 us -> 36 us
  waiting for transfers between devices: 47.4 us -> 40.8 us
  local copies, waits for them, and re-layouts: 10.6 us -> 4.08 us
  starting transfers between devices: 76.5 us -> 71.8 us
    all_to_all x1 -> x2, blocking collectives: 13.2 us -> 36 us  [spread(): lax.all_to_all(copies, axis, 0, 0, axis_index_groups=groups)]
    all_to_all x1 -> x0, waiting for transfers between devices: 5.98 us -> none  [spread(): lax.all_to_all(copies, axis, 0, 0, axis_index_groups=groups)]
    unnamed x40 -> x10, local copies, waits for them, and re-layouts: 9.95 us -> 4.02 us
    all_to_all x1 -> x0, starting transfers between devices: 5.73 us -> none  [spread(): lax.all_to_all(copies, axis, 0, 0, axis_index_groups=groups)]
  transfers between devices with their start and end apart: 22 -> 21, of which waited for: 16 -> 17; matrix products, arithmetic and copies ran while one was open for 0% -> 0% of each run, Pallas kernels for 3% -> 3%
where the time goes in v4:
time: 180 us; the launch traced here: 179 us
  starting transfers between devices  71.8 us (40%)
  waiting for transfers between devices  40.8 us (23%)
  blocking collectives  36 us (20%)
  Pallas kernels  25.9 us (14%)
  local copies, waits for them, and re-layouts  4.08 us (2%)
    ppermute x10, starting transfers between devices, exchange(): lax.ppermute(far, axis, pairs_far)  48.4 us
    all_to_all x2, blocking collectives, spread(): lax.all_to_all(copies, axis, 0, 0, axis_index_groups=groups)  36 us
    ppermute x10, waiting for transfers between devices, exchange(): lax.ppermute(far, axis, pairs_far)  29.7 us
    pallas_call x17, Pallas kernels, call(): pl.pallas_call(body, out_shape=[jax.ShapeDtypeStruct(s, F32) for s in out...  25.9 us
    ppermute x10, starting transfers between devices, exchange(): lax.ppermute(near, axis, pairs_near)  21.5 us
    ppermute x10, waiting for transfers between devices, exchange(): lax.ppermute(near, axis, pairs_near)  11.1 us
    unnamed x10, local copies, waits for them, and re-layouts  4.02 us
  transfers between devices with their start and end apart: 21, of which 17 were waited for; matrix products, arithmetic and copies ran while one was open for 0% of the time, Pallas kernels for 3%

profile of v4, /device:TPU:8, one launch (start us, length us, event | category | flops | bytes accessed | tf_op | source)
XLA Modules:
  0.0 179.0 jit_solution(16246502721060145054)
XLA Ops:
  0.0 0.1 pad_add_fusion.refs_0_
  0.1 1.1 copy-done.2
  1.2 0.9 copy-done.3
  2.2 0.7 copy-done.4
  2.8 1.2 order_kernel.1
  4.0 1.9 %collective-permute-start = (f32[1024,128]{1,0:T(8,128)S(1)}, f32[1024,128]{1,0:T(8,128)S(1)}, u32[]{:S(2)}, u32[]{:S(2)}) collective-permute-start(f32[1024,128]{1,0:T(8,128)S(1)} %get-tuple-element.59), channel_id=1, source_target_pairs={{0,15},{1,2},{2,1},{3,4},{4,3},{5,6},{6,5},{7,8},{8,7},{9,10},{10,... | collective-permute-start | bytes 1572872 | tf_op jit(solution)/shard_map/ppermute | solution.py:857
  6.0 3.4 %collective-permute-start.1 = (f32[1024,128]{1,0:T(8,128)S(1)}, f32[1024,128]{1,0:T(8,128)S(1)}, u32[]{:S(2)}, u32[]{:S(2)}) collective-permute-start(f32[1024,128]{1,0:T(8,128)S(1)} %get-tuple-element.60), channel_id=1, source_target_pairs={{0,1},{1,0},{2,3},{3,2},{4,5},{5,4},{6,7},{7,6},{8,9},{9,8},{10,11... | collective-permute-start | bytes 1572872 | tf_op jit(solution)/shard_map/ppermute | solution.py:857
  9.4 0.0 copy-start
  9.4 1.3 copy-done
  10.6 0.3 own_kernel.1.refs_3_
  11.0 9.2 %collective-permute-done.refs_4_ = f32[1024,128]{1,0:T(8,128)S(1)} collective-permute-done((f32[1024,128]{1,0:T(8,128)S(1)}, f32[1024,128]{1,0:T(8,128)S(1)}, u32[]{:S(2)}, u32[]{:S(2)}) %collective-permute-start) | collective-permute-done | bytes 524320 | tf_op jit(solution)/shard_map/ppermute | solution.py:857
  20.2 1.8 setup_kernel.1
  21.9 13.1 %collective-permute-start.2 = (f32[2,128,128]{2,1,0:T(8,128)S(1)}, f32[2,128,128]{2,1,0:T(8,128)S(1)}, u32[]{:S(2)}, u32[]{:S(2)}) collective-permute-start(f32[2,128,128]{2,1,0:T(8,128)S(1)} %get-tuple-element.63), channel_id=1, source_target_pairs={{0,496},{16,32},{32,16},{48,64},{64,48},{80,96},{96,80},{112,128},... | collective-permute-start | bytes 393224 | tf_op jit(solution)/shard_map/ppermute | solution.py:857
  35.1 1.9 %collective-permute-start.3 = (f32[2,128,128]{2,1,0:T(8,128)S(1)}, f32[2,128,128]{2,1,0:T(8,128)S(1)}, u32[]{:S(2)}, u32[]{:S(2)}) collective-permute-start(f32[2,128,128]{2,1,0:T(8,128)S(1)} %get-tuple-element.64), channel_id=1, source_target_pairs={{0,16},{16,0},{32,48},{48,32},{64,80},{80,64},{96,112},{112,96},{1... | collective-permute-start | bytes 393224 | tf_op jit(solution)/shard_map/ppermute | solution.py:857
  37.0 1.0 collective-permute-done.2.refs_3_
  38.0 3.9 %collective-permute-done.3.refs_4_ = f32[2,128,128]{2,1,0:T(8,128)S(1)} collective-permute-done((f32[2,128,128]{2,1,0:T(8,128)S(1)}, f32[2,128,128]{2,1,0:T(8,128)S(1)}, u32[]{:S(2)}, u32[]{:S(2)}) %collective-permute-start.3) | collective-permute-done | bytes 131104 | tf_op jit(solution)/shard_map/ppermute | solution.py:857
  41.9 1.6 first_kernel.1
  43.5 3.6 %collective-permute-start.4 = (f32[2,64,128]{2,1,0:T(8,128)S(1)}, f32[2,64,128]{2,1,0:T(8,128)S(1)}, u32[]{:S(2)}, u32[]{:S(2)}) collective-permute-start(f32[2,64,128]{2,1,0:T(8,128)S(1)} %get-tuple-element.70), channel_id=1, source_target_pairs={{0,496},{16,32},{32,16},{48,64},{64,48},{80,96},{96,80},{112,128},... | collective-permute-start | bytes 196616 | tf_op jit(solution)/shard_map/ppermute | solution.py:857
  47.1 1.9 %collective-permute-start.5 = (f32[2,64,128]{2,1,0:T(8,128)S(1)}, f32[2,64,128]{2,1,0:T(8,128)S(1)}, u32[]{:S(2)}, u32[]{:S(2)}) collective-permute-start(f32[2,64,128]{2,1,0:T(8,128)S(1)} %get-tuple-element.71), channel_id=1, source_target_pairs={{0,16},{16,0},{32,48},{48,32},{64,80},{80,64},{96,112},{112,96},{1... | collective-permute-start | bytes 196616 | tf_op jit(solution)/shard_map/ppermute | solution.py:857
  49.1 1.4 coarsen_kernel.1
  50.5 0.8 inner_kernel.2.refs_3_
  51.3 2.0 %collective-permute-done.4.refs_4_ = f32[2,64,128]{2,1,0:T(8,128)S(1)} collective-permute-done((f32[2,64,128]{2,1,0:T(8,128)S(1)}, f32[2,64,128]{2,1,0:T(8,128)S(1)}, u32[]{:S(2)}, u32[]{:S(2)}) %collective-permute-start.4) | collective-permute-done | bytes 65568 | tf_op jit(solution)/shard_map/ppermute | solution.py:857
  53.3 0.0 collective-permute-done.5.refs_5_
  53.3 2.2 %second_kernel.1 = (f32[2,1536,128]{2,1,0:T(8,128)S(1)}, f32[2,64,128]{2,1,0:T(8,128)S(1)}, f32[2,40,128]{2,1,0:T(8,128)S(1)}, f32[2,40,128]{2,1,0:T(8,128)S(1)}) custom-call(s32[2]{0:T(128)S(1)} %pad_add_fusion.refs_0_, f32[2,512,128]{2,1,0:T(8,128)S(1)} %get-tuple-element.66.refs_1_, f32[2,512,128]{2,1,0:T(8,128)S(1)} %get-tuple-element.67.refs_2_.refs_6_.refs_5_.refs_7_, ...), custom_call_target="tpu_custom_call" | custom-call | tf_op jit(solution)/shard_map/second_kernel/pallas_call | solution.py:842
  55.6 5.8 %collective-permute-start.6 = (f32[2,40,128]{2,1,0:T(8,128)S(1)}, f32[2,40,128]{2,1,0:T(8,128)S(1)}, u32[]{:S(2)}, u32[]{:S(2)}) collective-permute-start(f32[2,40,128]{2,1,0:T(8,128)S(1)} %get-tuple-element.77), channel_id=1, source_target_pairs={{0,496},{16,32},{32,16},{48,64},{64,48},{80,96},{96,80},{112,128},... | collective-permute-start | bytes 122888 | tf_op jit(solution)/shard_map/ppermute | solution.py:857
  61.4 1.9 %collective-permute-start.7 = (f32[2,40,128]{2,1,0:T(8,128)S(1)}, f32[2,40,128]{2,1,0:T(8,128)S(1)}, u32[]{:S(2)}, u32[]{:S(2)}) collective-permute-start(f32[2,40,128]{2,1,0:T(8,128)S(1)} %get-tuple-element.78), channel_id=1, source_target_pairs={{0,16},{16,0},{32,48},{48,32},{64,80},{80,64},{96,112},{112,96},{1... | collective-permute-start | bytes 122888 | tf_op jit(solution)/shard_map/ppermute | solution.py:857
  63.3 1.7 collective-permute-done.6.refs_4_
  65.1 2.2 %collective-permute-done.7.refs_5_ = f32[2,40,128]{2,1,0:T(8,128)S(1)} collective-permute-done((f32[2,40,128]{2,1,0:T(8,128)S(1)}, f32[2,40,128]{2,1,0:T(8,128)S(1)}, u32[]{:S(2)}, u32[]{:S(2)}) %collective-permute-start.7) | collective-permute-done | bytes 40992 | tf_op jit(solution)/shard_map/ppermute | solution.py:857
  67.3 1.2 third_kernel.1
  68.5 3.6 %collective-permute-start.8 = (f32[2,16,128]{2,1,0:T(8,128)S(1)}, f32[2,16,128]{2,1,0:T(8,128)S(1)}, u32[]{:S(2)}, u32[]{:S(2)}) collective-permute-start(f32[2,16,128]{2,1,0:T(8,128)S(1)} %get-tuple-element.84), channel_id=1, source_target_pairs={{0,496},{16,32},{32,16},{48,64},{64,48},{80,96},{96,80},{112,128},... | collective-permute-start | bytes 49160 | tf_op jit(solution)/shard_map/ppermute | solution.py:857
  72.1 1.9 %collective-permute-start.9 = (f32[2,16,128]{2,1,0:T(8,128)S(1)}, f32[2,16,128]{2,1,0:T(8,128)S(1)}, u32[]{:S(2)}, u32[]{:S(2)}) collective-permute-start(f32[2,16,128]{2,1,0:T(8,128)S(1)} %get-tuple-element.85), channel_id=1, source_target_pairs={{0,16},{16,0},{32,48},{48,32},{64,80},{80,64},{96,112},{112,96},{1... | collective-permute-start | bytes 49160 | tf_op jit(solution)/shard_map/ppermute | solution.py:857
  74.0 3.7 %collective-permute-done.8.refs_5_ = f32[2,16,128]{2,1,0:T(8,128)S(1)} collective-permute-done((f32[2,16,128]{2,1,0:T(8,128)S(1)}, f32[2,16,128]{2,1,0:T(8,128)S(1)}, u32[]{:S(2)}, u32[]{:S(2)}) %collective-permute-start.8) | collective-permute-done | bytes 16416 | tf_op jit(solution)/shard_map/ppermute | solution.py:857
  77.7 0.1 collective-permute-done.9.refs_6_
  77.8 1.3 fourth_kernel.1
  79.2 22.5 %all_to_all.10 = f32[32,8,128]{2,1,0:T(8,128)S(1)} all-to-all(f32[32,8,128]{2,1,0:T(8,128)S(1)} %broadcast_in_dim.4), channel_id=1, replica_groups=mesh['stream'=32,'azim'=16] {'stream'}, dimensions={0} | all-to-all | bytes 262144 | tf_op jit(solution)/shard_map/all_to_all | solution.py:863
  101.7 0.1 column_kernel.1
  101.9 13.5 %all_to_all.11 = f32[8,136,128]{2,1,0:T(8,128)S(1)} all-to-all(f32[8,136,128]{2,1,0:T(8,128)S(1)} %broadcast_in_dim.5), channel_id=1, replica_groups={{0,2,4,6,8,10,12,14},{1,3,5,7,9,11,13,15},{16,18,20,22,24,26,28,30},{17..., dimensions={0} | all-to-all | bytes 1114112 | tf_op jit(solution)/shard_map/all_to_all | solution.py:863
  115.4 1.9 %collective-permute-start.10 = (f32[1088,128]{1,0:T(8,128)S(1)}, f32[1088,128]{1,0:T(8,128)S(1)}, u32[]{:S(2)}, u32[]{:S(2)}) collective-permute-start(f32[1088,128]{1,0:T(8,128)S(1)} %bitcast.9), channel_id=1, source_target_pairs={{0,1},{1,0},{2,3},{3,2},{4,5},{5,4},{6,7},{7,6},{8,9},{9,8},{10,11... | collective-permute-start | bytes 1671176 | tf_op jit(solution)/shard_map/ppermute | solution.py:938
  117.3 3.3 %collective-permute-start.11 = (f32[192,128]{1,0:T(8,128)S(1)}, f32[192,128]{1,0:T(8,128)S(1)}, u32[]{:S(2)}, u32[]{:S(2)}) collective-permute-start(f32[192,128]{1,0:T(8,128)S(1)} %get-tuple-element.87.refs_1_), channel_id=1, source_target_pairs={{0,15},{1,2},{2,1},{3,4},{4,3},{5,6},{6,5},{7,8},{8,7},{9,10},{10,... | collective-permute-start | bytes 294920 | tf_op jit(solution)/shard_map/ppermute | solution.py:857
  120.7 1.9 %collective-permute-start.12 = (f32[192,128]{1,0:T(8,128)S(1)}, f32[192,128]{1,0:T(8,128)S(1)}, u32[]{:S(2)}, u32[]{:S(2)}) collective-permute-start(f32[192,128]{1,0:T(8,128)S(1)} %get-tuple-element.88.refs_2_), channel_id=1, source_target_pairs={{0,1},{1,0},{2,3},{3,2},{4,5},{5,4},{6,7},{7,6},{8,9},{9,8},{10,11... | collective-permute-start | bytes 294920 | tf_op jit(solution)/shard_map/ppermute | solution.py:857
  122.6 0.7 collective-permute-done.11.refs_3_
  123.3 0.6 collective-permute-done.12.refs_4_
  123.9 1.0 side_kernel.1
  124.9 1.9 %collective-permute-start.13 = (f32[2,64,128]{2,1,0:T(8,128)S(1)}, f32[2,64,128]{2,1,0:T(8,128)S(1)}, u32[]{:S(2)}, u32[]{:S(2)}) collective-permute-start(f32[2,64,128]{2,1,0:T(8,128)S(1)} %get-tuple-element.90), channel_id=1, source_target_pairs={{0,496},{16,32},{32,16},{48,64},{64,48},{80,96},{96,80},{112,128},... | collective-permute-start | bytes 196616 | tf_op jit(solution)/shard_map/ppermute | solution.py:857
  126.8 2.7 %collective-permute-start.14 = (f32[2,64,128]{2,1,0:T(8,128)S(1)}, f32[2,64,128]{2,1,0:T(8,128)S(1)}, u32[]{:S(2)}, u32[]{:S(2)}) collective-permute-start(f32[2,64,128]{2,1,0:T(8,128)S(1)} %get-tuple-element.91), channel_id=1, source_target_pairs={{0,16},{16,0},{32,48},{48,32},{64,80},{80,64},{96,112},{112,96},{1... | collective-permute-start | bytes 196616 | tf_op jit(solution)/shard_map/ppermute | solution.py:857
  129.6 5.6 %collective-permute-done.13.refs_4_ = f32[2,64,128]{2,1,0:T(8,128)S(1)} collective-permute-done((f32[2,64,128]{2,1,0:T(8,128)S(1)}, f32[2,64,128]{2,1,0:T(8,128)S(1)}, u32[]{:S(2)}, u32[]{:S(2)}) %collective-permute-start.13) | collective-permute-done | bytes 65568 | tf_op jit(solution)/shard_map/ppermute | solution.py:857
  135.2 6.5 %coarse_kernel.1 = (f32[2,64,128]{2,1,0:T(8,128)S(1)}, f32[2,64,128]{2,1,0:T(8,128)S(1)}, f32[2,64,128]{2,1,0:T(8,128)S(1)}, f32[2,64,128]{2,1,0:T(8,128)S(1)}, ...) custom-call(s32[2]{0:T(128)S(1)} %pad_add_fusion.refs_0_, f32[1088,128]{1,0:T(8,128)S(1)} %bitcast.10, ...), custom_call_target="tpu_custom_call" | custom-call | tf_op jit(solution)/shard_map/coarse_kernel/pallas_call | solution.py:842
  141.7 5.6 %collective-permute-start.15 = (f32[2,16,128]{2,1,0:T(8,128)S(1)}, f32[2,16,128]{2,1,0:T(8,128)S(1)}, u32[]{:S(2)}, u32[]{:S(2)}) collective-permute-start(f32[2,16,128]{2,1,0:T(8,128)S(1)} %get-tuple-element.96), channel_id=1, source_target_pairs={{0,496},{16,32},{32,16},{48,64},{64,48},{80,96},{96,80},{112,128},... | collective-permute-start | bytes 49160 | tf_op jit(solution)/shard_map/ppermute | solution.py:857
  147.3 1.9 %collective-permute-start.16 = (f32[2,16,128]{2,1,0:T(8,128)S(1)}, f32[2,16,128]{2,1,0:T(8,128)S(1)}, u32[]{:S(2)}, u32[]{:S(2)}) collective-permute-start(f32[2,16,128]{2,1,0:T(8,128)S(1)} %get-tuple-element.97), channel_id=1, source_target_pairs={{0,16},{16,0},{32,48},{48,32},{64,80},{80,64},{96,112},{112,96},{1... | collective-permute-start | bytes 49160 | tf_op jit(solution)/shard_map/ppermute | solution.py:857
  149.2 1.7 collective-permute-done.15.refs_5_
  150.9 2.0 %collective-permute-done.16.refs_6_ = f32[2,16,128]{2,1,0:T(8,128)S(1)} collective-permute-done((f32[2,16,128]{2,1,0:T(8,128)S(1)}, f32[2,16,128]{2,1,0:T(8,128)S(1)}, u32[]{:S(2)}, u32[]{:S(2)}) %collective-permute-start.16) | collective-permute-done | bytes 16416 | tf_op jit(solution)/shard_map/ppermute | solution.py:857
  152.9 1.6 sixth_kernel.1
  154.5 3.9 %collective-permute-start.17 = (f32[2,64,128]{2,1,0:T(8,128)S(1)}, f32[2,64,128]{2,1,0:T(8,128)S(1)}, u32[]{:S(2)}, u32[]{:S(2)}) collective-permute-start(f32[2,64,128]{2,1,0:T(8,128)S(1)} %get-tuple-element.101), channel_id=1, source_target_pairs={{0,496},{16,32},{32,16},{48,64},{64,48},{80,96},{96,80},{112,128},... | collective-permute-start | bytes 196616 | tf_op jit(solution)/shard_map/ppermute | solution.py:857
  158.4 1.9 %collective-permute-start.18 = (f32[2,64,128]{2,1,0:T(8,128)S(1)}, f32[2,64,128]{2,1,0:T(8,128)S(1)}, u32[]{:S(2)}, u32[]{:S(2)}) collective-permute-start(f32[2,64,128]{2,1,0:T(8,128)S(1)} %get-tuple-element.102), channel_id=1, source_target_pairs={{0,16},{16,0},{32,48},{48,32},{64,80},{80,64},{96,112},{112,96},{1... | collective-permute-start | bytes 196616 | tf_op jit(solution)/shard_map/ppermute | solution.py:857
  160.4 0.8 inner_kernel.3.refs_3_
  161.2 3.1 %collective-permute-done.17.refs_4_ = f32[2,64,128]{2,1,0:T(8,128)S(1)} collective-permute-done((f32[2,64,128]{2,1,0:T(8,128)S(1)}, f32[2,64,128]{2,1,0:T(8,128)S(1)}, u32[]{:S(2)}, u32[]{:S(2)}) %collective-permute-start.17) | collective-permute-done | bytes 65568 | tf_op jit(solution)/shard_map/ppermute | solution.py:857
  164.3 0.3 collective-permute-done.18.refs_5_
  164.6 1.6 seventh_kernel.1
  166.2 5.6 %collective-permute-start.19 = (f32[64,128]{1,0:T(8,128)S(1)}, f32[64,128]{1,0:T(8,128)S(1)}, u32[]{:S(2)}, u32[]{:S(2)}) collective-permute-start(f32[64,128]{1,0:T(8,128)S(1)} %get-tuple-element.107), channel_id=1, source_target_pairs={{0,496},{16,32},{32,16},{48,64},{64,48},{80,96},{96,80},{112,128},... | collective-permute-start | bytes 98312 | tf_op jit(solution)/shard_map/ppermute | solution.py:857
  171.8 1.9 %collective-permute-start.20 = (f32[64,128]{1,0:T(8,128)S(1)}, f32[64,128]{1,0:T(8,128)S(1)}, u32[]{:S(2)}, u32[]{:S(2)}) collective-permute-start(f32[64,128]{1,0:T(8,128)S(1)} %get-tuple-element.108), channel_id=1, source_target_pairs={{0,16},{16,0},{32,48},{48,32},{64,80},{80,64},{96,112},{112,96},{1... | collective-permute-start | bytes 98312 | tf_op jit(solution)/shard_map/ppermute | solution.py:857
  173.7 0.9 inner_last_kernel.1.refs_8_
  174.7 1.0 collective-permute-done.19.refs_5_
  175.6 2.0 %collective-permute-done.20.refs_6_ = f32[64,128]{1,0:T(8,128)S(1)} collective-permute-done((f32[64,128]{1,0:T(8,128)S(1)}, f32[64,128]{1,0:T(8,128)S(1)}, u32[]{:S(2)}, u32[]{:S(2)}) %collective-permute-start.20) | collective-permute-done | bytes 32800 | tf_op jit(solution)/shard_map/ppermute | solution.py:857
  177.6 1.4 last_kernel.1
  (10 shorter events, 0.1 us)
Async XLA Ops:
  0.1 1.1 copy-start.2
  1.2 0.9 copy-start.3
  2.2 0.7 copy-start.4
  4.0 16.1 %collective-permute-start = (f32[1024,128]{1,0:T(8,128)S(1)}, f32[1024,128]{1,0:T(8,128)S(1)}, u32[]{:S(2)}, u32[]{:S(2)}) collective-permute-start(f32[1024,128]{1,0:T(8,128)S(1)} %get-tuple-element.59), channel_id=1, source_target_pairs={{0,15},{1,2},{2,1},{3,4},{4,3},{5,6},{6,5},{7,8},{8,7},{9,10},{10,... | collective-permute-start | bytes 1572872 | tf_op jit(solution)/shard_map/ppermute | solution.py:857
  6.0 14.2 %collective-permute-start.1 = (f32[1024,128]{1,0:T(8,128)S(1)}, f32[1024,128]{1,0:T(8,128)S(1)}, u32[]{:S(2)}, u32[]{:S(2)}) collective-permute-start(f32[1024,128]{1,0:T(8,128)S(1)} %get-tuple-element.60), channel_id=1, source_target_pairs={{0,1},{1,0},{2,3},{3,2},{4,5},{5,4},{6,7},{7,6},{8,9},{9,8},{10,11... | collective-permute-start | bytes 1572872 | tf_op jit(solution)/shard_map/ppermute | solution.py:857
  9.4 1.3 copy-start
  10.6 9.5 %copy-start.1 = (f32[2352,128]{1,0:T(8,128)S(1)}, f32[2352,128]{1,0:T(8,128)}, u32[]{:S(2)}) copy-start(f32[2352,128]{1,0:T(8,128)} %constant.11.clone.refs_1_.refs_6_.refs_3_.refs_9_.refs_7_.refs_8_.refs_10_) | copy-start | bytes 3612676
  21.9 16.1 %collective-permute-start.2 = (f32[2,128,128]{2,1,0:T(8,128)S(1)}, f32[2,128,128]{2,1,0:T(8,128)S(1)}, u32[]{:S(2)}, u32[]{:S(2)}) collective-permute-start(f32[2,128,128]{2,1,0:T(8,128)S(1)} %get-tuple-element.63), channel_id=1, source_target_pairs={{0,496},{16,32},{32,16},{48,64},{64,48},{80,96},{96,80},{112,128},... | collective-permute-start | bytes 393224 | tf_op jit(solution)/shard_map/ppermute | solution.py:857
  35.1 6.9 %collective-permute-start.3 = (f32[2,128,128]{2,1,0:T(8,128)S(1)}, f32[2,128,128]{2,1,0:T(8,128)S(1)}, u32[]{:S(2)}, u32[]{:S(2)}) collective-permute-start(f32[2,128,128]{2,1,0:T(8,128)S(1)} %get-tuple-element.64), channel_id=1, source_target_pairs={{0,16},{16,0},{32,48},{48,32},{64,80},{80,64},{96,112},{112,96},{1... | collective-permute-start | bytes 393224 | tf_op jit(solution)/shard_map/ppermute | solution.py:857
  43.5 9.8 %collective-permute-start.4 = (f32[2,64,128]{2,1,0:T(8,128)S(1)}, f32[2,64,128]{2,1,0:T(8,128)S(1)}, u32[]{:S(2)}, u32[]{:S(2)}) collective-permute-start(f32[2,64,128]{2,1,0:T(8,128)S(1)} %get-tuple-element.70), channel_id=1, source_target_pairs={{0,496},{16,32},{32,16},{48,64},{64,48},{80,96},{96,80},{112,128},... | collective-permute-start | bytes 196616 | tf_op jit(solution)/shard_map/ppermute | solution.py:857
  47.1 6.2 %collective-permute-start.5 = (f32[2,64,128]{2,1,0:T(8,128)S(1)}, f32[2,64,128]{2,1,0:T(8,128)S(1)}, u32[]{:S(2)}, u32[]{:S(2)}) collective-permute-start(f32[2,64,128]{2,1,0:T(8,128)S(1)} %get-tuple-element.71), channel_id=1, source_target_pairs={{0,16},{16,0},{32,48},{48,32},{64,80},{80,64},{96,112},{112,96},{1... | collective-permute-start | bytes 196616 | tf_op jit(solution)/shard_map/ppermute | solution.py:857
  55.6 9.5 %collective-permute-start.6 = (f32[2,40,128]{2,1,0:T(8,128)S(1)}, f32[2,40,128]{2,1,0:T(8,128)S(1)}, u32[]{:S(2)}, u32[]{:S(2)}) collective-permute-start(f32[2,40,128]{2,1,0:T(8,128)S(1)} %get-tuple-element.77), channel_id=1, source_target_pairs={{0,496},{16,32},{32,16},{48,64},{64,48},{80,96},{96,80},{112,128},... | collective-permute-start | bytes 122888 | tf_op jit(solution)/shard_map/ppermute | solution.py:857
  61.4 5.9 %collective-permute-start.7 = (f32[2,40,128]{2,1,0:T(8,128)S(1)}, f32[2,40,128]{2,1,0:T(8,128)S(1)}, u32[]{:S(2)}, u32[]{:S(2)}) collective-permute-start(f32[2,40,128]{2,1,0:T(8,128)S(1)} %get-tuple-element.78), channel_id=1, source_target_pairs={{0,16},{16,0},{32,48},{48,32},{64,80},{80,64},{96,112},{112,96},{1... | collective-permute-start | bytes 122888 | tf_op jit(solution)/shard_map/ppermute | solution.py:857
  68.5 9.2 %collective-permute-start.8 = (f32[2,16,128]{2,1,0:T(8,128)S(1)}, f32[2,16,128]{2,1,0:T(8,128)S(1)}, u32[]{:S(2)}, u32[]{:S(2)}) collective-permute-start(f32[2,16,128]{2,1,0:T(8,128)S(1)} %get-tuple-element.84), channel_id=1, source_target_pairs={{0,496},{16,32},{32,16},{48,64},{64,48},{80,96},{96,80},{112,128},... | collective-permute-start | bytes 49160 | tf_op jit(solution)/shard_map/ppermute | solution.py:857
  72.1 5.7 %collective-permute-start.9 = (f32[2,16,128]{2,1,0:T(8,128)S(1)}, f32[2,16,128]{2,1,0:T(8,128)S(1)}, u32[]{:S(2)}, u32[]{:S(2)}) collective-permute-start(f32[2,16,128]{2,1,0:T(8,128)S(1)} %get-tuple-element.85), channel_id=1, source_target_pairs={{0,16},{16,0},{32,48},{48,32},{64,80},{80,64},{96,112},{112,96},{1... | collective-permute-start | bytes 49160 | tf_op jit(solution)/shard_map/ppermute | solution.py:857
  115.4 19.8 %collective-permute-start.10 = (f32[1088,128]{1,0:T(8,128)S(1)}, f32[1088,128]{1,0:T(8,128)S(1)}, u32[]{:S(2)}, u32[]{:S(2)}) collective-permute-start(f32[1088,128]{1,0:T(8,128)S(1)} %bitcast.9), channel_id=1, source_target_pairs={{0,1},{1,0},{2,3},{3,2},{4,5},{5,4},{6,7},{7,6},{8,9},{9,8},{10,11... | collective-permute-start | bytes 1671176 | tf_op jit(solution)/shard_map/ppermute | solution.py:938
  117.3 5.9 %collective-permute-start.11 = (f32[192,128]{1,0:T(8,128)S(1)}, f32[192,128]{1,0:T(8,128)S(1)}, u32[]{:S(2)}, u32[]{:S(2)}) collective-permute-start(f32[192,128]{1,0:T(8,128)S(1)} %get-tuple-element.87.refs_1_), channel_id=1, source_target_pairs={{0,15},{1,2},{2,1},{3,4},{4,3},{5,6},{6,5},{7,8},{8,7},{9,10},{10,... | collective-permute-start | bytes 294920 | tf_op jit(solution)/shard_map/ppermute | solution.py:857
  120.7 3.2 %collective-permute-start.12 = (f32[192,128]{1,0:T(8,128)S(1)}, f32[192,128]{1,0:T(8,128)S(1)}, u32[]{:S(2)}, u32[]{:S(2)}) collective-permute-start(f32[192,128]{1,0:T(8,128)S(1)} %get-tuple-element.88.refs_2_), channel_id=1, source_target_pairs={{0,1},{1,0},{2,3},{3,2},{4,5},{5,4},{6,7},{7,6},{8,9},{9,8},{10,11... | collective-permute-start | bytes 294920 | tf_op jit(solution)/shard_map/ppermute | solution.py:857
  124.9 10.3 %collective-permute-start.13 = (f32[2,64,128]{2,1,0:T(8,128)S(1)}, f32[2,64,128]{2,1,0:T(8,128)S(1)}, u32[]{:S(2)}, u32[]{:S(2)}) collective-permute-start(f32[2,64,128]{2,1,0:T(8,128)S(1)} %get-tuple-element.90), channel_id=1, source_target_pairs={{0,496},{16,32},{32,16},{48,64},{64,48},{80,96},{96,80},{112,128},... | collective-permute-start | bytes 196616 | tf_op jit(solution)/shard_map/ppermute | solution.py:857
  126.8 8.4 %collective-permute-start.14 = (f32[2,64,128]{2,1,0:T(8,128)S(1)}, f32[2,64,128]{2,1,0:T(8,128)S(1)}, u32[]{:S(2)}, u32[]{:S(2)}) collective-permute-start(f32[2,64,128]{2,1,0:T(8,128)S(1)} %get-tuple-element.91), channel_id=1, source_target_pairs={{0,16},{16,0},{32,48},{48,32},{64,80},{80,64},{96,112},{112,96},{1... | collective-permute-start | bytes 196616 | tf_op jit(solution)/shard_map/ppermute | solution.py:857
  141.7 9.2 %collective-permute-start.15 = (f32[2,16,128]{2,1,0:T(8,128)S(1)}, f32[2,16,128]{2,1,0:T(8,128)S(1)}, u32[]{:S(2)}, u32[]{:S(2)}) collective-permute-start(f32[2,16,128]{2,1,0:T(8,128)S(1)} %get-tuple-element.96), channel_id=1, source_target_pairs={{0,496},{16,32},{32,16},{48,64},{64,48},{80,96},{96,80},{112,128},... | collective-permute-start | bytes 49160 | tf_op jit(solution)/shard_map/ppermute | solution.py:857
  147.3 5.6 %collective-permute-start.16 = (f32[2,16,128]{2,1,0:T(8,128)S(1)}, f32[2,16,128]{2,1,0:T(8,128)S(1)}, u32[]{:S(2)}, u32[]{:S(2)}) collective-permute-start(f32[2,16,128]{2,1,0:T(8,128)S(1)} %get-tuple-element.97), channel_id=1, source_target_pairs={{0,16},{16,0},{32,48},{48,32},{64,80},{80,64},{96,112},{112,96},{1... | collective-permute-start | bytes 49160 | tf_op jit(solution)/shard_map/ppermute | solution.py:857
  154.5 9.8 %collective-permute-start.17 = (f32[2,64,128]{2,1,0:T(8,128)S(1)}, f32[2,64,128]{2,1,0:T(8,128)S(1)}, u32[]{:S(2)}, u32[]{:S(2)}) collective-permute-start(f32[2,64,128]{2,1,0:T(8,128)S(1)} %get-tuple-element.101), channel_id=1, source_target_pairs={{0,496},{16,32},{32,16},{48,64},{64,48},{80,96},{96,80},{112,128},... | collective-permute-start | bytes 196616 | tf_op jit(solution)/shard_map/ppermute | solution.py:857
  158.4 6.2 %collective-permute-start.18 = (f32[2,64,128]{2,1,0:T(8,128)S(1)}, f32[2,64,128]{2,1,0:T(8,128)S(1)}, u32[]{:S(2)}, u32[]{:S(2)}) collective-permute-start(f32[2,64,128]{2,1,0:T(8,128)S(1)} %get-tuple-element.102), channel_id=1, source_target_pairs={{0,16},{16,0},{32,48},{48,32},{64,80},{80,64},{96,112},{112,96},{1... | collective-permute-start | bytes 196616 | tf_op jit(solution)/shard_map/ppermute | solution.py:857
  166.2 9.4 %collective-permute-start.19 = (f32[64,128]{1,0:T(8,128)S(1)}, f32[64,128]{1,0:T(8,128)S(1)}, u32[]{:S(2)}, u32[]{:S(2)}) collective-permute-start(f32[64,128]{1,0:T(8,128)S(1)} %get-tuple-element.107), channel_id=1, source_target_pairs={{0,496},{16,32},{32,16},{48,64},{64,48},{80,96},{96,80},{112,128},... | collective-permute-start | bytes 98312 | tf_op jit(solution)/shard_map/ppermute | solution.py:857
  171.8 5.8 %collective-permute-start.20 = (f32[64,128]{1,0:T(8,128)S(1)}, f32[64,128]{1,0:T(8,128)S(1)}, u32[]{:S(2)}, u32[]{:S(2)}) collective-permute-start(f32[64,128]{1,0:T(8,128)S(1)} %get-tuple-element.108), channel_id=1, source_target_pairs={{0,16},{16,0},{32,48},{48,32},{64,80},{80,64},{96,112},{112,96},{1... | collective-permute-start | bytes 98312 | tf_op jit(solution)/shard_map/ppermute | solution.py:857
